TPU v7x, 32 devices: a whole 2x2x4 slice. The times are simulated.
32 devices in a mesh: rx: 8 (over z, y), ry: 4 (over x, core).
Axes of the slice: x: 2, y: 2, z: 4, core: 2. Of those that a mesh axis runs over, the one named last changes fastest.
Arguments:
- matrix: float32 [131072, 256], P(('rx', 'ry')), may hold values from -6 to 6
- signs: int32 [131072], P(('rx', 'ry')), may hold values from -1 to 1, as said below
- indices: int32 [8192], P(('rx', 'ry')), may hold values from 0 to 4095, as said below
- counts: int32 [32], P(('rx', 'ry')), may hold values from 64 to 256, as said below
Outputs:
- sketch: float32 [8192, 256], P(('rx', 'ry'))
- gram_blocks: float32 [4, 128, 128], P('ry')
Inputs may be any that keep to these rules, and one draw needn't show every extreme that they name: `signs`: each entry is -1 or 1. `indices`: local row numbers; repeats allowed; entries of dead slots are ignored. `counts`: some device has all 256 slots live.
All inputs are finite; a program needn't handle non-finite values.
Results may differ from a plain program's by a relative error of at most 0.00011.
Values sent between devices are 32-bit elements; how exact they have to be, the bound alone decides.
No kernel may reach another device: no remote copies, remote signals or barrier semaphores. Data moves between devices by JAX's collectives and lax.ppermute only.
A program may use at most 64 MiB of HBM per device.

v0:
```python
import jax
import jax.numpy as jnp
from jax import lax
from jax.sharding import PartitionSpec as P

BLK = 128


def partner_2(value, axis, distance):
    return lax.ppermute(value, axis, [(i, i ^ 1 << distance) for i in range(lax.axis_size(axis))])


def hadamard(order):
    idx = jnp.arange(order, dtype=jnp.int32)
    both = jnp.bitwise_and(idx[:, None], idx[None, :])
    parity = jnp.zeros((order, order), jnp.int32)
    for shift in range(order.bit_length() - 1):
        parity = parity + jnp.bitwise_and(jnp.right_shift(both, shift), 1)
    return (1 - 2 * (parity % 2)).astype(jnp.float32)


def local(matrix, signs, indices, counts):
    rows, width = matrix.shape
    panel = width // 2
    size_x = lax.axis_size("rx")
    size_y = lax.axis_size("ry")
    signed = matrix * signs[:, None].astype(jnp.float32)
    blocks = signed.reshape(rows // BLK, BLK, width)
    mixed = jnp.einsum(
        "ij,bjc->bic", hadamard(BLK), blocks, precision=lax.Precision.HIGHEST
    ).reshape(rows, width)
    for shift in range(size_y.bit_length() - 1):
        partner = partner_2(mixed, "ry", shift)
        upper = jnp.bitwise_and(jnp.right_shift(lax.axis_index("ry"), shift), 1) == 1
        mixed = jnp.where(upper, partner - mixed, mixed + partner)
    for shift in range(size_x.bit_length() - 1):
        partner = partner_2(mixed, "rx", shift)
        upper = jnp.bitwise_and(jnp.right_shift(lax.axis_index("rx"), shift), 1) == 1
        mixed = jnp.where(upper, partner - mixed, mixed + partner)
    mixed = mixed * (1.0 / (size_x * size_y * BLK) ** 0.5)
    slots = indices.shape[0]
    live = jnp.arange(slots, dtype=jnp.int32) < counts[0]
    picked = jnp.take(mixed, indices, axis=0)
    sketch = jnp.where(live[:, None], picked, jnp.float32(0.0))
    factor = 1.0 / (size_x * size_y * slots)
    owner = lax.axis_index("ry")
    left_start = owner // 2 * panel
    right_start = owner % 2 * panel
    piece = lax.all_gather(sketch, "ry", axis=0, tiled=True)
    left = lax.dynamic_slice_in_dim(piece, left_start, panel, 1)
    right = lax.dynamic_slice_in_dim(piece, right_start, panel, 1)
    partial_block = jnp.dot(left.T, right, precision=lax.Precision.HIGHEST)
    block = lax.psum(partial_block, "rx")
    gram_blocks = (block * factor)[None]
    return (sketch, gram_blocks)


def solution(mesh):
    in_specs = (P(("rx", "ry"), None), P(("rx", "ry")), P(("rx", "ry")), P(("rx", "ry")))
    out_specs = (P(("rx", "ry"), None), P("ry", None, None))
    return jax.shard_map(local, mesh=mesh, in_specs=in_specs, out_specs=out_specs, check_vma=False)
```

profile of v0, /device:TPU:0, one launch (start us, length us, event | category | flops | bytes accessed | tf_op | source)
XLA Modules:
  0.0 614.9 jit_solution(11630103567433232056)
XLA Ops:
  7.2 0.0 all-gather.2.cloned.1.call-start
  7.2 0.7 convert_element_type.7
  7.9 2.6 broadcast_multiply_fusion
  10.5 5.5 fusion.8
  16.0 0.5 collective-permute-start
  16.5 7.1 %collective-permute-done = f32[4096,256]{1,0:T(8,128)} collective-permute-done((f32[4096,256]{1,0:T(8,128)}, f32[4096,256]{1,0:T(8,128)}, u32[]{:S(2)}, u32[]{:S(2)}) %collective-permute-start) | collective-permute-done | bytes 4194336 | tf_op jit(solution)/shard_map/ppermute | solution.py:10
  23.6 6.0 add_select_fusion.3
  29.6 2.9 collective-permute-start.1
  32.4 91.2 %collective-permute-done.1 = f32[4096,256]{1,0:T(8,128)} collective-permute-done((f32[4096,256]{1,0:T(8,128)}, f32[4096,256]{1,0:T(8,128)}, u32[]{:S(2)}, u32[]{:S(2)}) %collective-permute-start.1) | collective-permute-done | bytes 4194336 | tf_op jit(solution)/shard_map/ppermute | solution.py:10
  123.6 6.0 add_select_fusion.2
  129.6 1.8 collective-permute-start.2
  131.3 90.6 %collective-permute-done.2 = f32[4096,256]{1,0:T(8,128)} collective-permute-done((f32[4096,256]{1,0:T(8,128)}, f32[4096,256]{1,0:T(8,128)}, u32[]{:S(2)}, u32[]{:S(2)}) %collective-permute-start.2) | collective-permute-done | bytes 4194336 | tf_op jit(solution)/shard_map/ppermute | solution.py:10
  222.0 6.0 add_select_fusion.1
  227.9 1.5 collective-permute-start.3
  229.4 0.0 copy-start
  229.4 90.0 %collective-permute-done.3 = f32[4096,256]{1,0:T(8,128)} collective-permute-done((f32[4096,256]{1,0:T(8,128)}, f32[4096,256]{1,0:T(8,128)}, u32[]{:S(2)}, u32[]{:S(2)}) %collective-permute-start.3) | collective-permute-done | bytes 4194336 | tf_op jit(solution)/shard_map/ppermute | solution.py:10
  319.5 6.0 add_select_fusion
  325.4 2.2 collective-permute-start.4
  328.2 0.0 copy-done
  328.3 178.5 %collective-permute-done.4 = f32[4096,256]{1,0:T(8,128)} collective-permute-done((f32[4096,256]{1,0:T(8,128)}, f32[4096,256]{1,0:T(8,128)}, u32[]{:S(2)}, u32[]{:S(2)}) %collective-permute-start.4) | collective-permute-done | bytes 4194336 | tf_op jit(solution)/shard_map/ppermute | solution.py:10
  506.8 6.0 select_multiply_fusion
  512.7 3.2 gather_fusion
  515.9 0.8 select_select_fusion
  516.7 0.0 all-gather.2.cloned.1.call-update
  516.8 0.0 all-reduce.2.cloned.1.call-start
  516.8 17.2 %all-gather.2.cloned.1.call-done = f32[1024,256]{1,0:T(8,128)} async-done(((f32[256,256]{1,0:T(8,128)}), f32[1024,256]{1,0:T(8,128)}) %all-gather.2.cloned.1.call-update) | async-done | bytes 1048592 | tf_op jit(solution)/shard_map/all_gather | solution.py:49
  534.0 2.8 fusion
  536.9 0.0 all-reduce.2.cloned.1.call-update
  536.9 69.6 %all-reduce.2.cloned.1.call-done = f32[128,128]{1,0:T(8,128)} async-done(((f32[128,128]{1,0:T(8,128)}), f32[128,128]{1,0:T(8,128)}) %all-reduce.2.cloned.1.call-update) | async-done | bytes 65552 | tf_op jit(solution)/shard_map/psum | solution.py:53
  606.5 1.5 multiply_bitcast_fusion
  (3 shorter events, 0.0 us)
Async XLA Ops:
  7.2 526.9 %all-gather.2.cloned.1.call-start = ((), (), s32[]{:S(2)}) async-start(), calls=%async_computation | async-start | bytes 1310720 | tf_op jit(solution)/shard_map/all_gather | solution.py:49
  16.0 7.6 %collective-permute-start = (f32[4096,256]{1,0:T(8,128)}, f32[4096,256]{1,0:T(8,128)}, u32[]{:S(2)}, u32[]{:S(2)}) collective-permute-start(f32[4096,256]{1,0:T(8,128)} %bitcast.4), channel_id=1, source_target_pairs={{0,1},{1,0},{2,3},{3,2},{4,5},{5,4},{6,7},{7,6},{8,9},{9,8},{10,11... | collective-permute-start | bytes 12582920 | tf_op jit(solution)/shard_map/ppermute | solution.py:10
  29.6 94.0 %collective-permute-start.1 = (f32[4096,256]{1,0:T(8,128)}, f32[4096,256]{1,0:T(8,128)}, u32[]{:S(2)}, u32[]{:S(2)}) collective-permute-start(f32[4096,256]{1,0:T(8,128)} %add_select_fusion.3), channel_id=1, source_target_pairs={{0,2},{1,3},{2,0},{3,1},{4,6},{5,7},{6,4},{7,5},{8,10},{9,11},{10,... | collective-permute-start | bytes 12582920 | tf_op jit(solution)/shard_map/ppermute | solution.py:10
  129.6 92.4 %collective-permute-start.2 = (f32[4096,256]{1,0:T(8,128)}, f32[4096,256]{1,0:T(8,128)}, u32[]{:S(2)}, u32[]{:S(2)}) collective-permute-start(f32[4096,256]{1,0:T(8,128)} %add_select_fusion.2), channel_id=1, source_target_pairs={{0,4},{4,0},{8,12},{12,8},{16,20},{20,16},{24,28},{28,24},{1,5},{5... | collective-permute-start | bytes 12582920 | tf_op jit(solution)/shard_map/ppermute | solution.py:10
  227.9 91.5 %collective-permute-start.3 = (f32[4096,256]{1,0:T(8,128)}, f32[4096,256]{1,0:T(8,128)}, u32[]{:S(2)}, u32[]{:S(2)}) collective-permute-start(f32[4096,256]{1,0:T(8,128)} %add_select_fusion.1), channel_id=1, source_target_pairs={{0,8},{4,12},{8,0},{12,4},{16,24},{20,28},{24,16},{28,20},{1,9},{5... | collective-permute-start | bytes 12582920 | tf_op jit(solution)/shard_map/ppermute | solution.py:10
  229.4 98.8 %copy-start = (s32[256]{0:T(256)S(1)}, s32[256]{0:T(256)}, u32[]{:S(2)}) copy-start(s32[256]{0:T(256)} %param.6) | copy-start | bytes 3076
  325.4 181.4 %collective-permute-start.4 = (f32[4096,256]{1,0:T(8,128)}, f32[4096,256]{1,0:T(8,128)}, u32[]{:S(2)}, u32[]{:S(2)}) collective-permute-start(f32[4096,256]{1,0:T(8,128)} %add_select_fusion), channel_id=1, source_target_pairs={{0,16},{4,20},{8,24},{12,28},{16,0},{20,4},{24,8},{28,12},{1,17},{... | collective-permute-start | bytes 12582920 | tf_op jit(solution)/shard_map/ppermute | solution.py:10
  516.8 89.8 %all-reduce.2.cloned.1.call-start = ((), (), s32[]{:S(2)}) async-start(), calls=%async_computation.1 | async-start | bytes 131072 | tf_op jit(solution)/shard_map/psum | solution.py:53
Sparse Core Ops, SparseCore 0:
  516.9 17.1 all-gather.1
  538.0 68.4 all-reduce.1
where the time goes:
time: 615 us
  waiting for transfers between devices  544 us (88%)
  other arithmetic  35.4 us (6%)
  between operations  14.8 us (2%)
  starting transfers between devices  8.85 us (1%)
  matrix products  8.34 us (1%)
    ppermute x5, waiting for transfers between devices, partner_2(): lax.ppermute(value, axis, [(i, i ^ 1 << distance) for i in range(lax.axis...  457 us
    psum x1, waiting for transfers between devices, local(): block = lax.psum(partial_block, 'rx')  69.6 us
    select_n x4, other arithmetic, local(): mixed = jnp.where(upper, partner - mixed, mixed + partner)  23.8 us
    all_gather x1, waiting for transfers between devices, local(): piece = lax.all_gather(sketch, 'ry', axis=0, tiled=True)  17.2 us
  transfers between devices with their start and end apart: 7, of which 7 were waited for; matrix products, arithmetic and copies ran while one was open for 0% of the time, Pallas kernels for 0%

commit v1 on v0

v1 whole, which is shorter than its diff:
```python
import functools

import jax
import jax.numpy as jnp
from jax import lax
from jax.experimental import pallas as pl
from jax.experimental.pallas import tpu as pltpu
from jax.sharding import PartitionSpec as P

BLK = 128
MESH_AXES = ("rx", "ry")
GRANT = 12 * 2**20
WIDE = 46 * 2**20
AHEAD = 3
REST = 4


def swap(value, bits):
    size = lax.axis_size("rx") * lax.axis_size("ry")
    return lax.ppermute(value, MESH_AXES, [(i, i ^ bits) for i in range(size)])


def parity_sign(both):
    for shift in (4, 2, 1):
        both = jnp.bitwise_xor(both, jnp.right_shift(both, shift))
    return 1 - 2 * jnp.bitwise_and(both, 1)


def transform_kernel(full, chunks, me_ref, signs_ref, other_signs_ref, *refs):
    matrix_refs, table_ref, buffer_refs, sems = refs[:2], refs[2], refs[3:5], refs[5]
    rows, cols = table_ref.shape[0] // 2, table_ref.shape[1]
    step = rows // chunks

    def fetch(chunk):
        at = pl.ds(chunk * step, step)
        return [
            pltpu.make_async_copy(matrix_ref.at[at, :], buffer_ref.at[at, :], sems.at[chunk, which])
            for which, (matrix_ref, buffer_ref) in enumerate(zip(matrix_refs, buffer_refs))
        ]

    for chunk in range(AHEAD):
        for copy in fetch(chunk):
            copy.start()
    down = lax.broadcasted_iota(jnp.int32, (BLK, BLK), 0)
    across = lax.broadcasted_iota(jnp.int32, (BLK, BLK), 1)
    order = parity_sign(jnp.bitwise_and(down, across))
    upper = jnp.bitwise_and(jnp.right_shift(me_ref[0], full - 1), 1)
    own_order = order * (1 - 2 * upper)
    for chunk in range(chunks):
        for copy in fetch(chunk):
            copy.wait()
        if chunk + AHEAD < chunks:
            for copy in fetch(chunk + AHEAD):
                copy.start()
        for block in range(chunk * step // BLK, (chunk + 1) * step // BLK):
            at = block * BLK
            weights, values = [], []
            for signed, sign_ref, buffer_ref in zip((own_order, order), (signs_ref, other_signs_ref), buffer_refs):
                row = sign_ref.shape[0] - rows // BLK + block
                weights += [(signed * sign_ref[row:row + 1, :]).astype(jnp.float32).astype(jnp.bfloat16)] * 2
                whole = buffer_ref[at:at + BLK, :]
                high = whole.astype(jnp.bfloat16)
                values += [high, (whole - high.astype(jnp.float32)).astype(jnp.bfloat16)]
            mixed = jnp.dot(
                jnp.concatenate(weights, axis=1),
                jnp.concatenate(values, axis=0),
                preferred_element_type=jnp.float32,
            )
            for half in range(2):
                table_ref[pl.ds(2 * at + half, BLK, stride=2), :] = mixed[:, half * cols:(half + 1) * cols]


def join_kernel(*refs):
    *list_refs, out_ref = refs
    for at, list_ref in enumerate(list_refs):
        rows = list_ref.shape[0]
        out_ref[at * rows:(at + 1) * rows, :] = list_ref[...]


def specs(smem, vmem):
    return [pl.BlockSpec(memory_space=pltpu.SMEM)] * smem + [pl.BlockSpec(memory_space=pltpu.VMEM)] * vmem


def floats(*shape):
    return jax.ShapeDtypeStruct(shape, jnp.float32)


def transform(full, me, matrix, signs, other_matrix, other_signs):
    rows, width = matrix.shape
    chunks = 8
    return pl.pallas_call(
        functools.partial(transform_kernel, full, chunks),
        in_specs=specs(1, 2) + [pl.BlockSpec(memory_space=pl.ANY)] * 2,
        out_specs=specs(0, 1)[0],
        out_shape=floats(2 * rows, width // 2),
        scratch_shapes=[pltpu.VMEM((rows, width), jnp.float32)] * 2 + [pltpu.SemaphoreType.DMA((chunks, 2))],
        compiler_params=pltpu.CompilerParams(vmem_limit_bytes=WIDE),
        cost_estimate=pl.CostEstimate(
            flops=16 * rows * BLK * width, bytes_accessed=12 * rows * width, transcendentals=0
        ),
        name="transform",
    )(me, signs, other_signs, matrix, other_matrix)


def pick_rows(geometry, me, list_refs, table_ref, out_ref, row, pick, start, slots):
    stride, full, scale = geometry
    unroll = 32
    group = jnp.right_shift(me, full)
    sign = parity_sign(jnp.bitwise_and(jnp.bitwise_xor(group, pick), group)).astype(jnp.float32) * scale
    list_ref = list_refs[pick % 4]
    base = pick // 4 * stride
    live = jnp.clip(list_ref[base + stride - BLK] - start, 0, slots)

    def body(step, carry):
        first = step * unroll
        for u in range(unroll):
            out_ref[row + first + u] = table_ref[list_ref[base + start + first + u]] * sign
        return carry

    lax.fori_loop(0, pl.cdiv(live, unroll), body, 0)


def distances(x, y):
    return [x | y << 1 | a << 2 | b << 3 for a in range(2) for b in range(2)]


def gather(geometry, parts, me_ref, *refs):
    list_refs, table_ref, out_refs = refs[:4], refs[4], refs[-len(parts):]
    for (start, slots, picks), out_ref in zip(parts, out_refs):
        for at, pick in enumerate(picks):
            pick_rows(geometry, me_ref[0], list_refs, table_ref, out_ref, at * slots, pick, start, slots)


def call(kernel, name, scalars, arrays, outs, after=(), scratch=(), flops=0):
    moved = 4 * sum(x.size for x in arrays) + 4 * sum(x.size for x in outs)
    return pl.pallas_call(
        kernel,
        in_specs=specs(len(scalars), len(arrays)) + [pl.BlockSpec(memory_space=pl.ANY)] * len(after),
        out_specs=specs(0, len(outs)),
        out_shape=list(outs),
        scratch_shapes=list(scratch),
        compiler_params=pltpu.CompilerParams(vmem_limit_bytes=GRANT),
        cost_estimate=pl.CostEstimate(flops=flops, bytes_accessed=moved, transcendentals=0),
        name=name,
    )(*scalars, *arrays, *after)


def gram_kernel(ry_ref, live_ref, *refs):
    *part_refs, sketch_ref, on_ref, mine_ref, next_ref, rows_ref, blocks_ref = refs
    slots, cols = rows_ref.shape[0] // 2, rows_ref.shape[1]
    start = 0
    for near_ref, add_ref in zip(part_refs[::2], part_refs[1::2]):
        rows_ref[start:start + near_ref.shape[0], :] = near_ref[...] + add_ref[...]
        start += near_ref.shape[0]
    values = jnp.concatenate([rows_ref[pl.ds(half, slots, stride=2), :] for half in range(2)], axis=1)
    live = lax.broadcasted_iota(jnp.int32, values.shape, 0) < live_ref[0]
    values = jnp.where(live, values, 0.0)
    sketch_ref[...] = values
    high = values.astype(jnp.bfloat16)
    low = (values - high.astype(jnp.float32)).astype(jnp.bfloat16)
    total = lax.dot_general(
        jnp.concatenate([high, high, low], axis=0),
        jnp.concatenate([high, low, high], axis=0),
        (((0,), (0,)), ((), ())),
        preferred_element_type=jnp.float32,
    )
    for block in range(4):
        a, b = block // 2, block % 2
        blocks_ref[block] = total[a * cols:(a + 1) * cols, b * cols:(b + 1) * cols]
    ry = ry_ref[0]
    mine_ref[...] = blocks_ref[ry]
    on_ref[:cols, :] = blocks_ref[jnp.bitwise_xor(ry, 1)]
    next_ref[...] = blocks_ref[jnp.bitwise_xor(ry, 2)]
    on_ref[cols:, :] = blocks_ref[jnp.bitwise_xor(ry, 3)]


def local(matrix, signs, indices, counts):
    rows, width = matrix.shape
    slots = indices.shape[0]
    cols = width // 2
    tail = slots // 4
    head = slots - tail
    first = slots // 8 * 3
    size_x = lax.axis_size("rx")
    size_y = lax.axis_size("ry")
    size = size_x * size_y
    full = size.bit_length() - 1 - REST
    assert full >= 1 and size_y == 4
    ry = lax.axis_index("ry")
    me = lax.axis_index("rx") * size_y + ry
    scale = 1.0 / (size * BLK) ** 0.5
    stride = slots + BLK

    me_one = me.astype(jnp.int32).reshape(1)
    signs = signs.reshape(rows // BLK, BLK)
    if full > 1:
        matrix = (matrix.reshape(rows // BLK, BLK, width) * signs[:, :, None].astype(jnp.float32)).reshape(rows, width)
        signs = jnp.ones_like(signs)
    for bit in range(full - 1):
        other = swap(matrix, 1 << bit)
        matrix = jnp.where(jnp.bitwise_and(jnp.right_shift(me, bit), 1) == 1, other - matrix, matrix + other)
    own = jnp.concatenate([indices, jnp.broadcast_to(counts, (BLK,)), signs.reshape(-1)]).reshape(-1, BLK)
    own = lax.optimization_barrier(own)
    own_list = own[:stride // BLK]
    last = 1 << (full - 1)
    table = transform(full, me_one, matrix, own, swap(matrix, last), swap(own, last)).reshape(rows, 2, cols)
    column_lists = [own_list] + [swap(own_list, step << full) for step in (4, 8, 12)]
    (joined,) = call(
        join_kernel, "join", (), column_lists, (jax.ShapeDtypeStruct((4 * stride // BLK, BLK), jnp.int32),)
    )
    lists = [joined.reshape(-1)] + [swap(joined, step << full).reshape(-1) for step in (1, 2, 3)]

    geometry = (stride, full, scale)
    scalars = (me_one, *lists)

    def gathered(name, parts, after=()):
        outs = [floats(slots * len(picks), 2, cols) for _, slots, picks in parts]
        kernel = functools.partial(gather, geometry, parts)
        return [x.reshape(-1, cols) for x in call(kernel, name, scalars, (table,), outs, after=after)]

    a, b = (0, first), (first, head - first)
    *fars, end_on = gathered(
        "gather_far",
        [
            (*a, distances(1, 0) + distances(1, 1)),
            (*b, distances(0, 1) + distances(1, 1)),
            (head, tail, [z + near for z in (4, 12) for near in (0, 2, 1, 3)]),
        ],
    )
    end_add = swap(end_on, 4 << full)
    ends = gathered("gather_end", [(head, tail, [z + near for near in (0, 2, 1, 3)]) for z in (0, 8)])
    nears = gathered(
        "gather_near",
        [(*a, distances(0, 0)), (*a, distances(0, 1)), (*b, distances(0, 0)), (*b, distances(1, 0))],
        after=(end_add,),
    )

    def halved(value):
        middle = value.shape[0] // 2
        return value[:middle], value[middle:]

    for bits in (8, 1, 2):
        end, end_on = (own + add for own, add in zip(ends, halved(end_add)))
        end_add = swap(end_on, bits << full)
        ends = halved(end)

    finals = []
    for stays, far, steps in ((nears[:2], fars[0], (1, 2, 4, 8)), (nears[2:], fars[1], (2, 1, 4, 8))):
        for step in steps[:-1]:
            near, far = (own + add for own, add in zip(stays, halved(swap(far, step << full))))
            stays = halved(near)
        finals += [near, swap(far, steps[-1] << full)]

    sketch, on, block, far_block = call(
        gram_kernel,
        "gram",
        (ry.astype(jnp.int32).reshape(1), counts),
        (*finals, end, end_add),
        (floats(slots, width), floats(2 * cols, cols), floats(cols, cols), floats(cols, cols)),
        scratch=[pltpu.VMEM((2 * slots, cols), jnp.float32), pltpu.VMEM((4, cols, cols), jnp.float32)],
        flops=6 * slots * width * width,
    )
    got = swap(on, 1)
    block, far_block = block + got[:cols], far_block + got[cols:]
    block = block + swap(far_block, 2) + swap(block, size_y) + swap(far_block, 2 + size_y)
    at, bits = 1, size_x.bit_length() - 1
    while at < bits:
        together = min(2, bits - at)
        block = sum([swap(block, size_y * (step << at)) for step in range(1, 2**together)], block)
        at += together
    return sketch, (block * (1.0 / (size * slots)))[None]


def solution(mesh):
    in_specs = (P(("rx", "ry"), None), P(("rx", "ry")), P(("rx", "ry")), P(("rx", "ry")))
    out_specs = (P(("rx", "ry"), None), P("ry", None, None))
    return jax.shard_map(local, mesh=mesh, in_specs=in_specs, out_specs=out_specs, check_vma=False)
```

time: 615 us -> 86.3 us (0.14)
  waiting for transfers between devices: 544 us -> 32.9 us
  other arithmetic: 35.4 us -> 1.89 us
  starting transfers between devices: 8.85 us -> 37.4 us
  between operations: 14.8 us -> 1.41 us
  Pallas kernels: 0 us -> 12.4 us
  matrix products: 8.34 us -> 0 us
    ppermute x5 -> x27, waiting for transfers between devices: 457 us -> 32.9 us  [swap(): return lax.ppermute(value, MESH_AXES, [(i, i ^ bits) for i in range(size)])]
    psum x1 -> x0, waiting for transfers between devices: 69.6 us -> none  [local(): block = lax.psum(partial_block, 'rx')]
    ppermute x5 -> x27, starting transfers between devices: 8.77 us -> 37.4 us  [swap(): return lax.ppermute(value, MESH_AXES, [(i, i ^ bits) for i in range(size)])]
    select_n x6 -> x0, other arithmetic: 24.7 us -> none  [the longest x4 23.8 us: local(): mixed = jnp.where(upper, partner - mixed, mixed + partner)]
    all_gather x1 -> x0, waiting for transfers between devices: 17.2 us -> none  [local(): piece = lax.all_gather(sketch, 'ry', axis=0, tiled=True)]
    pallas_call x0 -> x6, Pallas kernels: none -> 12.4 us  [the longest x5 7.68 us: call(): pl.pallas_call(kernel, in_specs=specs(len(scalars), len(arrays)) + [pl.Bl...]
    mul x2 -> x0, other arithmetic: 8.54 us -> none  [the longest x1 5.96 us: local(): mixed = mixed * (1.0 / (size_x * size_y * BLK) ** 0.5)]
    dot_general x2 -> x0, matrix products: 8.34 us -> none  [the longest x1 5.51 us: local(): jnp.einsum('ij,bjc->bic', hadamard(BLK), blocks, precision=lax.Precision....]
  transfers between devices with their start and end apart: 7 -> 27, of which waited for: 7 -> 14; matrix products, arithmetic and copies ran while one was open for 0% -> 1% of each run, Pallas kernels for 0% -> 10%
where the time goes in v1:
time: 86.3 us; the launch traced here: 86 us
  starting transfers between devices  37.4 us (43%)
  waiting for transfers between devices  32.9 us (38%)
  Pallas kernels  12.4 us (14%)
  other arithmetic  1.89 us (2%)
  between operations  1.41 us (2%)
    ppermute x27, starting transfers between devices, swap(): return lax.ppermute(value, MESH_AXES, [(i, i ^ bits) for i in range(size)])  37.4 us
    ppermute x27, waiting for transfers between devices, swap(): return lax.ppermute(value, MESH_AXES, [(i, i ^ bits) for i in range(size)])  32.9 us
    pallas_call x5, Pallas kernels, call(): pl.pallas_call(kernel, in_specs=specs(len(scalars), len(arrays)) + [pl.Bl...  7.68 us
    pallas_call x1, Pallas kernels, transform(): pl.pallas_call(functools.partial(transform_kernel, full, chunks), in_spec...  4.69 us
  transfers between devices with their start and end apart: 27, of which 14 were waited for; matrix products, arithmetic and copies ran while one was open for 1% of the time, Pallas kernels for 10%

profile of v1, /device:TPU:0, one launch (start us, length us, event | category | flops | bytes accessed | tf_op | source)
XLA Modules:
  0.0 86.0 jit_solution(7867470868599733408)
XLA Ops:
  0.6 0.5 collective-permute-start.7
  1.8 0.7 add_bitcast_fusion.signs_ref
  2.5 0.1 collective-permute-start.6
  2.6 5.0 %collective-permute-start.2 = (s32[3,128]{1,0:T(4,128)S(1)}, s32[3,128]{1,0:T(4,128)S(1)}, u32[]{:S(2)}, u32[]{:S(2)}) collective-permute-start(s32[3,128]{1,0:T(4,128)S(1)} %slice.132.refs_0_), channel_id=1, source_target_pairs={{0,24},{1,25},{2,26},{3,27},{4,28},{5,29},{6,30},{7,31},{8,16},{9,... | collective-permute-start | bytes 4616 | tf_op jit(solution)/shard_map/ppermute | solution.py:20
  7.7 0.0 collective-permute-start.1
  7.7 0.6 collective-permute-start
  8.2 1.0 %collective-permute-done.2.refs_3_ = s32[3,128]{1,0:T(4,128)S(1)} collective-permute-done((s32[3,128]{1,0:T(4,128)S(1)}, s32[3,128]{1,0:T(4,128)S(1)}, u32[]{:S(2)}, u32[]{:S(2)}) %collective-permute-start.2) | collective-permute-done | bytes 1568 | tf_op jit(solution)/shard_map/ppermute | solution.py:20
  9.2 2.9 %collective-permute-done.1.refs_2_ = s32[3,128]{1,0:T(4,128)S(1)} collective-permute-done((s32[3,128]{1,0:T(4,128)S(1)}, s32[3,128]{1,0:T(4,128)S(1)}, u32[]{:S(2)}, u32[]{:S(2)}) %collective-permute-start.1) | collective-permute-done | bytes 1568 | tf_op jit(solution)/shard_map/ppermute | solution.py:20
  12.1 0.0 collective-permute-done.refs_1_
  12.1 2.4 %collective-permute-start.5 = (s32[12,128]{1,0:T(8,128)S(1)}, s32[12,128]{1,0:T(8,128)S(1)}, u32[]{:S(2)}, u32[]{:S(2)}) collective-permute-start(s32[12,128]{1,0:T(8,128)S(1)} %join.1), channel_id=1, source_target_pairs={{0,6},{1,7},{2,4},{3,5},{4,2},{5,3},{6,0},{7,1},{8,14},{9,15},{10,... | collective-permute-start | bytes 18440 | tf_op jit(solution)/shard_map/ppermute | solution.py:20
  14.6 0.5 collective-permute-start.4
  15.1 0.5 collective-permute-start.3
  15.6 0.0 collective-permute-done.6.other_signs_ref
  15.6 0.0 collective-permute-done.7.refs_1_
  15.6 4.7 %transform.1 = f32[8192,128]{1,0:T(8,128)S(1)} custom-call(s32[1]{0:T(128)} %bitcast.1.me_ref, s32[35,128]{1,0:T(8,128)S(1)} %add_bitcast_fusion.signs_ref, s32[35,128]{1,0:T(8,128)S(1)} %collective-permute-done.6.other_signs_ref, f32[4096,256]{1,0:T(8,128)} %refs_0_.1, f32[4096,256]{1,0:T(8,128)} %collective-permute-done.7.refs_1_), custom_call_target="tpu_custom_call" | custom-call | flops 2147483648 | bytes 12582912 | tf_op jit(solution)/shard_map/transform/pallas_call | solution.py:91
  20.3 0.0 collective-permute-done.5
  20.3 0.0 collective-permute-done.4
  20.4 0.0 collective-permute-done.3
  20.4 3.1 %gather_far.1 = (f32[768,2,128]{2,1,0:T(2,128)S(1)}, f32[768,2,128]{2,1,0:T(2,128)S(1)}, f32[512,2,128]{2,1,0:T(2,128)S(1)}) custom-call(s32[1]{0:T(128)} %bitcast.1.me_ref, s32[1536]{0:T(1024)S(1)} %bitcast.31, s32[1536]{0:T(1024)S(1)} %bitcast.40, s32[1536]{0:T(1024)S(1)} %bitcast.37, s32[1536]{0:T(1024)S(1)} %bitcast.34, f32[4096,2,128]{2,1,0:T(2,128)S(1)} %bitcast.22), custom_call_target="tpu_custom_call" | custom-call | bytes 6291456 | tf_op jit(solution)/shard_map/gather_far/pallas_call | solution.py:136
  23.5 1.6 %collective-permute-start.9 = (f32[1536,128]{1,0:T(8,128)S(1)}, f32[1536,128]{1,0:T(8,128)S(1)}, u32[]{:S(2)}, u32[]{:S(2)}) collective-permute-start(f32[1536,128]{1,0:T(8,128)S(1)} %bitcast.44), channel_id=1, source_target_pairs={{0,2},{1,3},{2,0},{3,1},{4,6},{5,7},{6,4},{7,5},{8,10},{9,11},{10,... | collective-permute-start | bytes 2359304 | tf_op jit(solution)/shard_map/ppermute | solution.py:20
  25.1 1.5 %collective-permute-start.13 = (f32[1536,128]{1,0:T(8,128)S(1)}, f32[1536,128]{1,0:T(8,128)S(1)}, u32[]{:S(2)}, u32[]{:S(2)}) collective-permute-start(f32[1536,128]{1,0:T(8,128)S(1)} %bitcast.43), channel_id=1, source_target_pairs={{0,4},{1,5},{2,6},{3,7},{4,0},{5,1},{6,2},{7,3},{8,12},{9,13},{10,... | collective-permute-start | bytes 2359304 | tf_op jit(solution)/shard_map/ppermute | solution.py:20
  26.5 1.1 %gather_end.1 = (f32[256,2,128]{2,1,0:T(2,128)S(1)}, f32[256,2,128]{2,1,0:T(2,128)S(1)}) custom-call(s32[1]{0:T(128)} %bitcast.1.me_ref, s32[1536]{0:T(1024)S(1)} %bitcast.32, s32[1536]{0:T(1024)S(1)} %bitcast.41, s32[1536]{0:T(1024)S(1)} %bitcast.38, s32[1536]{0:T(1024)S(1)} %bitcast.35, f32[4096,2,128]{2,1,0:T(2,128)S(1)} %bitcast.23), custom_call_target="tpu_custom_call" | custom-call | bytes 4718592 | tf_op jit(solution)/shard_map/gather_end/pallas_call | solution.py:136
  27.6 8.6 %collective-permute-done.8.refs_5_ = f32[1024,128]{1,0:T(8,128)S(1)} collective-permute-done((f32[1024,128]{1,0:T(8,128)S(1)}, f32[1024,128]{1,0:T(8,128)S(1)}, u32[]{:S(2)}, u32[]{:S(2)}) %collective-permute-start.8) | collective-permute-done | bytes 524320 | tf_op jit(solution)/shard_map/ppermute | solution.py:20
  36.2 0.1 slice_add_fusion.5
  36.3 2.9 %collective-permute-start.17 = (f32[512,128]{1,0:T(8,128)S(1)}, f32[512,128]{1,0:T(8,128)S(1)}, u32[]{:S(2)}, u32[]{:S(2)}) collective-permute-start(f32[512,128]{1,0:T(8,128)S(1)} %get-tuple-element.39), channel_id=1, source_target_pairs={{0,16},{1,17},{2,18},{3,19},{4,20},{5,21},{6,22},{7,23},{8,24},{9,... | collective-permute-start | bytes 786440 | tf_op jit(solution)/shard_map/ppermute | solution.py:20
  39.2 2.7 %gather_near.1 = (f32[384,2,128]{2,1,0:T(2,128)S(1)}, f32[384,2,128]{2,1,0:T(2,128)S(1)}, f32[384,2,128]{2,1,0:T(2,128)S(1)}, f32[384,2,128]{2,1,0:T(2,128)S(1)}) custom-call(s32[1]{0:T(128)} %bitcast.1.me_ref, s32[1536]{0:T(1024)S(1)} %bitcast.33, s32[1536]{0:T(1024)S(1)} %bitcast.42, s32[1536]{0:T(1024)S(1)} %bitcast.39, s32[1536]{0:T(1024)S(1)} %bitcast.36, ...), custom_call_target="tpu_custom_call" | custom-call | bytes 5767168 | tf_op jit(solution)/shard_map/gather_near/pallas_call | solution.py:136
  41.8 0.0 collective-permute-done.9
  41.9 0.1 slice_add_fusion.3
  41.9 1.6 %collective-permute-start.10 = (f32[768,128]{1,0:T(8,128)S(1)}, f32[768,128]{1,0:T(8,128)S(1)}, u32[]{:S(2)}, u32[]{:S(2)}) collective-permute-start(f32[768,128]{1,0:T(8,128)S(1)} %get-tuple-element.35), channel_id=1, source_target_pairs={{0,4},{1,5},{2,6},{3,7},{4,0},{5,1},{6,2},{7,3},{8,12},{9,13},{10,... | collective-permute-start | bytes 1179656 | tf_op jit(solution)/shard_map/ppermute | solution.py:20
  43.5 0.0 collective-permute-done.13
  43.5 0.1 slice_add_fusion.1
  43.7 0.6 collective-permute-start.14
  44.3 2.9 %collective-permute-done.17 = f32[512,128]{1,0:T(8,128)S(1)} collective-permute-done((f32[512,128]{1,0:T(8,128)S(1)}, f32[512,128]{1,0:T(8,128)S(1)}, u32[]{:S(2)}, u32[]{:S(2)}) %collective-permute-start.17) | collective-permute-done | bytes 262176 | tf_op jit(solution)/shard_map/ppermute | solution.py:20
  47.2 0.6 collective-permute-start.18
  47.8 2.3 %collective-permute-done.10 = f32[768,128]{1,0:T(8,128)S(1)} collective-permute-done((f32[768,128]{1,0:T(8,128)S(1)}, f32[768,128]{1,0:T(8,128)S(1)}, u32[]{:S(2)}, u32[]{:S(2)}) %collective-permute-start.10) | collective-permute-done | bytes 393248 | tf_op jit(solution)/shard_map/ppermute | solution.py:20
  50.1 0.1 slice_add_fusion.9
  50.2 1.8 %collective-permute-start.11 = (f32[384,128]{1,0:T(8,128)S(1)}, f32[384,128]{1,0:T(8,128)S(1)}, u32[]{:S(2)}, u32[]{:S(2)}) collective-permute-start(f32[384,128]{1,0:T(8,128)S(1)} %get-tuple-element.33), channel_id=1, source_target_pairs={{0,8},{1,9},{2,10},{3,11},{4,12},{5,13},{6,14},{7,15},{8,0},{9,1},... | collective-permute-start | bytes 589832 | tf_op jit(solution)/shard_map/ppermute | solution.py:20
  52.0 0.9 %collective-permute-done.14 = f32[768,128]{1,0:T(8,128)S(1)} collective-permute-done((f32[768,128]{1,0:T(8,128)S(1)}, f32[768,128]{1,0:T(8,128)S(1)}, u32[]{:S(2)}, u32[]{:S(2)}) %collective-permute-start.14) | collective-permute-done | bytes 393248 | tf_op jit(solution)/shard_map/ppermute | solution.py:20
  52.9 0.1 slice_add_fusion.7
  53.0 1.6 %collective-permute-start.15 = (f32[384,128]{1,0:T(8,128)S(1)}, f32[384,128]{1,0:T(8,128)S(1)}, u32[]{:S(2)}, u32[]{:S(2)}) collective-permute-start(f32[384,128]{1,0:T(8,128)S(1)} %get-tuple-element.29), channel_id=1, source_target_pairs={{0,8},{1,9},{2,10},{3,11},{4,12},{5,13},{6,14},{7,15},{8,0},{9,1},... | collective-permute-start | bytes 589832 | tf_op jit(solution)/shard_map/ppermute | solution.py:20
  54.5 2.8 %collective-permute-done.11 = f32[384,128]{1,0:T(8,128)S(1)} collective-permute-done((f32[384,128]{1,0:T(8,128)S(1)}, f32[384,128]{1,0:T(8,128)S(1)}, u32[]{:S(2)}, u32[]{:S(2)}) %collective-permute-start.11) | collective-permute-done | bytes 196640 | tf_op jit(solution)/shard_map/ppermute | solution.py:20
  57.4 2.9 %collective-permute-start.12 = (f32[192,128]{1,0:T(8,128)S(1)}, f32[192,128]{1,0:T(8,128)S(1)}, u32[]{:S(2)}, u32[]{:S(2)}) collective-permute-start(f32[192,128]{1,0:T(8,128)S(1)} %get-tuple-element.42), channel_id=1, source_target_pairs={{0,16},{1,17},{2,18},{3,19},{4,20},{5,21},{6,22},{7,23},{8,24},{9,... | collective-permute-start | bytes 294920 | tf_op jit(solution)/shard_map/ppermute | solution.py:20
  60.3 0.1 collective-permute-done.15
  60.4 3.0 %collective-permute-start.16 = (f32[192,128]{1,0:T(8,128)S(1)}, f32[192,128]{1,0:T(8,128)S(1)}, u32[]{:S(2)}, u32[]{:S(2)}) collective-permute-start(f32[192,128]{1,0:T(8,128)S(1)} %get-tuple-element.40), channel_id=1, source_target_pairs={{0,16},{1,17},{2,18},{3,19},{4,20},{5,21},{6,22},{7,23},{8,24},{9,... | collective-permute-start | bytes 294920 | tf_op jit(solution)/shard_map/ppermute | solution.py:20
  63.4 0.0 collective-permute-done.18
  63.4 1.8 %collective-permute-start.19 = (f32[128,128]{1,0:T(8,128)S(1)}, f32[128,128]{1,0:T(8,128)S(1)}, u32[]{:S(2)}, u32[]{:S(2)}) collective-permute-start(f32[128,128]{1,0:T(8,128)S(1)} %get-tuple-element.44), channel_id=1, source_target_pairs={{0,4},{1,5},{2,6},{3,7},{4,0},{5,1},{6,2},{7,3},{8,12},{9,13},{10,... | collective-permute-start | bytes 196616 | tf_op jit(solution)/shard_map/ppermute | solution.py:20
  65.2 2.5 %collective-permute-done.19.refs_5_ = f32[128,128]{1,0:T(8,128)S(1)} collective-permute-done((f32[128,128]{1,0:T(8,128)S(1)}, f32[128,128]{1,0:T(8,128)S(1)}, u32[]{:S(2)}, u32[]{:S(2)}) %collective-permute-start.19) | collective-permute-done | bytes 65568 | tf_op jit(solution)/shard_map/ppermute | solution.py:20
  67.8 0.0 collective-permute-done.12.refs_1_
  67.8 0.0 collective-permute-done.16.refs_3_
  67.8 0.8 gram.1
  68.6 0.0 collective-permute-start.20
  68.6 1.3 %collective-permute-done.20 = f32[256,128]{1,0:T(8,128)S(1)} collective-permute-done((f32[256,128]{1,0:T(8,128)S(1)}, f32[256,128]{1,0:T(8,128)S(1)}, u32[]{:S(2)}, u32[]{:S(2)}) %collective-permute-start.20) | collective-permute-done | bytes 131104 | tf_op jit(solution)/shard_map/ppermute | solution.py:20
  69.9 1.8 %collective-permute-start.22 = (f32[128,128]{1,0:T(8,128)S(1)}, f32[128,128]{1,0:T(8,128)S(1)}, u32[]{:S(2)}, u32[]{:S(2)}) collective-permute-start(f32[128,128]{1,0:T(8,128)S(1)} %get-tuple-element.46), channel_id=1, source_target_pairs={{0,4},{1,5},{2,6},{3,7},{4,0},{5,1},{6,2},{7,3},{8,12},{9,13},{10,... | collective-permute-start | bytes 196616 | tf_op jit(solution)/shard_map/ppermute | solution.py:20
  71.7 1.8 %collective-permute-start.21 = (f32[128,128]{1,0:T(8,128)S(1)}, f32[128,128]{1,0:T(8,128)S(1)}, u32[]{:S(2)}, u32[]{:S(2)}) collective-permute-start(f32[128,128]{1,0:T(8,128)S(1)} %get-tuple-element.47), channel_id=1, source_target_pairs={{0,2},{1,3},{2,0},{3,1},{4,6},{5,7},{6,4},{7,5},{8,10},{9,11},{10,... | collective-permute-start | bytes 196616 | tf_op jit(solution)/shard_map/ppermute | solution.py:20
  73.5 0.8 collective-permute-done.22
  74.3 2.9 %collective-permute-done.23 = f32[128,128]{1,0:T(8,128)S(1)} collective-permute-done((f32[128,128]{1,0:T(8,128)S(1)}, f32[128,128]{1,0:T(8,128)S(1)}, u32[]{:S(2)}, u32[]{:S(2)}) %collective-permute-start.23) | collective-permute-done | bytes 65568 | tf_op jit(solution)/shard_map/ppermute | solution.py:20
  77.2 0.0 collective-permute-done.21
  77.2 2.5 %collective-permute-start.26 = (f32[128,128]{1,0:T(8,128)S(1)}, f32[128,128]{1,0:T(8,128)S(1)}, u32[]{:S(2)}, u32[]{:S(2)}) collective-permute-start(f32[128,128]{1,0:T(8,128)S(1)} %add_add_fusion), channel_id=1, source_target_pairs={{0,24},{1,25},{2,26},{3,27},{4,28},{5,29},{6,30},{7,31},{8,16},{9,... | collective-permute-start | bytes 196616 | tf_op jit(solution)/shard_map/ppermute | solution.py:20
  79.7 0.0 collective-permute-start.25
  79.7 1.9 %collective-permute-start.24 = (f32[128,128]{1,0:T(8,128)S(1)}, f32[128,128]{1,0:T(8,128)S(1)}, u32[]{:S(2)}, u32[]{:S(2)}) collective-permute-start(f32[128,128]{1,0:T(8,128)S(1)} %add_add_fusion), channel_id=1, source_target_pairs={{0,8},{1,9},{2,10},{3,11},{4,12},{5,13},{6,14},{7,15},{8,0},{9,1},... | collective-permute-start | bytes 196616 | tf_op jit(solution)/shard_map/ppermute | solution.py:20
  81.7 2.4 %collective-permute-done.26 = f32[128,128]{1,0:T(8,128)S(1)} collective-permute-done((f32[128,128]{1,0:T(8,128)S(1)}, f32[128,128]{1,0:T(8,128)S(1)}, u32[]{:S(2)}, u32[]{:S(2)}) %collective-permute-start.26) | collective-permute-done | bytes 65568 | tf_op jit(solution)/shard_map/ppermute | solution.py:20
  84.1 1.3 %collective-permute-done.25 = f32[128,128]{1,0:T(8,128)S(1)} collective-permute-done((f32[128,128]{1,0:T(8,128)S(1)}, f32[128,128]{1,0:T(8,128)S(1)}, u32[]{:S(2)}, u32[]{:S(2)}) %collective-permute-start.25) | collective-permute-done | bytes 65568 | tf_op jit(solution)/shard_map/ppermute | solution.py:20
  85.3 0.0 collective-permute-done.24
  85.4 0.6 multiply_bitcast_fusion
  (11 shorter events, 0.1 us)
Async XLA Ops:
  0.6 15.0 %collective-permute-start.7 = (f32[4096,256]{1,0:T(8,128)}, f32[4096,256]{1,0:T(8,128)}, u32[]{:S(2)}, u32[]{:S(2)}) collective-permute-start(f32[4096,256]{1,0:T(8,128)} %refs_0_.1), channel_id=1, source_target_pairs={{0,1},{1,0},{2,3},{3,2},{4,5},{5,4},{6,7},{7,6},{8,9},{9,8},{10,11... | collective-permute-start | bytes 12582920 | tf_op jit(solution)/shard_map/ppermute | solution.py:20
  2.5 13.1 %collective-permute-start.6 = (s32[35,128]{1,0:T(8,128)S(1)}, s32[35,128]{1,0:T(8,128)S(1)}, u32[]{:S(2)}, u32[]{:S(2)}) collective-permute-start(s32[35,128]{1,0:T(8,128)S(1)} %add_bitcast_fusion.signs_ref), channel_id=1, source_target_pairs={{0,1},{1,0},{2,3},{3,2},{4,5},{5,4},{6,7},{7,6},{8,9},{9,8},{10,11... | collective-permute-start | bytes 53768 | tf_op jit(solution)/shard_map/ppermute | solution.py:20
  2.6 6.6 %collective-permute-start.2 = (s32[3,128]{1,0:T(4,128)S(1)}, s32[3,128]{1,0:T(4,128)S(1)}, u32[]{:S(2)}, u32[]{:S(2)}) collective-permute-start(s32[3,128]{1,0:T(4,128)S(1)} %slice.132.refs_0_), channel_id=1, source_target_pairs={{0,24},{1,25},{2,26},{3,27},{4,28},{5,29},{6,30},{7,31},{8,16},{9,... | collective-permute-start | bytes 4616 | tf_op jit(solution)/shard_map/ppermute | solution.py:20
  7.7 4.5 %collective-permute-start.1 = (s32[3,128]{1,0:T(4,128)S(1)}, s32[3,128]{1,0:T(4,128)S(1)}, u32[]{:S(2)}, u32[]{:S(2)}) collective-permute-start(s32[3,128]{1,0:T(4,128)S(1)} %slice.132.refs_0_), channel_id=1, source_target_pairs={{0,16},{1,17},{2,18},{3,19},{4,20},{5,21},{6,22},{7,23},{8,24},{9,... | collective-permute-start | bytes 4616 | tf_op jit(solution)/shard_map/ppermute | solution.py:20
  7.7 4.5 %collective-permute-start = (s32[3,128]{1,0:T(4,128)S(1)}, s32[3,128]{1,0:T(4,128)S(1)}, u32[]{:S(2)}, u32[]{:S(2)}) collective-permute-start(s32[3,128]{1,0:T(4,128)S(1)} %slice.132.refs_0_), channel_id=1, source_target_pairs={{0,8},{1,9},{2,10},{3,11},{4,12},{5,13},{6,14},{7,15},{8,0},{9,1},... | collective-permute-start | bytes 4616 | tf_op jit(solution)/shard_map/ppermute | solution.py:20
  12.1 8.2 %collective-permute-start.5 = (s32[12,128]{1,0:T(8,128)S(1)}, s32[12,128]{1,0:T(8,128)S(1)}, u32[]{:S(2)}, u32[]{:S(2)}) collective-permute-start(s32[12,128]{1,0:T(8,128)S(1)} %join.1), channel_id=1, source_target_pairs={{0,6},{1,7},{2,4},{3,5},{4,2},{5,3},{6,0},{7,1},{8,14},{9,15},{10,... | collective-permute-start | bytes 18440 | tf_op jit(solution)/shard_map/ppermute | solution.py:20
  14.6 5.8 %collective-permute-start.4 = (s32[12,128]{1,0:T(8,128)S(1)}, s32[12,128]{1,0:T(8,128)S(1)}, u32[]{:S(2)}, u32[]{:S(2)}) collective-permute-start(s32[12,128]{1,0:T(8,128)S(1)} %join.1), channel_id=1, source_target_pairs={{0,4},{1,5},{2,6},{3,7},{4,0},{5,1},{6,2},{7,3},{8,12},{9,13},{10,... | collective-permute-start | bytes 18440 | tf_op jit(solution)/shard_map/ppermute | solution.py:20
  15.1 5.3 %collective-permute-start.3 = (s32[12,128]{1,0:T(8,128)S(1)}, s32[12,128]{1,0:T(8,128)S(1)}, u32[]{:S(2)}, u32[]{:S(2)}) collective-permute-start(s32[12,128]{1,0:T(8,128)S(1)} %join.1), channel_id=1, source_target_pairs={{0,2},{1,3},{2,0},{3,1},{4,6},{5,7},{6,4},{7,5},{8,10},{9,11},{10,... | collective-permute-start | bytes 18440 | tf_op jit(solution)/shard_map/ppermute | solution.py:20
  23.5 18.3 %collective-permute-start.9 = (f32[1536,128]{1,0:T(8,128)S(1)}, f32[1536,128]{1,0:T(8,128)S(1)}, u32[]{:S(2)}, u32[]{:S(2)}) collective-permute-start(f32[1536,128]{1,0:T(8,128)S(1)} %bitcast.44), channel_id=1, source_target_pairs={{0,2},{1,3},{2,0},{3,1},{4,6},{5,7},{6,4},{7,5},{8,10},{9,11},{10,... | collective-permute-start | bytes 2359304 | tf_op jit(solution)/shard_map/ppermute | solution.py:20
  25.1 11.1 %collective-permute-start.8 = (f32[1024,128]{1,0:T(8,128)S(1)}, f32[1024,128]{1,0:T(8,128)S(1)}, u32[]{:S(2)}, u32[]{:S(2)}) collective-permute-start(f32[1024,128]{1,0:T(8,128)S(1)} %bitcast.45), channel_id=1, source_target_pairs={{0,8},{1,9},{2,10},{3,11},{4,12},{5,13},{6,14},{7,15},{8,0},{9,1},... | collective-permute-start | bytes 1572872 | tf_op jit(solution)/shard_map/ppermute | solution.py:20
  25.1 18.5 %collective-permute-start.13 = (f32[1536,128]{1,0:T(8,128)S(1)}, f32[1536,128]{1,0:T(8,128)S(1)}, u32[]{:S(2)}, u32[]{:S(2)}) collective-permute-start(f32[1536,128]{1,0:T(8,128)S(1)} %bitcast.43), channel_id=1, source_target_pairs={{0,4},{1,5},{2,6},{3,7},{4,0},{5,1},{6,2},{7,3},{8,12},{9,13},{10,... | collective-permute-start | bytes 2359304 | tf_op jit(solution)/shard_map/ppermute | solution.py:20
  36.3 11.0 %collective-permute-start.17 = (f32[512,128]{1,0:T(8,128)S(1)}, f32[512,128]{1,0:T(8,128)S(1)}, u32[]{:S(2)}, u32[]{:S(2)}) collective-permute-start(f32[512,128]{1,0:T(8,128)S(1)} %get-tuple-element.39), channel_id=1, source_target_pairs={{0,16},{1,17},{2,18},{3,19},{4,20},{5,21},{6,22},{7,23},{8,24},{9,... | collective-permute-start | bytes 786440 | tf_op jit(solution)/shard_map/ppermute | solution.py:20
  41.9 8.2 %collective-permute-start.10 = (f32[768,128]{1,0:T(8,128)S(1)}, f32[768,128]{1,0:T(8,128)S(1)}, u32[]{:S(2)}, u32[]{:S(2)}) collective-permute-start(f32[768,128]{1,0:T(8,128)S(1)} %get-tuple-element.35), channel_id=1, source_target_pairs={{0,4},{1,5},{2,6},{3,7},{4,0},{5,1},{6,2},{7,3},{8,12},{9,13},{10,... | collective-permute-start | bytes 1179656 | tf_op jit(solution)/shard_map/ppermute | solution.py:20
  43.7 9.2 %collective-permute-start.14 = (f32[768,128]{1,0:T(8,128)S(1)}, f32[768,128]{1,0:T(8,128)S(1)}, u32[]{:S(2)}, u32[]{:S(2)}) collective-permute-start(f32[768,128]{1,0:T(8,128)S(1)} %get-tuple-element.31), channel_id=1, source_target_pairs={{0,2},{1,3},{2,0},{3,1},{4,6},{5,7},{6,4},{7,5},{8,10},{9,11},{10,... | collective-permute-start | bytes 1179656 | tf_op jit(solution)/shard_map/ppermute | solution.py:20
  47.2 16.2 %collective-permute-start.18 = (f32[256,128]{1,0:T(8,128)S(1)}, f32[256,128]{1,0:T(8,128)S(1)}, u32[]{:S(2)}, u32[]{:S(2)}) collective-permute-start(f32[256,128]{1,0:T(8,128)S(1)} %get-tuple-element.37), channel_id=1, source_target_pairs={{0,2},{1,3},{2,0},{3,1},{4,6},{5,7},{6,4},{7,5},{8,10},{9,11},{10,... | collective-permute-start | bytes 393224 | tf_op jit(solution)/shard_map/ppermute | solution.py:20
  50.2 7.2 %collective-permute-start.11 = (f32[384,128]{1,0:T(8,128)S(1)}, f32[384,128]{1,0:T(8,128)S(1)}, u32[]{:S(2)}, u32[]{:S(2)}) collective-permute-start(f32[384,128]{1,0:T(8,128)S(1)} %get-tuple-element.33), channel_id=1, source_target_pairs={{0,8},{1,9},{2,10},{3,11},{4,12},{5,13},{6,14},{7,15},{8,0},{9,1},... | collective-permute-start | bytes 589832 | tf_op jit(solution)/shard_map/ppermute | solution.py:20
  53.0 7.4 %collective-permute-start.15 = (f32[384,128]{1,0:T(8,128)S(1)}, f32[384,128]{1,0:T(8,128)S(1)}, u32[]{:S(2)}, u32[]{:S(2)}) collective-permute-start(f32[384,128]{1,0:T(8,128)S(1)} %get-tuple-element.29), channel_id=1, source_target_pairs={{0,8},{1,9},{2,10},{3,11},{4,12},{5,13},{6,14},{7,15},{8,0},{9,1},... | collective-permute-start | bytes 589832 | tf_op jit(solution)/shard_map/ppermute | solution.py:20
  57.4 10.4 %collective-permute-start.12 = (f32[192,128]{1,0:T(8,128)S(1)}, f32[192,128]{1,0:T(8,128)S(1)}, u32[]{:S(2)}, u32[]{:S(2)}) collective-permute-start(f32[192,128]{1,0:T(8,128)S(1)} %get-tuple-element.42), channel_id=1, source_target_pairs={{0,16},{1,17},{2,18},{3,19},{4,20},{5,21},{6,22},{7,23},{8,24},{9,... | collective-permute-start | bytes 294920 | tf_op jit(solution)/shard_map/ppermute | solution.py:20
  60.4 7.4 %collective-permute-start.16 = (f32[192,128]{1,0:T(8,128)S(1)}, f32[192,128]{1,0:T(8,128)S(1)}, u32[]{:S(2)}, u32[]{:S(2)}) collective-permute-start(f32[192,128]{1,0:T(8,128)S(1)} %get-tuple-element.40), channel_id=1, source_target_pairs={{0,16},{1,17},{2,18},{3,19},{4,20},{5,21},{6,22},{7,23},{8,24},{9,... | collective-permute-start | bytes 294920 | tf_op jit(solution)/shard_map/ppermute | solution.py:20
  63.4 4.3 %collective-permute-start.19 = (f32[128,128]{1,0:T(8,128)S(1)}, f32[128,128]{1,0:T(8,128)S(1)}, u32[]{:S(2)}, u32[]{:S(2)}) collective-permute-start(f32[128,128]{1,0:T(8,128)S(1)} %get-tuple-element.44), channel_id=1, source_target_pairs={{0,4},{1,5},{2,6},{3,7},{4,0},{5,1},{6,2},{7,3},{8,12},{9,13},{10,... | collective-permute-start | bytes 196616 | tf_op jit(solution)/shard_map/ppermute | solution.py:20
  68.6 1.3 %collective-permute-start.20 = (f32[256,128]{1,0:T(8,128)S(1)}, f32[256,128]{1,0:T(8,128)S(1)}, u32[]{:S(2)}, u32[]{:S(2)}) collective-permute-start(f32[256,128]{1,0:T(8,128)S(1)} %get-tuple-element.26), channel_id=1, source_target_pairs={{0,1},{1,0},{2,3},{3,2},{4,5},{5,4},{6,7},{7,6},{8,9},{9,8},{10,11... | collective-permute-start | bytes 393224 | tf_op jit(solution)/shard_map/ppermute | solution.py:20
  69.9 4.4 %collective-permute-start.22 = (f32[128,128]{1,0:T(8,128)S(1)}, f32[128,128]{1,0:T(8,128)S(1)}, u32[]{:S(2)}, u32[]{:S(2)}) collective-permute-start(f32[128,128]{1,0:T(8,128)S(1)} %get-tuple-element.46), channel_id=1, source_target_pairs={{0,4},{1,5},{2,6},{3,7},{4,0},{5,1},{6,2},{7,3},{8,12},{9,13},{10,... | collective-permute-start | bytes 196616 | tf_op jit(solution)/shard_map/ppermute | solution.py:20
  71.7 5.5 %collective-permute-start.23 = (f32[128,128]{1,0:T(8,128)S(1)}, f32[128,128]{1,0:T(8,128)S(1)}, u32[]{:S(2)}, u32[]{:S(2)}) collective-permute-start(f32[128,128]{1,0:T(8,128)S(1)} %get-tuple-element.47), channel_id=1, source_target_pairs={{0,6},{1,7},{2,4},{3,5},{4,2},{5,3},{6,0},{7,1},{8,14},{9,15},{10,... | collective-permute-start | bytes 196616 | tf_op jit(solution)/shard_map/ppermute | solution.py:20
  71.7 5.5 %collective-permute-start.21 = (f32[128,128]{1,0:T(8,128)S(1)}, f32[128,128]{1,0:T(8,128)S(1)}, u32[]{:S(2)}, u32[]{:S(2)}) collective-permute-start(f32[128,128]{1,0:T(8,128)S(1)} %get-tuple-element.47), channel_id=1, source_target_pairs={{0,2},{1,3},{2,0},{3,1},{4,6},{5,7},{6,4},{7,5},{8,10},{9,11},{10,... | collective-permute-start | bytes 196616 | tf_op jit(solution)/shard_map/ppermute | solution.py:20
  77.2 6.8 %collective-permute-start.26 = (f32[128,128]{1,0:T(8,128)S(1)}, f32[128,128]{1,0:T(8,128)S(1)}, u32[]{:S(2)}, u32[]{:S(2)}) collective-permute-start(f32[128,128]{1,0:T(8,128)S(1)} %add_add_fusion), channel_id=1, source_target_pairs={{0,24},{1,25},{2,26},{3,27},{4,28},{5,29},{6,30},{7,31},{8,16},{9,... | collective-permute-start | bytes 196616 | tf_op jit(solution)/shard_map/ppermute | solution.py:20
  79.7 5.6 %collective-permute-start.25 = (f32[128,128]{1,0:T(8,128)S(1)}, f32[128,128]{1,0:T(8,128)S(1)}, u32[]{:S(2)}, u32[]{:S(2)}) collective-permute-start(f32[128,128]{1,0:T(8,128)S(1)} %add_add_fusion), channel_id=1, source_target_pairs={{0,16},{1,17},{2,18},{3,19},{4,20},{5,21},{6,22},{7,23},{8,24},{9,... | collective-permute-start | bytes 196616 | tf_op jit(solution)/shard_map/ppermute | solution.py:20
  79.7 5.6 %collective-permute-start.24 = (f32[128,128]{1,0:T(8,128)S(1)}, f32[128,128]{1,0:T(8,128)S(1)}, u32[]{:S(2)}, u32[]{:S(2)}) collective-permute-start(f32[128,128]{1,0:T(8,128)S(1)} %add_add_fusion), channel_id=1, source_target_pairs={{0,8},{1,9},{2,10},{3,11},{4,12},{5,13},{6,14},{7,15},{8,0},{9,1},... | collective-permute-start | bytes 196616 | tf_op jit(solution)/shard_map/ppermute | solution.py:20

commit v2 on v1

--- a/solution.py
+++ b/solution.py
@@ -45,7 +45,9 @@
     across = lax.broadcasted_iota(jnp.int32, (BLK, BLK), 1)
     order = parity_sign(jnp.bitwise_and(down, across))
     upper = jnp.bitwise_and(jnp.right_shift(me_ref[0], full - 1), 1)
-    own_order = order * (1 - 2 * upper)
+    last = signs_ref.shape[0] - rows // BLK
+    signs = signs_ref[last:, :] * (1 - 2 * upper)
+    both = (signs * other_signs_ref[last:, :]).astype(jnp.float32).T
     for chunk in range(chunks):
         for copy in fetch(chunk):
             copy.wait()
@@ -54,16 +56,14 @@
                 copy.start()
         for block in range(chunk * step // BLK, (chunk + 1) * step // BLK):
             at = block * BLK
-            weights, values = [], []
-            for signed, sign_ref, buffer_ref in zip((own_order, order), (signs_ref, other_signs_ref), buffer_refs):
-                row = sign_ref.shape[0] - rows // BLK + block
-                weights += [(signed * sign_ref[row:row + 1, :]).astype(jnp.float32).astype(jnp.bfloat16)] * 2
-                whole = buffer_ref[at:at + BLK, :]
-                high = whole.astype(jnp.bfloat16)
-                values += [high, (whole - high.astype(jnp.float32)).astype(jnp.bfloat16)]
+            weights = (order * signs[block:block + 1, :]).astype(jnp.float32).astype(jnp.bfloat16)
+            own, other = (buffer_ref[at:at + BLK, :] for buffer_ref in buffer_refs)
+            values = own + both[:, block:block + 1] * other
+            high = values.astype(jnp.bfloat16)
+            low = (values - high.astype(jnp.float32)).astype(jnp.bfloat16)
             mixed = jnp.dot(
-                jnp.concatenate(weights, axis=1),
-                jnp.concatenate(values, axis=0),
+                jnp.concatenate([weights, weights], axis=1),
+                jnp.concatenate([high, low], axis=0),
                 preferred_element_type=jnp.float32,
             )
             for half in range(2):
@@ -104,7 +104,7 @@
 
 def pick_rows(geometry, me, list_refs, table_ref, out_ref, row, pick, start, slots):
     stride, full, scale = geometry
-    unroll = 32
+    unroll = max(u for u in range(1, 33) if slots % u == 0)
     group = jnp.right_shift(me, full)
     sign = parity_sign(jnp.bitwise_and(jnp.bitwise_xor(group, pick), group)).astype(jnp.float32) * scale
     list_ref = list_refs[pick % 4]
@@ -178,7 +178,7 @@
     rows, width = matrix.shape
     slots = indices.shape[0]
     cols = width // 2
-    tail = slots // 4
+    tail = slots // 32 * 9
     head = slots - tail
     first = slots // 8 * 3
     size_x = lax.axis_size("rx")

time: 86.3 us -> 87.2 us (1.010)
  waiting for transfers between devices: 32.9 us -> 36.7 us
  starting transfers between devices: 37.4 us -> 33.8 us
    ppermute x27, waiting for transfers between devices: 32.9 us -> 36.7 us  [swap(): return lax.ppermute(value, MESH_AXES, [(i, i ^ bits) for i in range(size)])]
    ppermute x27, starting transfers between devices: 37.4 us -> 33.8 us  [swap(): return lax.ppermute(value, MESH_AXES, [(i, i ^ bits) for i in range(size)])]
where the time goes in v2:
time: 87.2 us; the launch traced here: 86.7 us
  waiting for transfers between devices  36.7 us (42%)
  starting transfers between devices  33.8 us (39%)
  Pallas kernels  12.8 us (15%)
  other arithmetic  1.86 us (2%)
  between operations  1.42 us (2%)
    ppermute x27, waiting for transfers between devices, swap(): return lax.ppermute(value, MESH_AXES, [(i, i ^ bits) for i in range(size)])  36.7 us
    ppermute x27, starting transfers between devices, swap(): return lax.ppermute(value, MESH_AXES, [(i, i ^ bits) for i in range(size)])  33.8 us
    pallas_call x5, Pallas kernels, call(): pl.pallas_call(kernel, in_specs=specs(len(scalars), len(arrays)) + [pl.Bl...  8.04 us
    pallas_call x1, Pallas kernels, transform(): pl.pallas_call(functools.partial(transform_kernel, full, chunks), in_spec...  4.78 us
  transfers between devices with their start and end apart: 27, of which 14 were waited for; matrix products, arithmetic and copies ran while one was open for 1% of the time, Pallas kernels for 10%

profile of v2, /device:TPU:0, one launch (start us, length us, event | category | flops | bytes accessed | tf_op | source)
XLA Modules:
  0.0 86.7 jit_solution(8118606293792336993)
XLA Ops:
  0.6 0.5 collective-permute-start.7
  1.8 0.7 add_bitcast_fusion.signs_ref
  2.5 0.1 collective-permute-start.6
  2.6 5.0 %collective-permute-start.2 = (s32[3,128]{1,0:T(4,128)S(1)}, s32[3,128]{1,0:T(4,128)S(1)}, u32[]{:S(2)}, u32[]{:S(2)}) collective-permute-start(s32[3,128]{1,0:T(4,128)S(1)} %slice.132.refs_0_), channel_id=1, source_target_pairs={{0,24},{1,25},{2,26},{3,27},{4,28},{5,29},{6,30},{7,31},{8,16},{9,... | collective-permute-start | bytes 4616 | tf_op jit(solution)/shard_map/ppermute | solution.py:20
  7.7 0.0 collective-permute-start.1
  7.7 0.6 collective-permute-start
  8.2 1.0 %collective-permute-done.2.refs_3_ = s32[3,128]{1,0:T(4,128)S(1)} collective-permute-done((s32[3,128]{1,0:T(4,128)S(1)}, s32[3,128]{1,0:T(4,128)S(1)}, u32[]{:S(2)}, u32[]{:S(2)}) %collective-permute-start.2) | collective-permute-done | bytes 1568 | tf_op jit(solution)/shard_map/ppermute | solution.py:20
  9.2 2.9 %collective-permute-done.1.refs_2_ = s32[3,128]{1,0:T(4,128)S(1)} collective-permute-done((s32[3,128]{1,0:T(4,128)S(1)}, s32[3,128]{1,0:T(4,128)S(1)}, u32[]{:S(2)}, u32[]{:S(2)}) %collective-permute-start.1) | collective-permute-done | bytes 1568 | tf_op jit(solution)/shard_map/ppermute | solution.py:20
  12.1 0.0 collective-permute-done.refs_1_
  12.1 2.4 %collective-permute-start.5 = (s32[12,128]{1,0:T(8,128)S(1)}, s32[12,128]{1,0:T(8,128)S(1)}, u32[]{:S(2)}, u32[]{:S(2)}) collective-permute-start(s32[12,128]{1,0:T(8,128)S(1)} %join.1), channel_id=1, source_target_pairs={{0,6},{1,7},{2,4},{3,5},{4,2},{5,3},{6,0},{7,1},{8,14},{9,15},{10,... | collective-permute-start | bytes 18440 | tf_op jit(solution)/shard_map/ppermute | solution.py:20
  14.6 0.5 collective-permute-start.4
  15.1 0.5 collective-permute-start.3
  15.6 0.0 collective-permute-done.6.other_signs_ref
  15.6 0.0 collective-permute-done.7.refs_1_
  15.6 4.8 %transform.1 = f32[8192,128]{1,0:T(8,128)S(1)} custom-call(s32[1]{0:T(128)} %bitcast.1.me_ref, s32[35,128]{1,0:T(8,128)S(1)} %add_bitcast_fusion.signs_ref, s32[35,128]{1,0:T(8,128)S(1)} %collective-permute-done.6.other_signs_ref, f32[4096,256]{1,0:T(8,128)} %refs_0_.1, f32[4096,256]{1,0:T(8,128)} %collective-permute-done.7.refs_1_), custom_call_target="tpu_custom_call" | custom-call | flops 2147483648 | bytes 12582912 | tf_op jit(solution)/shard_map/transform/pallas_call | solution.py:91
  20.4 0.0 collective-permute-done.5
  20.4 0.0 collective-permute-done.4
  20.4 0.0 collective-permute-done.3
  20.5 3.2 %gather_far.1 = (f32[768,2,128]{2,1,0:T(2,128)S(1)}, f32[704,2,128]{2,1,0:T(2,128)S(1)}, f32[576,2,128]{2,1,0:T(2,128)S(1)}) custom-call(s32[1]{0:T(128)} %bitcast.1.me_ref, s32[1536]{0:T(1024)S(1)} %bitcast.31, s32[1536]{0:T(1024)S(1)} %bitcast.40, s32[1536]{0:T(1024)S(1)} %bitcast.37, s32[1536]{0:T(1024)S(1)} %bitcast.34, f32[4096,2,128]{2,1,0:T(2,128)S(1)} %bitcast.22), custom_call_target="tpu_custom_call" | custom-call | bytes 6291456 | tf_op jit(solution)/shard_map/gather_far/pallas_call | solution.py:136
  23.6 0.1 collective-permute-start.8
  23.7 1.4 %collective-permute-start.13 = (f32[1408,128]{1,0:T(8,128)S(1)}, f32[1408,128]{1,0:T(8,128)S(1)}, u32[]{:S(2)}, u32[]{:S(2)}) collective-permute-start(f32[1408,128]{1,0:T(8,128)S(1)} %bitcast.44), channel_id=1, source_target_pairs={{0,4},{1,5},{2,6},{3,7},{4,0},{5,1},{6,2},{7,3},{8,12},{9,13},{10,... | collective-permute-start | bytes 2162696 | tf_op jit(solution)/shard_map/ppermute | solution.py:20
  25.1 1.5 %collective-permute-start.9 = (f32[1536,128]{1,0:T(8,128)S(1)}, f32[1536,128]{1,0:T(8,128)S(1)}, u32[]{:S(2)}, u32[]{:S(2)}) collective-permute-start(f32[1536,128]{1,0:T(8,128)S(1)} %bitcast.43), channel_id=1, source_target_pairs={{0,2},{1,3},{2,0},{3,1},{4,6},{5,7},{6,4},{7,5},{8,10},{9,11},{10,... | collective-permute-start | bytes 2359304 | tf_op jit(solution)/shard_map/ppermute | solution.py:20
  26.6 1.5 %gather_end.1 = (f32[288,2,128]{2,1,0:T(2,128)S(1)}, f32[288,2,128]{2,1,0:T(2,128)S(1)}) custom-call(s32[1]{0:T(128)} %bitcast.1.me_ref, s32[1536]{0:T(1024)S(1)} %bitcast.32, s32[1536]{0:T(1024)S(1)} %bitcast.41, s32[1536]{0:T(1024)S(1)} %bitcast.38, s32[1536]{0:T(1024)S(1)} %bitcast.35, f32[4096,2,128]{2,1,0:T(2,128)S(1)} %bitcast.23), custom_call_target="tpu_custom_call" | custom-call | bytes 4784128 | tf_op jit(solution)/shard_map/gather_end/pallas_call | solution.py:136
  28.1 8.6 %collective-permute-done.8.refs_5_ = f32[1152,128]{1,0:T(8,128)S(1)} collective-permute-done((f32[1152,128]{1,0:T(8,128)S(1)}, f32[1152,128]{1,0:T(8,128)S(1)}, u32[]{:S(2)}, u32[]{:S(2)}) %collective-permute-start.8) | collective-permute-done | bytes 589856 | tf_op jit(solution)/shard_map/ppermute | solution.py:20
  36.6 0.1 slice_add_fusion.5
  36.7 2.5 %collective-permute-start.17 = (f32[576,128]{1,0:T(8,128)S(1)}, f32[576,128]{1,0:T(8,128)S(1)}, u32[]{:S(2)}, u32[]{:S(2)}) collective-permute-start(f32[576,128]{1,0:T(8,128)S(1)} %get-tuple-element.39), channel_id=1, source_target_pairs={{0,16},{1,17},{2,18},{3,19},{4,20},{5,21},{6,22},{7,23},{8,24},{9,... | collective-permute-start | bytes 884744 | tf_op jit(solution)/shard_map/ppermute | solution.py:20
  39.2 2.6 %gather_near.1 = (f32[384,2,128]{2,1,0:T(2,128)S(1)}, f32[384,2,128]{2,1,0:T(2,128)S(1)}, f32[352,2,128]{2,1,0:T(2,128)S(1)}, f32[352,2,128]{2,1,0:T(2,128)S(1)}) custom-call(s32[1]{0:T(128)} %bitcast.1.me_ref, s32[1536]{0:T(1024)S(1)} %bitcast.33, s32[1536]{0:T(1024)S(1)} %bitcast.42, s32[1536]{0:T(1024)S(1)} %bitcast.39, s32[1536]{0:T(1024)S(1)} %bitcast.36, ...), custom_call_target="tpu_custom_call" | custom-call | bytes 5701632 | tf_op jit(solution)/shard_map/gather_near/pallas_call | solution.py:136
  41.8 0.0 collective-permute-done.13
  41.8 0.1 slice_add_fusion.3
  41.9 1.7 %collective-permute-start.14 = (f32[704,128]{1,0:T(8,128)S(1)}, f32[704,128]{1,0:T(8,128)S(1)}, u32[]{:S(2)}, u32[]{:S(2)}) collective-permute-start(f32[704,128]{1,0:T(8,128)S(1)} %get-tuple-element.35), channel_id=1, source_target_pairs={{0,2},{1,3},{2,0},{3,1},{4,6},{5,7},{6,4},{7,5},{8,10},{9,11},{10,... | collective-permute-start | bytes 1081352 | tf_op jit(solution)/shard_map/ppermute | solution.py:20
  43.6 0.4 collective-permute-done.9
  44.0 0.1 slice_add_fusion.1
  44.1 1.2 %collective-permute-start.10 = (f32[768,128]{1,0:T(8,128)S(1)}, f32[768,128]{1,0:T(8,128)S(1)}, u32[]{:S(2)}, u32[]{:S(2)}) collective-permute-start(f32[768,128]{1,0:T(8,128)S(1)} %get-tuple-element.31), channel_id=1, source_target_pairs={{0,4},{1,5},{2,6},{3,7},{4,0},{5,1},{6,2},{7,3},{8,12},{9,13},{10,... | collective-permute-start | bytes 1179656 | tf_op jit(solution)/shard_map/ppermute | solution.py:20
  45.3 4.4 %collective-permute-done.17 = f32[576,128]{1,0:T(8,128)S(1)} collective-permute-done((f32[576,128]{1,0:T(8,128)S(1)}, f32[576,128]{1,0:T(8,128)S(1)}, u32[]{:S(2)}, u32[]{:S(2)}) %collective-permute-start.17) | collective-permute-done | bytes 294944 | tf_op jit(solution)/shard_map/ppermute | solution.py:20
  49.7 1.5 %collective-permute-start.18 = (f32[288,128]{1,0:T(8,128)S(1)}, f32[288,128]{1,0:T(8,128)S(1)}, u32[]{:S(2)}, u32[]{:S(2)}) collective-permute-start(f32[288,128]{1,0:T(8,128)S(1)} %get-tuple-element.37), channel_id=1, source_target_pairs={{0,2},{1,3},{2,0},{3,1},{4,6},{5,7},{6,4},{7,5},{8,10},{9,11},{10,... | collective-permute-start | bytes 442376 | tf_op jit(solution)/shard_map/ppermute | solution.py:20
  51.2 0.0 collective-permute-done.14
  51.2 0.1 slice_add_fusion.9
  51.3 1.6 %collective-permute-start.15 = (f32[352,128]{1,0:T(8,128)S(1)}, f32[352,128]{1,0:T(8,128)S(1)}, u32[]{:S(2)}, u32[]{:S(2)}) collective-permute-start(f32[352,128]{1,0:T(8,128)S(1)} %get-tuple-element.33), channel_id=1, source_target_pairs={{0,8},{1,9},{2,10},{3,11},{4,12},{5,13},{6,14},{7,15},{8,0},{9,1},... | collective-permute-start | bytes 540680 | tf_op jit(solution)/shard_map/ppermute | solution.py:20
  52.9 0.0 collective-permute-done.10
  52.9 0.1 slice_add_fusion.7
  53.0 1.7 %collective-permute-start.11 = (f32[384,128]{1,0:T(8,128)S(1)}, f32[384,128]{1,0:T(8,128)S(1)}, u32[]{:S(2)}, u32[]{:S(2)}) collective-permute-start(f32[384,128]{1,0:T(8,128)S(1)} %get-tuple-element.29), channel_id=1, source_target_pairs={{0,8},{1,9},{2,10},{3,11},{4,12},{5,13},{6,14},{7,15},{8,0},{9,1},... | collective-permute-start | bytes 589832 | tf_op jit(solution)/shard_map/ppermute | solution.py:20
  54.7 4.4 %collective-permute-done.15 = f32[352,128]{1,0:T(8,128)S(1)} collective-permute-done((f32[352,128]{1,0:T(8,128)S(1)}, f32[352,128]{1,0:T(8,128)S(1)}, u32[]{:S(2)}, u32[]{:S(2)}) %collective-permute-start.15) | collective-permute-done | bytes 180256 | tf_op jit(solution)/shard_map/ppermute | solution.py:20
  59.2 0.5 collective-permute-start.16
  59.6 2.2 %collective-permute-done.11 = f32[384,128]{1,0:T(8,128)S(1)} collective-permute-done((f32[384,128]{1,0:T(8,128)S(1)}, f32[384,128]{1,0:T(8,128)S(1)}, u32[]{:S(2)}, u32[]{:S(2)}) %collective-permute-start.11) | collective-permute-done | bytes 196640 | tf_op jit(solution)/shard_map/ppermute | solution.py:20
  61.9 0.4 collective-permute-start.12
  62.3 0.0 collective-permute-done.18
  62.3 1.8 %collective-permute-start.19 = (f32[144,128]{1,0:T(8,128)S(1)}, f32[144,128]{1,0:T(8,128)S(1)}, u32[]{:S(2)}, u32[]{:S(2)}) collective-permute-start(f32[144,128]{1,0:T(8,128)S(1)} %get-tuple-element.44), channel_id=1, source_target_pairs={{0,4},{1,5},{2,6},{3,7},{4,0},{5,1},{6,2},{7,3},{8,12},{9,13},{10,... | collective-permute-start | bytes 221192 | tf_op jit(solution)/shard_map/ppermute | solution.py:20
  64.1 2.6 %collective-permute-done.19.refs_5_ = f32[144,128]{1,0:T(8,128)S(1)} collective-permute-done((f32[144,128]{1,0:T(8,128)S(1)}, f32[144,128]{1,0:T(8,128)S(1)}, u32[]{:S(2)}, u32[]{:S(2)}) %collective-permute-start.19) | collective-permute-done | bytes 73760 | tf_op jit(solution)/shard_map/ppermute | solution.py:20
  66.8 1.5 %collective-permute-done.12.refs_1_ = f32[192,128]{1,0:T(8,128)S(1)} collective-permute-done((f32[192,128]{1,0:T(8,128)S(1)}, f32[192,128]{1,0:T(8,128)S(1)}, u32[]{:S(2)}, u32[]{:S(2)}) %collective-permute-start.12) | collective-permute-done | bytes 98336 | tf_op jit(solution)/shard_map/ppermute | solution.py:20
  68.3 0.8 gram.1
  69.0 0.0 collective-permute-start.20
  69.0 1.3 %collective-permute-done.20 = f32[256,128]{1,0:T(8,128)S(1)} collective-permute-done((f32[256,128]{1,0:T(8,128)S(1)}, f32[256,128]{1,0:T(8,128)S(1)}, u32[]{:S(2)}, u32[]{:S(2)}) %collective-permute-start.20) | collective-permute-done | bytes 131104 | tf_op jit(solution)/shard_map/ppermute | solution.py:20
  70.4 2.3 %collective-permute-start.22 = (f32[128,128]{1,0:T(8,128)S(1)}, f32[128,128]{1,0:T(8,128)S(1)}, u32[]{:S(2)}, u32[]{:S(2)}) collective-permute-start(f32[128,128]{1,0:T(8,128)S(1)} %get-tuple-element.46), channel_id=1, source_target_pairs={{0,4},{1,5},{2,6},{3,7},{4,0},{5,1},{6,2},{7,3},{8,12},{9,13},{10,... | collective-permute-start | bytes 196616 | tf_op jit(solution)/shard_map/ppermute | solution.py:20
  72.7 1.5 %collective-permute-start.21 = (f32[128,128]{1,0:T(8,128)S(1)}, f32[128,128]{1,0:T(8,128)S(1)}, u32[]{:S(2)}, u32[]{:S(2)}) collective-permute-start(f32[128,128]{1,0:T(8,128)S(1)} %get-tuple-element.47), channel_id=1, source_target_pairs={{0,2},{1,3},{2,0},{3,1},{4,6},{5,7},{6,4},{7,5},{8,10},{9,11},{10,... | collective-permute-start | bytes 196616 | tf_op jit(solution)/shard_map/ppermute | solution.py:20
  74.3 1.3 %collective-permute-done.22 = f32[128,128]{1,0:T(8,128)S(1)} collective-permute-done((f32[128,128]{1,0:T(8,128)S(1)}, f32[128,128]{1,0:T(8,128)S(1)}, u32[]{:S(2)}, u32[]{:S(2)}) %collective-permute-start.22) | collective-permute-done | bytes 65568 | tf_op jit(solution)/shard_map/ppermute | solution.py:20
  75.5 2.7 %collective-permute-done.23 = f32[128,128]{1,0:T(8,128)S(1)} collective-permute-done((f32[128,128]{1,0:T(8,128)S(1)}, f32[128,128]{1,0:T(8,128)S(1)}, u32[]{:S(2)}, u32[]{:S(2)}) %collective-permute-start.23) | collective-permute-done | bytes 65568 | tf_op jit(solution)/shard_map/ppermute | solution.py:20
  78.2 0.0 collective-permute-done.21
  78.2 1.9 %collective-permute-start.26 = (f32[128,128]{1,0:T(8,128)S(1)}, f32[128,128]{1,0:T(8,128)S(1)}, u32[]{:S(2)}, u32[]{:S(2)}) collective-permute-start(f32[128,128]{1,0:T(8,128)S(1)} %add_add_fusion), channel_id=1, source_target_pairs={{0,24},{1,25},{2,26},{3,27},{4,28},{5,29},{6,30},{7,31},{8,16},{9,... | collective-permute-start | bytes 196616 | tf_op jit(solution)/shard_map/ppermute | solution.py:20
  80.1 0.0 collective-permute-start.25
  80.1 2.5 %collective-permute-start.24 = (f32[128,128]{1,0:T(8,128)S(1)}, f32[128,128]{1,0:T(8,128)S(1)}, u32[]{:S(2)}, u32[]{:S(2)}) collective-permute-start(f32[128,128]{1,0:T(8,128)S(1)} %add_add_fusion), channel_id=1, source_target_pairs={{0,8},{1,9},{2,10},{3,11},{4,12},{5,13},{6,14},{7,15},{8,0},{9,1},... | collective-permute-start | bytes 196616 | tf_op jit(solution)/shard_map/ppermute | solution.py:20
  82.7 1.9 %collective-permute-done.26 = f32[128,128]{1,0:T(8,128)S(1)} collective-permute-done((f32[128,128]{1,0:T(8,128)S(1)}, f32[128,128]{1,0:T(8,128)S(1)}, u32[]{:S(2)}, u32[]{:S(2)}) %collective-permute-start.26) | collective-permute-done | bytes 65568 | tf_op jit(solution)/shard_map/ppermute | solution.py:20
  84.6 1.4 %collective-permute-done.25 = f32[128,128]{1,0:T(8,128)S(1)} collective-permute-done((f32[128,128]{1,0:T(8,128)S(1)}, f32[128,128]{1,0:T(8,128)S(1)}, u32[]{:S(2)}, u32[]{:S(2)}) %collective-permute-start.25) | collective-permute-done | bytes 65568 | tf_op jit(solution)/shard_map/ppermute | solution.py:20
  86.0 0.0 collective-permute-done.24
  86.0 0.6 multiply_bitcast_fusion
  (11 shorter events, 0.1 us)
Async XLA Ops:
  0.6 15.0 %collective-permute-start.7 = (f32[4096,256]{1,0:T(8,128)}, f32[4096,256]{1,0:T(8,128)}, u32[]{:S(2)}, u32[]{:S(2)}) collective-permute-start(f32[4096,256]{1,0:T(8,128)} %refs_0_.1), channel_id=1, source_target_pairs={{0,1},{1,0},{2,3},{3,2},{4,5},{5,4},{6,7},{7,6},{8,9},{9,8},{10,11... | collective-permute-start | bytes 12582920 | tf_op jit(solution)/shard_map/ppermute | solution.py:20
  2.5 13.1 %collective-permute-start.6 = (s32[35,128]{1,0:T(8,128)S(1)}, s32[35,128]{1,0:T(8,128)S(1)}, u32[]{:S(2)}, u32[]{:S(2)}) collective-permute-start(s32[35,128]{1,0:T(8,128)S(1)} %add_bitcast_fusion.signs_ref), channel_id=1, source_target_pairs={{0,1},{1,0},{2,3},{3,2},{4,5},{5,4},{6,7},{7,6},{8,9},{9,8},{10,11... | collective-permute-start | bytes 53768 | tf_op jit(solution)/shard_map/ppermute | solution.py:20
  2.6 6.6 %collective-permute-start.2 = (s32[3,128]{1,0:T(4,128)S(1)}, s32[3,128]{1,0:T(4,128)S(1)}, u32[]{:S(2)}, u32[]{:S(2)}) collective-permute-start(s32[3,128]{1,0:T(4,128)S(1)} %slice.132.refs_0_), channel_id=1, source_target_pairs={{0,24},{1,25},{2,26},{3,27},{4,28},{5,29},{6,30},{7,31},{8,16},{9,... | collective-permute-start | bytes 4616 | tf_op jit(solution)/shard_map/ppermute | solution.py:20
  7.7 4.5 %collective-permute-start.1 = (s32[3,128]{1,0:T(4,128)S(1)}, s32[3,128]{1,0:T(4,128)S(1)}, u32[]{:S(2)}, u32[]{:S(2)}) collective-permute-start(s32[3,128]{1,0:T(4,128)S(1)} %slice.132.refs_0_), channel_id=1, source_target_pairs={{0,16},{1,17},{2,18},{3,19},{4,20},{5,21},{6,22},{7,23},{8,24},{9,... | collective-permute-start | bytes 4616 | tf_op jit(solution)/shard_map/ppermute | solution.py:20
  7.7 4.5 %collective-permute-start = (s32[3,128]{1,0:T(4,128)S(1)}, s32[3,128]{1,0:T(4,128)S(1)}, u32[]{:S(2)}, u32[]{:S(2)}) collective-permute-start(s32[3,128]{1,0:T(4,128)S(1)} %slice.132.refs_0_), channel_id=1, source_target_pairs={{0,8},{1,9},{2,10},{3,11},{4,12},{5,13},{6,14},{7,15},{8,0},{9,1},... | collective-permute-start | bytes 4616 | tf_op jit(solution)/shard_map/ppermute | solution.py:20
  12.1 8.3 %collective-permute-start.5 = (s32[12,128]{1,0:T(8,128)S(1)}, s32[12,128]{1,0:T(8,128)S(1)}, u32[]{:S(2)}, u32[]{:S(2)}) collective-permute-start(s32[12,128]{1,0:T(8,128)S(1)} %join.1), channel_id=1, source_target_pairs={{0,6},{1,7},{2,4},{3,5},{4,2},{5,3},{6,0},{7,1},{8,14},{9,15},{10,... | collective-permute-start | bytes 18440 | tf_op jit(solution)/shard_map/ppermute | solution.py:20
  14.6 5.8 %collective-permute-start.4 = (s32[12,128]{1,0:T(8,128)S(1)}, s32[12,128]{1,0:T(8,128)S(1)}, u32[]{:S(2)}, u32[]{:S(2)}) collective-permute-start(s32[12,128]{1,0:T(8,128)S(1)} %join.1), channel_id=1, source_target_pairs={{0,4},{1,5},{2,6},{3,7},{4,0},{5,1},{6,2},{7,3},{8,12},{9,13},{10,... | collective-permute-start | bytes 18440 | tf_op jit(solution)/shard_map/ppermute | solution.py:20
  15.1 5.4 %collective-permute-start.3 = (s32[12,128]{1,0:T(8,128)S(1)}, s32[12,128]{1,0:T(8,128)S(1)}, u32[]{:S(2)}, u32[]{:S(2)}) collective-permute-start(s32[12,128]{1,0:T(8,128)S(1)} %join.1), channel_id=1, source_target_pairs={{0,2},{1,3},{2,0},{3,1},{4,6},{5,7},{6,4},{7,5},{8,10},{9,11},{10,... | collective-permute-start | bytes 18440 | tf_op jit(solution)/shard_map/ppermute | solution.py:20
  23.6 13.0 %collective-permute-start.8 = (f32[1152,128]{1,0:T(8,128)S(1)}, f32[1152,128]{1,0:T(8,128)S(1)}, u32[]{:S(2)}, u32[]{:S(2)}) collective-permute-start(f32[1152,128]{1,0:T(8,128)S(1)} %bitcast.45), channel_id=1, source_target_pairs={{0,8},{1,9},{2,10},{3,11},{4,12},{5,13},{6,14},{7,15},{8,0},{9,1},... | collective-permute-start | bytes 1769480 | tf_op jit(solution)/shard_map/ppermute | solution.py:20
  23.7 18.1 %collective-permute-start.13 = (f32[1408,128]{1,0:T(8,128)S(1)}, f32[1408,128]{1,0:T(8,128)S(1)}, u32[]{:S(2)}, u32[]{:S(2)}) collective-permute-start(f32[1408,128]{1,0:T(8,128)S(1)} %bitcast.44), channel_id=1, source_target_pairs={{0,4},{1,5},{2,6},{3,7},{4,0},{5,1},{6,2},{7,3},{8,12},{9,13},{10,... | collective-permute-start | bytes 2162696 | tf_op jit(solution)/shard_map/ppermute | solution.py:20
  25.1 18.9 %collective-permute-start.9 = (f32[1536,128]{1,0:T(8,128)S(1)}, f32[1536,128]{1,0:T(8,128)S(1)}, u32[]{:S(2)}, u32[]{:S(2)}) collective-permute-start(f32[1536,128]{1,0:T(8,128)S(1)} %bitcast.43), channel_id=1, source_target_pairs={{0,2},{1,3},{2,0},{3,1},{4,6},{5,7},{6,4},{7,5},{8,10},{9,11},{10,... | collective-permute-start | bytes 2359304 | tf_op jit(solution)/shard_map/ppermute | solution.py:20
  36.7 13.0 %collective-permute-start.17 = (f32[576,128]{1,0:T(8,128)S(1)}, f32[576,128]{1,0:T(8,128)S(1)}, u32[]{:S(2)}, u32[]{:S(2)}) collective-permute-start(f32[576,128]{1,0:T(8,128)S(1)} %get-tuple-element.39), channel_id=1, source_target_pairs={{0,16},{1,17},{2,18},{3,19},{4,20},{5,21},{6,22},{7,23},{8,24},{9,... | collective-permute-start | bytes 884744 | tf_op jit(solution)/shard_map/ppermute | solution.py:20
  41.9 9.3 %collective-permute-start.14 = (f32[704,128]{1,0:T(8,128)S(1)}, f32[704,128]{1,0:T(8,128)S(1)}, u32[]{:S(2)}, u32[]{:S(2)}) collective-permute-start(f32[704,128]{1,0:T(8,128)S(1)} %get-tuple-element.35), channel_id=1, source_target_pairs={{0,2},{1,3},{2,0},{3,1},{4,6},{5,7},{6,4},{7,5},{8,10},{9,11},{10,... | collective-permute-start | bytes 1081352 | tf_op jit(solution)/shard_map/ppermute | solution.py:20
  44.1 8.8 %collective-permute-start.10 = (f32[768,128]{1,0:T(8,128)S(1)}, f32[768,128]{1,0:T(8,128)S(1)}, u32[]{:S(2)}, u32[]{:S(2)}) collective-permute-start(f32[768,128]{1,0:T(8,128)S(1)} %get-tuple-element.31), channel_id=1, source_target_pairs={{0,4},{1,5},{2,6},{3,7},{4,0},{5,1},{6,2},{7,3},{8,12},{9,13},{10,... | collective-permute-start | bytes 1179656 | tf_op jit(solution)/shard_map/ppermute | solution.py:20
  49.7 12.6 %collective-permute-start.18 = (f32[288,128]{1,0:T(8,128)S(1)}, f32[288,128]{1,0:T(8,128)S(1)}, u32[]{:S(2)}, u32[]{:S(2)}) collective-permute-start(f32[288,128]{1,0:T(8,128)S(1)} %get-tuple-element.37), channel_id=1, source_target_pairs={{0,2},{1,3},{2,0},{3,1},{4,6},{5,7},{6,4},{7,5},{8,10},{9,11},{10,... | collective-permute-start | bytes 442376 | tf_op jit(solution)/shard_map/ppermute | solution.py:20
  51.3 7.8 %collective-permute-start.15 = (f32[352,128]{1,0:T(8,128)S(1)}, f32[352,128]{1,0:T(8,128)S(1)}, u32[]{:S(2)}, u32[]{:S(2)}) collective-permute-start(f32[352,128]{1,0:T(8,128)S(1)} %get-tuple-element.33), channel_id=1, source_target_pairs={{0,8},{1,9},{2,10},{3,11},{4,12},{5,13},{6,14},{7,15},{8,0},{9,1},... | collective-permute-start | bytes 540680 | tf_op jit(solution)/shard_map/ppermute | solution.py:20
  53.0 8.9 %collective-permute-start.11 = (f32[384,128]{1,0:T(8,128)S(1)}, f32[384,128]{1,0:T(8,128)S(1)}, u32[]{:S(2)}, u32[]{:S(2)}) collective-permute-start(f32[384,128]{1,0:T(8,128)S(1)} %get-tuple-element.29), channel_id=1, source_target_pairs={{0,8},{1,9},{2,10},{3,11},{4,12},{5,13},{6,14},{7,15},{8,0},{9,1},... | collective-permute-start | bytes 589832 | tf_op jit(solution)/shard_map/ppermute | solution.py:20
  59.2 7.6 %collective-permute-start.16 = (f32[176,128]{1,0:T(8,128)S(1)}, f32[176,128]{1,0:T(8,128)S(1)}, u32[]{:S(2)}, u32[]{:S(2)}) collective-permute-start(f32[176,128]{1,0:T(8,128)S(1)} %get-tuple-element.42), channel_id=1, source_target_pairs={{0,16},{1,17},{2,18},{3,19},{4,20},{5,21},{6,22},{7,23},{8,24},{9,... | collective-permute-start | bytes 270344 | tf_op jit(solution)/shard_map/ppermute | solution.py:20
  61.9 6.4 %collective-permute-start.12 = (f32[192,128]{1,0:T(8,128)S(1)}, f32[192,128]{1,0:T(8,128)S(1)}, u32[]{:S(2)}, u32[]{:S(2)}) collective-permute-start(f32[192,128]{1,0:T(8,128)S(1)} %get-tuple-element.40), channel_id=1, source_target_pairs={{0,16},{1,17},{2,18},{3,19},{4,20},{5,21},{6,22},{7,23},{8,24},{9,... | collective-permute-start | bytes 294920 | tf_op jit(solution)/shard_map/ppermute | solution.py:20
  62.3 4.4 %collective-permute-start.19 = (f32[144,128]{1,0:T(8,128)S(1)}, f32[144,128]{1,0:T(8,128)S(1)}, u32[]{:S(2)}, u32[]{:S(2)}) collective-permute-start(f32[144,128]{1,0:T(8,128)S(1)} %get-tuple-element.44), channel_id=1, source_target_pairs={{0,4},{1,5},{2,6},{3,7},{4,0},{5,1},{6,2},{7,3},{8,12},{9,13},{10,... | collective-permute-start | bytes 221192 | tf_op jit(solution)/shard_map/ppermute | solution.py:20
  69.0 1.3 %collective-permute-start.20 = (f32[256,128]{1,0:T(8,128)S(1)}, f32[256,128]{1,0:T(8,128)S(1)}, u32[]{:S(2)}, u32[]{:S(2)}) collective-permute-start(f32[256,128]{1,0:T(8,128)S(1)} %get-tuple-element.26), channel_id=1, source_target_pairs={{0,1},{1,0},{2,3},{3,2},{4,5},{5,4},{6,7},{7,6},{8,9},{9,8},{10,11... | collective-permute-start | bytes 393224 | tf_op jit(solution)/shard_map/ppermute | solution.py:20
  70.4 5.1 %collective-permute-start.22 = (f32[128,128]{1,0:T(8,128)S(1)}, f32[128,128]{1,0:T(8,128)S(1)}, u32[]{:S(2)}, u32[]{:S(2)}) collective-permute-start(f32[128,128]{1,0:T(8,128)S(1)} %get-tuple-element.46), channel_id=1, source_target_pairs={{0,4},{1,5},{2,6},{3,7},{4,0},{5,1},{6,2},{7,3},{8,12},{9,13},{10,... | collective-permute-start | bytes 196616 | tf_op jit(solution)/shard_map/ppermute | solution.py:20
  72.7 5.5 %collective-permute-start.23 = (f32[128,128]{1,0:T(8,128)S(1)}, f32[128,128]{1,0:T(8,128)S(1)}, u32[]{:S(2)}, u32[]{:S(2)}) collective-permute-start(f32[128,128]{1,0:T(8,128)S(1)} %get-tuple-element.47), channel_id=1, source_target_pairs={{0,6},{1,7},{2,4},{3,5},{4,2},{5,3},{6,0},{7,1},{8,14},{9,15},{10,... | collective-permute-start | bytes 196616 | tf_op jit(solution)/shard_map/ppermute | solution.py:20
  72.7 5.5 %collective-permute-start.21 = (f32[128,128]{1,0:T(8,128)S(1)}, f32[128,128]{1,0:T(8,128)S(1)}, u32[]{:S(2)}, u32[]{:S(2)}) collective-permute-start(f32[128,128]{1,0:T(8,128)S(1)} %get-tuple-element.47), channel_id=1, source_target_pairs={{0,2},{1,3},{2,0},{3,1},{4,6},{5,7},{6,4},{7,5},{8,10},{9,11},{10,... | collective-permute-start | bytes 196616 | tf_op jit(solution)/shard_map/ppermute | solution.py:20
  78.2 6.4 %collective-permute-start.26 = (f32[128,128]{1,0:T(8,128)S(1)}, f32[128,128]{1,0:T(8,128)S(1)}, u32[]{:S(2)}, u32[]{:S(2)}) collective-permute-start(f32[128,128]{1,0:T(8,128)S(1)} %add_add_fusion), channel_id=1, source_target_pairs={{0,24},{1,25},{2,26},{3,27},{4,28},{5,29},{6,30},{7,31},{8,16},{9,... | collective-permute-start | bytes 196616 | tf_op jit(solution)/shard_map/ppermute | solution.py:20
  80.1 5.9 %collective-permute-start.25 = (f32[128,128]{1,0:T(8,128)S(1)}, f32[128,128]{1,0:T(8,128)S(1)}, u32[]{:S(2)}, u32[]{:S(2)}) collective-permute-start(f32[128,128]{1,0:T(8,128)S(1)} %add_add_fusion), channel_id=1, source_target_pairs={{0,16},{1,17},{2,18},{3,19},{4,20},{5,21},{6,22},{7,23},{8,24},{9,... | collective-permute-start | bytes 196616 | tf_op jit(solution)/shard_map/ppermute | solution.py:20
  80.1 5.9 %collective-permute-start.24 = (f32[128,128]{1,0:T(8,128)S(1)}, f32[128,128]{1,0:T(8,128)S(1)}, u32[]{:S(2)}, u32[]{:S(2)}) collective-permute-start(f32[128,128]{1,0:T(8,128)S(1)} %add_add_fusion), channel_id=1, source_target_pairs={{0,8},{1,9},{2,10},{3,11},{4,12},{5,13},{6,14},{7,15},{8,0},{9,1},... | collective-permute-start | bytes 196616 | tf_op jit(solution)/shard_map/ppermute | solution.py:20

commit v3 on v2

--- a/solution.py
+++ b/solution.py
@@ -11,7 +11,7 @@
 MESH_AXES = ("rx", "ry")
 GRANT = 12 * 2**20
 WIDE = 46 * 2**20
-AHEAD = 3
+AHEAD = 2
 REST = 4
 
 
@@ -87,7 +87,7 @@
 
 def transform(full, me, matrix, signs, other_matrix, other_signs):
     rows, width = matrix.shape
-    chunks = 8
+    chunks = 4
     return pl.pallas_call(
         functools.partial(transform_kernel, full, chunks),
         in_specs=specs(1, 2) + [pl.BlockSpec(memory_space=pl.ANY)] * 2,
@@ -145,7 +145,16 @@
     )(*scalars, *arrays, *after)
 
 
-def gram_kernel(ry_ref, live_ref, *refs):
+def sum_kernel(first_ref, first_add_ref, second_ref, second_add_ref, *refs):
+    near_ref, far_ref = refs[-2:]
+    rows = first_ref.shape[0] // 2
+    for at, (own_ref, add_ref) in enumerate(((first_ref, first_add_ref), (second_ref, second_add_ref))):
+        total = own_ref[...] + add_ref[...]
+        near_ref[at * rows:(at + 1) * rows, :] = total[:rows]
+        far_ref[at * rows:(at + 1) * rows, :] = total[rows:]
+
+
+def gram_kernel(ry_ref, list_ref, *refs):
     *part_refs, sketch_ref, on_ref, mine_ref, next_ref, rows_ref, blocks_ref = refs
     slots, cols = rows_ref.shape[0] // 2, rows_ref.shape[1]
     start = 0
@@ -153,7 +162,7 @@
         rows_ref[start:start + near_ref.shape[0], :] = near_ref[...] + add_ref[...]
         start += near_ref.shape[0]
     values = jnp.concatenate([rows_ref[pl.ds(half, slots, stride=2), :] for half in range(2)], axis=1)
-    live = lax.broadcasted_iota(jnp.int32, values.shape, 0) < live_ref[0]
+    live = lax.broadcasted_iota(jnp.int32, values.shape, 0) < list_ref[slots]
     values = jnp.where(live, values, 0.0)
     sketch_ref[...] = values
     high = values.astype(jnp.bfloat16)
@@ -178,9 +187,9 @@
     rows, width = matrix.shape
     slots = indices.shape[0]
     cols = width // 2
-    tail = slots // 32 * 9
+    tail = slots // 16 * 5
     head = slots - tail
-    first = slots // 8 * 3
+    first = head // 2
     size_x = lax.axis_size("rx")
     size_y = lax.axis_size("ry")
     size = size_x * size_y
@@ -199,7 +208,7 @@
     for bit in range(full - 1):
         other = swap(matrix, 1 << bit)
         matrix = jnp.where(jnp.bitwise_and(jnp.right_shift(me, bit), 1) == 1, other - matrix, matrix + other)
-    own = jnp.concatenate([indices, jnp.broadcast_to(counts, (BLK,)), signs.reshape(-1)]).reshape(-1, BLK)
+    own = jnp.concatenate([indices, jnp.pad(counts, (0, BLK - 1)), signs.reshape(-1)]).reshape(-1, BLK)
     own = lax.optimization_barrier(own)
     own_list = own[:stride // BLK]
     last = 1 << (full - 1)
@@ -219,43 +228,59 @@
         return [x.reshape(-1, cols) for x in call(kernel, name, scalars, (table,), outs, after=after)]
 
     a, b = (0, first), (first, head - first)
-    *fars, end_on = gathered(
+    xy = (0, 2, 1, 3)
+    routes = (((4, 12), (0, 8)), ((8, 12), (0, 4)))
+    ends = [(head + at * tail // 2, tail // 2) for at in range(2)]
+    *fars, end_on, other_end_on = gathered(
         "gather_far",
         [
             (*a, distances(1, 0) + distances(1, 1)),
             (*b, distances(0, 1) + distances(1, 1)),
-            (head, tail, [z + near for z in (4, 12) for near in (0, 2, 1, 3)]),
+            *((*end, [z + near for z in sent for near in xy]) for end, (sent, _) in zip(ends, routes)),
         ],
     )
-    end_add = swap(end_on, 4 << full)
-    ends = gathered("gather_end", [(head, tail, [z + near for near in (0, 2, 1, 3)]) for z in (0, 8)])
+    end_adds = [swap(end_on, 4 << full), swap(other_end_on, 8 << full)]
+    end_stays = gathered(
+        "gather_end",
+        [(*end, [z + near for near in xy]) for end, (_, stays) in zip(ends, routes) for z in stays],
+        after=(end_adds[0],),
+    )
     nears = gathered(
         "gather_near",
         [(*a, distances(0, 0)), (*a, distances(0, 1)), (*b, distances(0, 0)), (*b, distances(1, 0))],
-        after=(end_add,),
+        after=(end_adds[0],),
     )
 
     def halved(value):
         middle = value.shape[0] // 2
         return value[:middle], value[middle:]
 
-    for bits in (8, 1, 2):
-        end, end_on = (own + add for own, add in zip(ends, halved(end_add)))
-        end_add = swap(end_on, bits << full)
-        ends = halved(end)
-
-    finals = []
+    finals, seconds = [], []
     for stays, far, steps in ((nears[:2], fars[0], (1, 2, 4, 8)), (nears[2:], fars[1], (2, 1, 4, 8))):
-        for step in steps[:-1]:
+        for at, step in enumerate(steps[:-1]):
             near, far = (own + add for own, add in zip(stays, halved(swap(far, step << full))))
             stays = halved(near)
+            if at == 2 and not seconds:
+                seconds.append(far)
         finals += [near, swap(far, steps[-1] << full)]
+
+    pairs = []
+    for stays, add, step in zip((end_stays[:2], end_stays[2:]), end_adds, (8, 4)):
+        near, far = (own + got for own, got in zip(stays, halved(add)))
+        pairs += [near, swap(far, step << full)]
+    middle = floats(4 * tail, cols)
+    end, end_on = call(sum_kernel, "sum_ends", (), pairs, (middle, middle), after=seconds)
+    own, got = ([part[at * tail:(at + 1) * tail] for at in range(4)] for part in (end, swap(end_on, 1 << full)))
+    last_parts = [
+        jnp.concatenate([own[0] + got[0], own[2] + got[2]]),
+        swap(jnp.concatenate([own[1] + got[1], own[3] + got[3]]), 2 << full),
+    ]
 
     sketch, on, block, far_block = call(
         gram_kernel,
         "gram",
-        (ry.astype(jnp.int32).reshape(1), counts),
-        (*finals, end, end_add),
+        (ry.astype(jnp.int32).reshape(1), lists[0]),
+        (*finals, *last_parts),
         (floats(slots, width), floats(2 * cols, cols), floats(cols, cols), floats(cols, cols)),
         scratch=[pltpu.VMEM((2 * slots, cols), jnp.float32), pltpu.VMEM((4, cols, cols), jnp.float32)],
         flops=6 * slots * width * width,

time: 87.2 us -> 90.6 us (1.039)
  starting transfers between devices: 33.8 us -> 36.1 us
  Pallas kernels: 12.8 us -> 14.1 us
    ppermute x27 -> x29, starting transfers between devices: 33.8 us -> 36.1 us  [swap(): return lax.ppermute(value, MESH_AXES, [(i, i ^ bits) for i in range(size)])]
    pallas_call x5 -> x6, Pallas kernels: 8.04 us -> 9.65 us  [call(): pl.pallas_call(kernel, in_specs=specs(len(scalars), len(arrays)) + [pl.Bl...]
    ppermute x27 -> x29, waiting for transfers between devices: 36.7 us -> 36.9 us  [swap(): return lax.ppermute(value, MESH_AXES, [(i, i ^ bits) for i in range(size)])]
  transfers between devices with their start and end apart: 27 -> 29, of which waited for: 14 -> 15; matrix products, arithmetic and copies ran while one was open for 1% -> 1% of each run, Pallas kernels for 10% -> 10%
where the time goes in v3:
time: 90.6 us; the launch traced here: 90.3 us
  waiting for transfers between devices  36.9 us (41%)
  starting transfers between devices  36.1 us (40%)
  Pallas kernels  14.1 us (16%)
  other arithmetic  1.81 us (2%)
  between operations  1.46 us (2%)
    ppermute x29, waiting for transfers between devices, swap(): return lax.ppermute(value, MESH_AXES, [(i, i ^ bits) for i in range(size)])  36.9 us
    ppermute x29, starting transfers between devices, swap(): return lax.ppermute(value, MESH_AXES, [(i, i ^ bits) for i in range(size)])  36.1 us
    pallas_call x6, Pallas kernels, call(): pl.pallas_call(kernel, in_specs=specs(len(scalars), len(arrays)) + [pl.Bl...  9.65 us
    pallas_call x1, Pallas kernels, transform(): pl.pallas_call(functools.partial(transform_kernel, full, chunks), in_spec...  4.4 us
  transfers between devices with their start and end apart: 29, of which 15 were waited for; matrix products, arithmetic and copies ran while one was open for 1% of the time, Pallas kernels for 10%

profile of v3, /device:TPU:0, one launch (start us, length us, event | category | flops | bytes accessed | tf_op | source)
XLA Modules:
  0.0 90.3 jit_solution(15220272826281631847)
XLA Ops:
  0.6 0.5 collective-permute-start.7
  1.8 0.7 fusion.1.signs_ref
  2.5 0.1 collective-permute-start.6
  2.6 5.0 %collective-permute-start.2 = (s32[3,128]{1,0:T(4,128)S(1)}, s32[3,128]{1,0:T(4,128)S(1)}, u32[]{:S(2)}, u32[]{:S(2)}) collective-permute-start(s32[3,128]{1,0:T(4,128)S(1)} %slice.140.refs_0_), channel_id=1, source_target_pairs={{0,24},{1,25},{2,26},{3,27},{4,28},{5,29},{6,30},{7,31},{8,16},{9,... | collective-permute-start | bytes 4616 | tf_op jit(solution)/shard_map/ppermute | solution.py:20
  7.6 0.0 collective-permute-start.1
  7.6 0.6 collective-permute-start
  8.2 1.0 %collective-permute-done.2.refs_3_ = s32[3,128]{1,0:T(4,128)S(1)} collective-permute-done((s32[3,128]{1,0:T(4,128)S(1)}, s32[3,128]{1,0:T(4,128)S(1)}, u32[]{:S(2)}, u32[]{:S(2)}) %collective-permute-start.2) | collective-permute-done | bytes 1568 | tf_op jit(solution)/shard_map/ppermute | solution.py:20
  9.2 2.9 %collective-permute-done.1.refs_2_ = s32[3,128]{1,0:T(4,128)S(1)} collective-permute-done((s32[3,128]{1,0:T(4,128)S(1)}, s32[3,128]{1,0:T(4,128)S(1)}, u32[]{:S(2)}, u32[]{:S(2)}) %collective-permute-start.1) | collective-permute-done | bytes 1568 | tf_op jit(solution)/shard_map/ppermute | solution.py:20
  12.1 0.0 collective-permute-done.refs_1_
  12.1 2.4 %collective-permute-start.5 = (s32[12,128]{1,0:T(8,128)S(1)}, s32[12,128]{1,0:T(8,128)S(1)}, u32[]{:S(2)}, u32[]{:S(2)}) collective-permute-start(s32[12,128]{1,0:T(8,128)S(1)} %join.1), channel_id=1, source_target_pairs={{0,6},{1,7},{2,4},{3,5},{4,2},{5,3},{6,0},{7,1},{8,14},{9,15},{10,... | collective-permute-start | bytes 18440 | tf_op jit(solution)/shard_map/ppermute | solution.py:20
  14.6 0.5 collective-permute-start.4
  15.1 0.5 collective-permute-start.3
  15.6 0.0 collective-permute-done.6.other_signs_ref
  15.6 0.0 collective-permute-done.7.refs_1_
  15.6 4.4 %transform.1 = f32[8192,128]{1,0:T(8,128)S(1)} custom-call(s32[1]{0:T(128)} %bitcast.3.me_ref, s32[35,128]{1,0:T(8,128)S(1)} %fusion.1.signs_ref, s32[35,128]{1,0:T(8,128)S(1)} %collective-permute-done.6.other_signs_ref, f32[4096,256]{1,0:T(8,128)} %refs_0_.1, f32[4096,256]{1,0:T(8,128)} %collective-permute-done.7.refs_1_), custom_call_target="tpu_custom_call" | custom-call | flops 2147483648 | bytes 12582912 | tf_op jit(solution)/shard_map/transform/pallas_call | solution.py:91
  20.0 0.0 collective-permute-done.5
  20.1 0.0 collective-permute-done.3
  20.1 3.6 %gather_far.1 = (f32[704,2,128]{2,1,0:T(2,128)S(1)}, f32[704,2,128]{2,1,0:T(2,128)S(1)}, f32[320,2,128]{2,1,0:T(2,128)S(1)}, f32[320,2,128]{2,1,0:T(2,128)S(1)}) custom-call(s32[1]{0:T(128)} %bitcast.3.me_ref, s32[1536]{0:T(1024)S(1)} %bitcast.30, s32[1536]{0:T(1024)S(1)} %bitcast.44, s32[1536]{0:T(1024)S(1)} %bitcast.41, s32[1536]{0:T(1024)S(1)} %bitcast.38, ...), custom_call_target="tpu_custom_call" | custom-call | bytes 6291456 | tf_op jit(solution)/shard_map/gather_far/pallas_call | solution.py:136
  23.7 1.6 %collective-permute-start.9 = (f32[1408,128]{1,0:T(8,128)S(1)}, f32[1408,128]{1,0:T(8,128)S(1)}, u32[]{:S(2)}, u32[]{:S(2)}) collective-permute-start(f32[1408,128]{1,0:T(8,128)S(1)} %bitcast.48), channel_id=1, source_target_pairs={{0,2},{1,3},{2,0},{3,1},{4,6},{5,7},{6,4},{7,5},{8,10},{9,11},{10,... | collective-permute-start | bytes 2162696 | tf_op jit(solution)/shard_map/ppermute | solution.py:20
  25.2 0.0 collective-permute-start.8
  25.3 2.1 %collective-permute-start.18 = (f32[640,128]{1,0:T(8,128)S(1)}, f32[640,128]{1,0:T(8,128)S(1)}, u32[]{:S(2)}, u32[]{:S(2)}) collective-permute-start(f32[640,128]{1,0:T(8,128)S(1)} %bitcast.49), channel_id=1, source_target_pairs={{0,16},{1,17},{2,18},{3,19},{4,20},{5,21},{6,22},{7,23},{8,24},{9,... | collective-permute-start | bytes 983048 | tf_op jit(solution)/shard_map/ppermute | solution.py:20
  27.4 1.5 %collective-permute-start.13 = (f32[1408,128]{1,0:T(8,128)S(1)}, f32[1408,128]{1,0:T(8,128)S(1)}, u32[]{:S(2)}, u32[]{:S(2)}) collective-permute-start(f32[1408,128]{1,0:T(8,128)S(1)} %bitcast.47), channel_id=1, source_target_pairs={{0,4},{1,5},{2,6},{3,7},{4,0},{5,1},{6,2},{7,3},{8,12},{9,13},{10,... | collective-permute-start | bytes 2162696 | tf_op jit(solution)/shard_map/ppermute | solution.py:20
  28.9 10.3 %collective-permute-done.8.refs_5_ = f32[640,128]{1,0:T(8,128)S(1)} collective-permute-done((f32[640,128]{1,0:T(8,128)S(1)}, f32[640,128]{1,0:T(8,128)S(1)}, u32[]{:S(2)}, u32[]{:S(2)}) %collective-permute-start.8) | collective-permute-done | bytes 327712 | tf_op jit(solution)/shard_map/ppermute | solution.py:20
  39.1 1.6 %gather_end.1 = (f32[160,2,128]{2,1,0:T(2,128)S(1)}, f32[160,2,128]{2,1,0:T(2,128)S(1)}, f32[160,2,128]{2,1,0:T(2,128)S(1)}, f32[160,2,128]{2,1,0:T(2,128)S(1)}) custom-call(s32[1]{0:T(128)} %bitcast.3.me_ref, s32[1536]{0:T(1024)S(1)} %bitcast.31, s32[1536]{0:T(1024)S(1)} %bitcast.45, s32[1536]{0:T(1024)S(1)} %bitcast.42, s32[1536]{0:T(1024)S(1)} %bitcast.39, ...), custom_call_target="tpu_custom_call" | custom-call | bytes 4849664 | tf_op jit(solution)/shard_map/gather_end/pallas_call | solution.py:136
  40.8 0.0 collective-permute-done.18
  40.8 1.4 %collective-permute-start.19 = (f32[320,128]{1,0:T(8,128)S(1)}, f32[320,128]{1,0:T(8,128)S(1)}, u32[]{:S(2)}, u32[]{:S(2)}) collective-permute-start(f32[320,128]{1,0:T(8,128)S(1)} %get-tuple-element.54), channel_id=1, source_target_pairs={{0,8},{1,9},{2,10},{3,11},{4,12},{5,13},{6,14},{7,15},{8,0},{9,1},... | collective-permute-start | bytes 491528 | tf_op jit(solution)/shard_map/ppermute | solution.py:20
  42.3 3.0 %gather_near.1 = (f32[352,2,128]{2,1,0:T(2,128)S(1)}, f32[352,2,128]{2,1,0:T(2,128)S(1)}, f32[352,2,128]{2,1,0:T(2,128)S(1)}, f32[352,2,128]{2,1,0:T(2,128)S(1)}) custom-call(s32[1]{0:T(128)} %bitcast.3.me_ref, s32[1536]{0:T(1024)S(1)} %bitcast.32, s32[1536]{0:T(1024)S(1)} %bitcast.46, s32[1536]{0:T(1024)S(1)} %bitcast.43, s32[1536]{0:T(1024)S(1)} %bitcast.40, ...), custom_call_target="tpu_custom_call" | custom-call | bytes 5636096 | tf_op jit(solution)/shard_map/gather_near/pallas_call | solution.py:136
  45.2 0.0 collective-permute-done.9
  45.2 0.1 slice_add_fusion.3
  45.3 1.3 %collective-permute-start.10 = (f32[704,128]{1,0:T(8,128)S(1)}, f32[704,128]{1,0:T(8,128)S(1)}, u32[]{:S(2)}, u32[]{:S(2)}) collective-permute-start(f32[704,128]{1,0:T(8,128)S(1)} %get-tuple-element.45), channel_id=1, source_target_pairs={{0,4},{1,5},{2,6},{3,7},{4,0},{5,1},{6,2},{7,3},{8,12},{9,13},{10,... | collective-permute-start | bytes 1081352 | tf_op jit(solution)/shard_map/ppermute | solution.py:20
  46.7 0.1 slice_add_fusion.1
  46.8 0.6 collective-permute-start.14
  47.4 1.8 %collective-permute-start.17 = (f32[320,128]{1,0:T(8,128)S(1)}, f32[320,128]{1,0:T(8,128)S(1)}, u32[]{:S(2)}, u32[]{:S(2)}) collective-permute-start(f32[320,128]{1,0:T(8,128)S(1)} %get-tuple-element.56), channel_id=1, source_target_pairs={{0,16},{1,17},{2,18},{3,19},{4,20},{5,21},{6,22},{7,23},{8,24},{9,... | collective-permute-start | bytes 491528 | tf_op jit(solution)/shard_map/ppermute | solution.py:20
  49.2 3.8 %collective-permute-done.10 = f32[704,128]{1,0:T(8,128)S(1)} collective-permute-done((f32[704,128]{1,0:T(8,128)S(1)}, f32[704,128]{1,0:T(8,128)S(1)}, u32[]{:S(2)}, u32[]{:S(2)}) %collective-permute-start.10) | collective-permute-done | bytes 360480 | tf_op jit(solution)/shard_map/ppermute | solution.py:20
  53.0 0.1 slice_add_fusion.7
  53.1 1.8 %collective-permute-start.11 = (f32[352,128]{1,0:T(8,128)S(1)}, f32[352,128]{1,0:T(8,128)S(1)}, u32[]{:S(2)}, u32[]{:S(2)}) collective-permute-start(f32[352,128]{1,0:T(8,128)S(1)} %get-tuple-element.43), channel_id=1, source_target_pairs={{0,8},{1,9},{2,10},{3,11},{4,12},{5,13},{6,14},{7,15},{8,0},{9,1},... | collective-permute-start | bytes 540680 | tf_op jit(solution)/shard_map/ppermute | solution.py:20
  54.9 0.0 collective-permute-done.14
  54.9 1.3 %collective-permute-start.15 = (f32[352,128]{1,0:T(8,128)S(1)}, f32[352,128]{1,0:T(8,128)S(1)}, u32[]{:S(2)}, u32[]{:S(2)}) collective-permute-start(f32[352,128]{1,0:T(8,128)S(1)} %get-tuple-element.39), channel_id=1, source_target_pairs={{0,8},{1,9},{2,10},{3,11},{4,12},{5,13},{6,14},{7,15},{8,0},{9,1},... | collective-permute-start | bytes 540680 | tf_op jit(solution)/shard_map/ppermute | solution.py:20
  56.3 4.4 %collective-permute-done.11 = f32[352,128]{1,0:T(8,128)S(1)} collective-permute-done((f32[352,128]{1,0:T(8,128)S(1)}, f32[352,128]{1,0:T(8,128)S(1)}, u32[]{:S(2)}, u32[]{:S(2)}) %collective-permute-start.11) | collective-permute-done | bytes 180256 | tf_op jit(solution)/shard_map/ppermute | solution.py:20
  60.7 0.1 collective-permute-start.12
  60.8 0.0 collective-permute-done.17.first_add_ref
  60.9 1.3 %collective-permute-start.20 = (f32[320,128]{1,0:T(8,128)S(1)}, f32[320,128]{1,0:T(8,128)S(1)}, u32[]{:S(2)}, u32[]{:S(2)}) collective-permute-start(f32[320,128]{1,0:T(8,128)S(1)} %get-tuple-element.33), channel_id=1, source_target_pairs={{0,2},{1,3},{2,0},{3,1},{4,6},{5,7},{6,4},{7,5},{8,10},{9,11},{10,... | collective-permute-start | bytes 491528 | tf_op jit(solution)/shard_map/ppermute | solution.py:20
  62.2 0.6 collective-permute-done.15
  62.8 2.3 %collective-permute-start.16 = (f32[176,128]{1,0:T(8,128)S(1)}, f32[176,128]{1,0:T(8,128)S(1)}, u32[]{:S(2)}, u32[]{:S(2)}) collective-permute-start(f32[176,128]{1,0:T(8,128)S(1)} %get-tuple-element.46), channel_id=1, source_target_pairs={{0,16},{1,17},{2,18},{3,19},{4,20},{5,21},{6,22},{7,23},{8,24},{9,... | collective-permute-start | bytes 270344 | tf_op jit(solution)/shard_map/ppermute | solution.py:20
  65.2 1.1 %collective-permute-done.20 = f32[320,128]{1,0:T(8,128)S(1)} collective-permute-done((f32[320,128]{1,0:T(8,128)S(1)}, f32[320,128]{1,0:T(8,128)S(1)}, u32[]{:S(2)}, u32[]{:S(2)}) %collective-permute-start.20) | collective-permute-done | bytes 163872 | tf_op jit(solution)/shard_map/ppermute | solution.py:20
  66.3 1.2 %collective-permute-start.21 = (f32[160,128]{1,0:T(8,128)S(1)}, f32[160,128]{1,0:T(8,128)S(1)}, u32[]{:S(2)}, u32[]{:S(2)}) collective-permute-start(f32[160,128]{1,0:T(8,128)S(1)} %pad_maximum_fusion.1), channel_id=1, source_target_pairs={{0,4},{1,5},{2,6},{3,7},{4,0},{5,1},{6,2},{7,3},{8,12},{9,13},{10,... | collective-permute-start | bytes 245768 | tf_op jit(solution)/shard_map/ppermute | solution.py:20
  67.5 0.0 collective-permute-done.12.refs_1_
  67.5 0.8 collective-permute-done.16.refs_3_
  68.3 2.5 %collective-permute-done.21.refs_5_ = f32[160,128]{1,0:T(8,128)S(1)} collective-permute-done((f32[160,128]{1,0:T(8,128)S(1)}, f32[160,128]{1,0:T(8,128)S(1)}, u32[]{:S(2)}, u32[]{:S(2)}) %collective-permute-start.21) | collective-permute-done | bytes 81952 | tf_op jit(solution)/shard_map/ppermute | solution.py:20
  70.8 1.4 %gram.1 = (f32[256,256]{1,0:T(8,128)}, f32[256,128]{1,0:T(8,128)S(1)}, f32[128,128]{1,0:T(8,128)S(1)}, f32[128,128]{1,0:T(8,128)S(1)}) custom-call(s32[1]{0:T(128)} %bitcast.ry_ref, s32[1536]{0:T(1024)S(1)} %bitcast.33, f32[176,128]{1,0:T(8,128)S(1)} %get-tuple-element.49.refs_0_, f32[176,128]{1,0:T(8,128)S(1)} %collective-permute-done.12.refs_1_, ...), custom_call_target="tpu_custom_call" | custom-call | flops 100663296 | bytes 1048576 | tf_op jit(solution)/shard_map/gram/pallas_call | solution.py:136
  72.2 0.0 collective-permute-start.22
  72.2 1.3 %collective-permute-done.22 = f32[256,128]{1,0:T(8,128)S(1)} collective-permute-done((f32[256,128]{1,0:T(8,128)S(1)}, f32[256,128]{1,0:T(8,128)S(1)}, u32[]{:S(2)}, u32[]{:S(2)}) %collective-permute-start.22) | collective-permute-done | bytes 131104 | tf_op jit(solution)/shard_map/ppermute | solution.py:20
  73.6 1.2 %collective-permute-start.24 = (f32[128,128]{1,0:T(8,128)S(1)}, f32[128,128]{1,0:T(8,128)S(1)}, u32[]{:S(2)}, u32[]{:S(2)}) collective-permute-start(f32[128,128]{1,0:T(8,128)S(1)} %get-tuple-element.58), channel_id=1, source_target_pairs={{0,4},{1,5},{2,6},{3,7},{4,0},{5,1},{6,2},{7,3},{8,12},{9,13},{10,... | collective-permute-start | bytes 196616 | tf_op jit(solution)/shard_map/ppermute | solution.py:20
  74.8 1.6 %collective-permute-start.25 = (f32[128,128]{1,0:T(8,128)S(1)}, f32[128,128]{1,0:T(8,128)S(1)}, u32[]{:S(2)}, u32[]{:S(2)}) collective-permute-start(f32[128,128]{1,0:T(8,128)S(1)} %get-tuple-element.59), channel_id=1, source_target_pairs={{0,6},{1,7},{2,4},{3,5},{4,2},{5,3},{6,0},{7,1},{8,14},{9,15},{10,... | collective-permute-start | bytes 196616 | tf_op jit(solution)/shard_map/ppermute | solution.py:20
  76.4 0.8 collective-permute-start.23
  77.1 0.8 collective-permute-done.24
  77.9 2.3 %collective-permute-done.25 = f32[128,128]{1,0:T(8,128)S(1)} collective-permute-done((f32[128,128]{1,0:T(8,128)S(1)}, f32[128,128]{1,0:T(8,128)S(1)}, u32[]{:S(2)}, u32[]{:S(2)}) %collective-permute-start.25) | collective-permute-done | bytes 65568 | tf_op jit(solution)/shard_map/ppermute | solution.py:20
  80.3 0.4 collective-permute-done.23
  80.7 3.3 %collective-permute-start.28 = (f32[128,128]{1,0:T(8,128)S(1)}, f32[128,128]{1,0:T(8,128)S(1)}, u32[]{:S(2)}, u32[]{:S(2)}) collective-permute-start(f32[128,128]{1,0:T(8,128)S(1)} %add_add_fusion), channel_id=1, source_target_pairs={{0,24},{1,25},{2,26},{3,27},{4,28},{5,29},{6,30},{7,31},{8,16},{9,... | collective-permute-start | bytes 196616 | tf_op jit(solution)/shard_map/ppermute | solution.py:20
  84.0 1.1 %collective-permute-start.26 = (f32[128,128]{1,0:T(8,128)S(1)}, f32[128,128]{1,0:T(8,128)S(1)}, u32[]{:S(2)}, u32[]{:S(2)}) collective-permute-start(f32[128,128]{1,0:T(8,128)S(1)} %add_add_fusion), channel_id=1, source_target_pairs={{0,8},{1,9},{2,10},{3,11},{4,12},{5,13},{6,14},{7,15},{8,0},{9,1},... | collective-permute-start | bytes 196616 | tf_op jit(solution)/shard_map/ppermute | solution.py:20
  85.1 2.5 %collective-permute-done.28 = f32[128,128]{1,0:T(8,128)S(1)} collective-permute-done((f32[128,128]{1,0:T(8,128)S(1)}, f32[128,128]{1,0:T(8,128)S(1)}, u32[]{:S(2)}, u32[]{:S(2)}) %collective-permute-start.28) | collective-permute-done | bytes 65568 | tf_op jit(solution)/shard_map/ppermute | solution.py:20
  87.6 2.1 %collective-permute-done.27 = f32[128,128]{1,0:T(8,128)S(1)} collective-permute-done((f32[128,128]{1,0:T(8,128)S(1)}, f32[128,128]{1,0:T(8,128)S(1)}, u32[]{:S(2)}, u32[]{:S(2)}) %collective-permute-start.27) | collective-permute-done | bytes 65568 | tf_op jit(solution)/shard_map/ppermute | solution.py:20
  89.6 0.0 collective-permute-done.26
  89.6 0.6 multiply_bitcast_fusion
  (17 shorter events, 0.3 us)
Async XLA Ops:
  0.6 15.0 %collective-permute-start.7 = (f32[4096,256]{1,0:T(8,128)}, f32[4096,256]{1,0:T(8,128)}, u32[]{:S(2)}, u32[]{:S(2)}) collective-permute-start(f32[4096,256]{1,0:T(8,128)} %refs_0_.1), channel_id=1, source_target_pairs={{0,1},{1,0},{2,3},{3,2},{4,5},{5,4},{6,7},{7,6},{8,9},{9,8},{10,11... | collective-permute-start | bytes 12582920 | tf_op jit(solution)/shard_map/ppermute | solution.py:20
  2.5 13.1 %collective-permute-start.6 = (s32[35,128]{1,0:T(8,128)S(1)}, s32[35,128]{1,0:T(8,128)S(1)}, u32[]{:S(2)}, u32[]{:S(2)}) collective-permute-start(s32[35,128]{1,0:T(8,128)S(1)} %fusion.1.signs_ref), channel_id=1, source_target_pairs={{0,1},{1,0},{2,3},{3,2},{4,5},{5,4},{6,7},{7,6},{8,9},{9,8},{10,11... | collective-permute-start | bytes 53768 | tf_op jit(solution)/shard_map/ppermute | solution.py:20
  2.6 6.6 %collective-permute-start.2 = (s32[3,128]{1,0:T(4,128)S(1)}, s32[3,128]{1,0:T(4,128)S(1)}, u32[]{:S(2)}, u32[]{:S(2)}) collective-permute-start(s32[3,128]{1,0:T(4,128)S(1)} %slice.140.refs_0_), channel_id=1, source_target_pairs={{0,24},{1,25},{2,26},{3,27},{4,28},{5,29},{6,30},{7,31},{8,16},{9,... | collective-permute-start | bytes 4616 | tf_op jit(solution)/shard_map/ppermute | solution.py:20
  7.6 4.5 %collective-permute-start.1 = (s32[3,128]{1,0:T(4,128)S(1)}, s32[3,128]{1,0:T(4,128)S(1)}, u32[]{:S(2)}, u32[]{:S(2)}) collective-permute-start(s32[3,128]{1,0:T(4,128)S(1)} %slice.140.refs_0_), channel_id=1, source_target_pairs={{0,16},{1,17},{2,18},{3,19},{4,20},{5,21},{6,22},{7,23},{8,24},{9,... | collective-permute-start | bytes 4616 | tf_op jit(solution)/shard_map/ppermute | solution.py:20
  7.6 4.5 %collective-permute-start = (s32[3,128]{1,0:T(4,128)S(1)}, s32[3,128]{1,0:T(4,128)S(1)}, u32[]{:S(2)}, u32[]{:S(2)}) collective-permute-start(s32[3,128]{1,0:T(4,128)S(1)} %slice.140.refs_0_), channel_id=1, source_target_pairs={{0,8},{1,9},{2,10},{3,11},{4,12},{5,13},{6,14},{7,15},{8,0},{9,1},... | collective-permute-start | bytes 4616 | tf_op jit(solution)/shard_map/ppermute | solution.py:20
  12.1 7.9 %collective-permute-start.5 = (s32[12,128]{1,0:T(8,128)S(1)}, s32[12,128]{1,0:T(8,128)S(1)}, u32[]{:S(2)}, u32[]{:S(2)}) collective-permute-start(s32[12,128]{1,0:T(8,128)S(1)} %join.1), channel_id=1, source_target_pairs={{0,6},{1,7},{2,4},{3,5},{4,2},{5,3},{6,0},{7,1},{8,14},{9,15},{10,... | collective-permute-start | bytes 18440 | tf_op jit(solution)/shard_map/ppermute | solution.py:20
  14.6 5.5 %collective-permute-start.4 = (s32[12,128]{1,0:T(8,128)S(1)}, s32[12,128]{1,0:T(8,128)S(1)}, u32[]{:S(2)}, u32[]{:S(2)}) collective-permute-start(s32[12,128]{1,0:T(8,128)S(1)} %join.1), channel_id=1, source_target_pairs={{0,4},{1,5},{2,6},{3,7},{4,0},{5,1},{6,2},{7,3},{8,12},{9,13},{10,... | collective-permute-start | bytes 18440 | tf_op jit(solution)/shard_map/ppermute | solution.py:20
  15.1 5.0 %collective-permute-start.3 = (s32[12,128]{1,0:T(8,128)S(1)}, s32[12,128]{1,0:T(8,128)S(1)}, u32[]{:S(2)}, u32[]{:S(2)}) collective-permute-start(s32[12,128]{1,0:T(8,128)S(1)} %join.1), channel_id=1, source_target_pairs={{0,2},{1,3},{2,0},{3,1},{4,6},{5,7},{6,4},{7,5},{8,10},{9,11},{10,... | collective-permute-start | bytes 18440 | tf_op jit(solution)/shard_map/ppermute | solution.py:20
  23.7 21.6 %collective-permute-start.9 = (f32[1408,128]{1,0:T(8,128)S(1)}, f32[1408,128]{1,0:T(8,128)S(1)}, u32[]{:S(2)}, u32[]{:S(2)}) collective-permute-start(f32[1408,128]{1,0:T(8,128)S(1)} %bitcast.48), channel_id=1, source_target_pairs={{0,2},{1,3},{2,0},{3,1},{4,6},{5,7},{6,4},{7,5},{8,10},{9,11},{10,... | collective-permute-start | bytes 2162696 | tf_op jit(solution)/shard_map/ppermute | solution.py:20
  25.2 13.9 %collective-permute-start.8 = (f32[640,128]{1,0:T(8,128)S(1)}, f32[640,128]{1,0:T(8,128)S(1)}, u32[]{:S(2)}, u32[]{:S(2)}) collective-permute-start(f32[640,128]{1,0:T(8,128)S(1)} %bitcast.50), channel_id=1, source_target_pairs={{0,8},{1,9},{2,10},{3,11},{4,12},{5,13},{6,14},{7,15},{8,0},{9,1},... | collective-permute-start | bytes 983048 | tf_op jit(solution)/shard_map/ppermute | solution.py:20
  25.3 15.5 %collective-permute-start.18 = (f32[640,128]{1,0:T(8,128)S(1)}, f32[640,128]{1,0:T(8,128)S(1)}, u32[]{:S(2)}, u32[]{:S(2)}) collective-permute-start(f32[640,128]{1,0:T(8,128)S(1)} %bitcast.49), channel_id=1, source_target_pairs={{0,16},{1,17},{2,18},{3,19},{4,20},{5,21},{6,22},{7,23},{8,24},{9,... | collective-permute-start | bytes 983048 | tf_op jit(solution)/shard_map/ppermute | solution.py:20
  27.4 19.3 %collective-permute-start.13 = (f32[1408,128]{1,0:T(8,128)S(1)}, f32[1408,128]{1,0:T(8,128)S(1)}, u32[]{:S(2)}, u32[]{:S(2)}) collective-permute-start(f32[1408,128]{1,0:T(8,128)S(1)} %bitcast.47), channel_id=1, source_target_pairs={{0,4},{1,5},{2,6},{3,7},{4,0},{5,1},{6,2},{7,3},{8,12},{9,13},{10,... | collective-permute-start | bytes 2162696 | tf_op jit(solution)/shard_map/ppermute | solution.py:20
  40.8 20.0 %collective-permute-start.19 = (f32[320,128]{1,0:T(8,128)S(1)}, f32[320,128]{1,0:T(8,128)S(1)}, u32[]{:S(2)}, u32[]{:S(2)}) collective-permute-start(f32[320,128]{1,0:T(8,128)S(1)} %get-tuple-element.54), channel_id=1, source_target_pairs={{0,8},{1,9},{2,10},{3,11},{4,12},{5,13},{6,14},{7,15},{8,0},{9,1},... | collective-permute-start | bytes 491528 | tf_op jit(solution)/shard_map/ppermute | solution.py:20
  45.3 7.7 %collective-permute-start.10 = (f32[704,128]{1,0:T(8,128)S(1)}, f32[704,128]{1,0:T(8,128)S(1)}, u32[]{:S(2)}, u32[]{:S(2)}) collective-permute-start(f32[704,128]{1,0:T(8,128)S(1)} %get-tuple-element.45), channel_id=1, source_target_pairs={{0,4},{1,5},{2,6},{3,7},{4,0},{5,1},{6,2},{7,3},{8,12},{9,13},{10,... | collective-permute-start | bytes 1081352 | tf_op jit(solution)/shard_map/ppermute | solution.py:20
  46.8 8.1 %collective-permute-start.14 = (f32[704,128]{1,0:T(8,128)S(1)}, f32[704,128]{1,0:T(8,128)S(1)}, u32[]{:S(2)}, u32[]{:S(2)}) collective-permute-start(f32[704,128]{1,0:T(8,128)S(1)} %get-tuple-element.41), channel_id=1, source_target_pairs={{0,2},{1,3},{2,0},{3,1},{4,6},{5,7},{6,4},{7,5},{8,10},{9,11},{10,... | collective-permute-start | bytes 1081352 | tf_op jit(solution)/shard_map/ppermute | solution.py:20
  47.4 13.4 %collective-permute-start.17 = (f32[320,128]{1,0:T(8,128)S(1)}, f32[320,128]{1,0:T(8,128)S(1)}, u32[]{:S(2)}, u32[]{:S(2)}) collective-permute-start(f32[320,128]{1,0:T(8,128)S(1)} %get-tuple-element.56), channel_id=1, source_target_pairs={{0,16},{1,17},{2,18},{3,19},{4,20},{5,21},{6,22},{7,23},{8,24},{9,... | collective-permute-start | bytes 491528 | tf_op jit(solution)/shard_map/ppermute | solution.py:20
  53.1 7.6 %collective-permute-start.11 = (f32[352,128]{1,0:T(8,128)S(1)}, f32[352,128]{1,0:T(8,128)S(1)}, u32[]{:S(2)}, u32[]{:S(2)}) collective-permute-start(f32[352,128]{1,0:T(8,128)S(1)} %get-tuple-element.43), channel_id=1, source_target_pairs={{0,8},{1,9},{2,10},{3,11},{4,12},{5,13},{6,14},{7,15},{8,0},{9,1},... | collective-permute-start | bytes 540680 | tf_op jit(solution)/shard_map/ppermute | solution.py:20
  54.9 7.9 %collective-permute-start.15 = (f32[352,128]{1,0:T(8,128)S(1)}, f32[352,128]{1,0:T(8,128)S(1)}, u32[]{:S(2)}, u32[]{:S(2)}) collective-permute-start(f32[352,128]{1,0:T(8,128)S(1)} %get-tuple-element.39), channel_id=1, source_target_pairs={{0,8},{1,9},{2,10},{3,11},{4,12},{5,13},{6,14},{7,15},{8,0},{9,1},... | collective-permute-start | bytes 540680 | tf_op jit(solution)/shard_map/ppermute | solution.py:20
  60.7 6.8 %collective-permute-start.12 = (f32[176,128]{1,0:T(8,128)S(1)}, f32[176,128]{1,0:T(8,128)S(1)}, u32[]{:S(2)}, u32[]{:S(2)}) collective-permute-start(f32[176,128]{1,0:T(8,128)S(1)} %get-tuple-element.48.refs_0_), channel_id=1, source_target_pairs={{0,16},{1,17},{2,18},{3,19},{4,20},{5,21},{6,22},{7,23},{8,24},{9,... | collective-permute-start | bytes 270344 | tf_op jit(solution)/shard_map/ppermute | solution.py:20
  60.9 5.4 %collective-permute-start.20 = (f32[320,128]{1,0:T(8,128)S(1)}, f32[320,128]{1,0:T(8,128)S(1)}, u32[]{:S(2)}, u32[]{:S(2)}) collective-permute-start(f32[320,128]{1,0:T(8,128)S(1)} %get-tuple-element.33), channel_id=1, source_target_pairs={{0,2},{1,3},{2,0},{3,1},{4,6},{5,7},{6,4},{7,5},{8,10},{9,11},{10,... | collective-permute-start | bytes 491528 | tf_op jit(solution)/shard_map/ppermute | solution.py:20
  62.8 5.5 %collective-permute-start.16 = (f32[176,128]{1,0:T(8,128)S(1)}, f32[176,128]{1,0:T(8,128)S(1)}, u32[]{:S(2)}, u32[]{:S(2)}) collective-permute-start(f32[176,128]{1,0:T(8,128)S(1)} %get-tuple-element.46), channel_id=1, source_target_pairs={{0,16},{1,17},{2,18},{3,19},{4,20},{5,21},{6,22},{7,23},{8,24},{9,... | collective-permute-start | bytes 270344 | tf_op jit(solution)/shard_map/ppermute | solution.py:20
  66.3 4.5 %collective-permute-start.21 = (f32[160,128]{1,0:T(8,128)S(1)}, f32[160,128]{1,0:T(8,128)S(1)}, u32[]{:S(2)}, u32[]{:S(2)}) collective-permute-start(f32[160,128]{1,0:T(8,128)S(1)} %pad_maximum_fusion.1), channel_id=1, source_target_pairs={{0,4},{1,5},{2,6},{3,7},{4,0},{5,1},{6,2},{7,3},{8,12},{9,13},{10,... | collective-permute-start | bytes 245768 | tf_op jit(solution)/shard_map/ppermute | solution.py:20
  72.2 1.3 %collective-permute-start.22 = (f32[256,128]{1,0:T(8,128)S(1)}, f32[256,128]{1,0:T(8,128)S(1)}, u32[]{:S(2)}, u32[]{:S(2)}) collective-permute-start(f32[256,128]{1,0:T(8,128)S(1)} %get-tuple-element.36), channel_id=1, source_target_pairs={{0,1},{1,0},{2,3},{3,2},{4,5},{5,4},{6,7},{7,6},{8,9},{9,8},{10,11... | collective-permute-start | bytes 393224 | tf_op jit(solution)/shard_map/ppermute | solution.py:20
  73.6 4.3 %collective-permute-start.24 = (f32[128,128]{1,0:T(8,128)S(1)}, f32[128,128]{1,0:T(8,128)S(1)}, u32[]{:S(2)}, u32[]{:S(2)}) collective-permute-start(f32[128,128]{1,0:T(8,128)S(1)} %get-tuple-element.58), channel_id=1, source_target_pairs={{0,4},{1,5},{2,6},{3,7},{4,0},{5,1},{6,2},{7,3},{8,12},{9,13},{10,... | collective-permute-start | bytes 196616 | tf_op jit(solution)/shard_map/ppermute | solution.py:20
  74.8 5.5 %collective-permute-start.25 = (f32[128,128]{1,0:T(8,128)S(1)}, f32[128,128]{1,0:T(8,128)S(1)}, u32[]{:S(2)}, u32[]{:S(2)}) collective-permute-start(f32[128,128]{1,0:T(8,128)S(1)} %get-tuple-element.59), channel_id=1, source_target_pairs={{0,6},{1,7},{2,4},{3,5},{4,2},{5,3},{6,0},{7,1},{8,14},{9,15},{10,... | collective-permute-start | bytes 196616 | tf_op jit(solution)/shard_map/ppermute | solution.py:20
  76.4 4.3 %collective-permute-start.23 = (f32[128,128]{1,0:T(8,128)S(1)}, f32[128,128]{1,0:T(8,128)S(1)}, u32[]{:S(2)}, u32[]{:S(2)}) collective-permute-start(f32[128,128]{1,0:T(8,128)S(1)} %get-tuple-element.59), channel_id=1, source_target_pairs={{0,2},{1,3},{2,0},{3,1},{4,6},{5,7},{6,4},{7,5},{8,10},{9,11},{10,... | collective-permute-start | bytes 196616 | tf_op jit(solution)/shard_map/ppermute | solution.py:20
  80.7 6.9 %collective-permute-start.28 = (f32[128,128]{1,0:T(8,128)S(1)}, f32[128,128]{1,0:T(8,128)S(1)}, u32[]{:S(2)}, u32[]{:S(2)}) collective-permute-start(f32[128,128]{1,0:T(8,128)S(1)} %add_add_fusion), channel_id=1, source_target_pairs={{0,24},{1,25},{2,26},{3,27},{4,28},{5,29},{6,30},{7,31},{8,16},{9,... | collective-permute-start | bytes 196616 | tf_op jit(solution)/shard_map/ppermute | solution.py:20
  84.0 5.6 %collective-permute-start.27 = (f32[128,128]{1,0:T(8,128)S(1)}, f32[128,128]{1,0:T(8,128)S(1)}, u32[]{:S(2)}, u32[]{:S(2)}) collective-permute-start(f32[128,128]{1,0:T(8,128)S(1)} %add_add_fusion), channel_id=1, source_target_pairs={{0,16},{1,17},{2,18},{3,19},{4,20},{5,21},{6,22},{7,23},{8,24},{9,... | collective-permute-start | bytes 196616 | tf_op jit(solution)/shard_map/ppermute | solution.py:20
  84.0 5.6 %collective-permute-start.26 = (f32[128,128]{1,0:T(8,128)S(1)}, f32[128,128]{1,0:T(8,128)S(1)}, u32[]{:S(2)}, u32[]{:S(2)}) collective-permute-start(f32[128,128]{1,0:T(8,128)S(1)} %add_add_fusion), channel_id=1, source_target_pairs={{0,8},{1,9},{2,10},{3,11},{4,12},{5,13},{6,14},{7,15},{8,0},{9,1},... | collective-permute-start | bytes 196616 | tf_op jit(solution)/shard_map/ppermute | solution.py:20

commit v4 on v3

--- a/solution.py
+++ b/solution.py
@@ -243,12 +243,12 @@
     end_stays = gathered(
         "gather_end",
         [(*end, [z + near for near in xy]) for end, (_, stays) in zip(ends, routes) for z in stays],
-        after=(end_adds[0],),
+        after=(end_on,),
     )
     nears = gathered(
         "gather_near",
         [(*a, distances(0, 0)), (*a, distances(0, 1)), (*b, distances(0, 0)), (*b, distances(1, 0))],
-        after=(end_adds[0],),
+        after=(end_on,),
     )
 
     def halved(value):

time: 90.6 us -> 88.7 us (0.979)
  starting transfers between devices: 36.1 us -> 34.6 us
  waiting for transfers between devices: 36.9 us -> 38.4 us
  Pallas kernels: 14.1 us -> 12.8 us
    ppermute x29, waiting for transfers between devices: 36.9 us -> 38.4 us  [swap(): return lax.ppermute(value, MESH_AXES, [(i, i ^ bits) for i in range(size)])]
    ppermute x29, starting transfers between devices: 36.1 us -> 34.6 us  [swap(): return lax.ppermute(value, MESH_AXES, [(i, i ^ bits) for i in range(size)])]
    pallas_call x6, Pallas kernels: 9.65 us -> 8.43 us  [call(): pl.pallas_call(kernel, in_specs=specs(len(scalars), len(arrays)) + [pl.Bl...]
  transfers between devices with their start and end apart: 29 -> 29, of which waited for: 15 -> 16; matrix products, arithmetic and copies ran while one was open for 1% -> 1% of each run, Pallas kernels for 10% -> 9%
where the time goes in v4:
time: 88.7 us; the launch traced here: 89.1 us
  waiting for transfers between devices  38.4 us (43%)
  starting transfers between devices  34.6 us (39%)
  Pallas kernels  12.8 us (14%)
  other arithmetic  1.79 us (2%)
  between operations  1.41 us (2%)
    ppermute x29, waiting for transfers between devices, swap(): return lax.ppermute(value, MESH_AXES, [(i, i ^ bits) for i in range(size)])  38.4 us
    ppermute x29, starting transfers between devices, swap(): return lax.ppermute(value, MESH_AXES, [(i, i ^ bits) for i in range(size)])  34.6 us
    pallas_call x6, Pallas kernels, call(): pl.pallas_call(kernel, in_specs=specs(len(scalars), len(arrays)) + [pl.Bl...  8.43 us
    pallas_call x1, Pallas kernels, transform(): pl.pallas_call(functools.partial(transform_kernel, full, chunks), in_spec...  4.4 us
  transfers between devices with their start and end apart: 29, of which 16 were waited for; matrix products, arithmetic and copies ran while one was open for 1% of the time, Pallas kernels for 9%

profile of v4, /device:TPU:0, one launch (start us, length us, event | category | flops | bytes accessed | tf_op | source)
XLA Modules:
  0.0 89.1 jit_solution(3403432501743312489)
XLA Ops:
  0.6 0.5 collective-permute-start.7
  1.8 0.7 fusion.1.signs_ref
  2.5 0.1 collective-permute-start.6
  2.6 3.0 %collective-permute-start = (s32[3,128]{1,0:T(4,128)S(1)}, s32[3,128]{1,0:T(4,128)S(1)}, u32[]{:S(2)}, u32[]{:S(2)}) collective-permute-start(s32[3,128]{1,0:T(4,128)S(1)} %slice.140.refs_0_), channel_id=1, source_target_pairs={{0,8},{1,9},{2,10},{3,11},{4,12},{5,13},{6,14},{7,15},{8,0},{9,1},... | collective-permute-start | bytes 4616 | tf_op jit(solution)/shard_map/ppermute | solution.py:20
  5.6 2.6 %collective-permute-start.1 = (s32[3,128]{1,0:T(4,128)S(1)}, s32[3,128]{1,0:T(4,128)S(1)}, u32[]{:S(2)}, u32[]{:S(2)}) collective-permute-start(s32[3,128]{1,0:T(4,128)S(1)} %slice.140.refs_0_), channel_id=1, source_target_pairs={{0,16},{1,17},{2,18},{3,19},{4,20},{5,21},{6,22},{7,23},{8,24},{9,... | collective-permute-start | bytes 4616 | tf_op jit(solution)/shard_map/ppermute | solution.py:20
  8.2 0.0 collective-permute-start.2
  8.2 0.0 collective-permute-done.refs_1_
  8.2 1.9 %collective-permute-done.1.refs_2_ = s32[3,128]{1,0:T(4,128)S(1)} collective-permute-done((s32[3,128]{1,0:T(4,128)S(1)}, s32[3,128]{1,0:T(4,128)S(1)}, u32[]{:S(2)}, u32[]{:S(2)}) %collective-permute-start.1) | collective-permute-done | bytes 1568 | tf_op jit(solution)/shard_map/ppermute | solution.py:20
  10.1 3.5 %collective-permute-done.2.refs_3_ = s32[3,128]{1,0:T(4,128)S(1)} collective-permute-done((s32[3,128]{1,0:T(4,128)S(1)}, s32[3,128]{1,0:T(4,128)S(1)}, u32[]{:S(2)}, u32[]{:S(2)}) %collective-permute-start.2) | collective-permute-done | bytes 1568 | tf_op jit(solution)/shard_map/ppermute | solution.py:20
  13.6 1.5 %collective-permute-start.3 = (s32[12,128]{1,0:T(8,128)S(1)}, s32[12,128]{1,0:T(8,128)S(1)}, u32[]{:S(2)}, u32[]{:S(2)}) collective-permute-start(s32[12,128]{1,0:T(8,128)S(1)} %join.1), channel_id=1, source_target_pairs={{0,2},{1,3},{2,0},{3,1},{4,6},{5,7},{6,4},{7,5},{8,10},{9,11},{10,... | collective-permute-start | bytes 18440 | tf_op jit(solution)/shard_map/ppermute | solution.py:20
  15.1 1.5 %collective-permute-start.4 = (s32[12,128]{1,0:T(8,128)S(1)}, s32[12,128]{1,0:T(8,128)S(1)}, u32[]{:S(2)}, u32[]{:S(2)}) collective-permute-start(s32[12,128]{1,0:T(8,128)S(1)} %join.1), channel_id=1, source_target_pairs={{0,4},{1,5},{2,6},{3,7},{4,0},{5,1},{6,2},{7,3},{8,12},{9,13},{10,... | collective-permute-start | bytes 18440 | tf_op jit(solution)/shard_map/ppermute | solution.py:20
  16.6 0.5 collective-permute-start.5
  17.1 0.0 collective-permute-done.6.other_signs_ref
  17.1 0.0 collective-permute-done.7.refs_1_
  17.1 4.4 %transform.1 = f32[8192,128]{1,0:T(8,128)S(1)} custom-call(s32[1]{0:T(128)} %bitcast.3.me_ref, s32[35,128]{1,0:T(8,128)S(1)} %fusion.1.signs_ref, s32[35,128]{1,0:T(8,128)S(1)} %collective-permute-done.6.other_signs_ref, f32[4096,256]{1,0:T(8,128)} %refs_0_.1, f32[4096,256]{1,0:T(8,128)} %collective-permute-done.7.refs_1_), custom_call_target="tpu_custom_call" | custom-call | flops 2147483648 | bytes 12582912 | tf_op jit(solution)/shard_map/transform/pallas_call | solution.py:91
  21.5 0.0 collective-permute-done.4
  21.5 0.0 collective-permute-done.5
  21.5 3.1 %gather_far.1 = (f32[704,2,128]{2,1,0:T(2,128)S(1)}, f32[704,2,128]{2,1,0:T(2,128)S(1)}, f32[320,2,128]{2,1,0:T(2,128)S(1)}, f32[320,2,128]{2,1,0:T(2,128)S(1)}) custom-call(s32[1]{0:T(128)} %bitcast.3.me_ref, s32[1536]{0:T(1024)S(1)} %bitcast.33, s32[1536]{0:T(1024)S(1)} %bitcast.41, s32[1536]{0:T(1024)S(1)} %bitcast.44, s32[1536]{0:T(1024)S(1)} %bitcast.47, ...), custom_call_target="tpu_custom_call" | custom-call | bytes 6291456 | tf_op jit(solution)/shard_map/gather_far/pallas_call | solution.py:136
  24.6 1.6 %collective-permute-start.8 = (f32[1408,128]{1,0:T(8,128)S(1)}, f32[1408,128]{1,0:T(8,128)S(1)}, u32[]{:S(2)}, u32[]{:S(2)}) collective-permute-start(f32[1408,128]{1,0:T(8,128)S(1)} %bitcast.51), channel_id=1, source_target_pairs={{0,2},{1,3},{2,0},{3,1},{4,6},{5,7},{6,4},{7,5},{8,10},{9,11},{10,... | collective-permute-start | bytes 2162696 | tf_op jit(solution)/shard_map/ppermute | solution.py:20
  26.2 0.0 collective-permute-start.18
  26.2 1.5 %collective-permute-start.12 = (f32[1408,128]{1,0:T(8,128)S(1)}, f32[1408,128]{1,0:T(8,128)S(1)}, u32[]{:S(2)}, u32[]{:S(2)}) collective-permute-start(f32[1408,128]{1,0:T(8,128)S(1)} %bitcast.50), channel_id=1, source_target_pairs={{0,4},{1,5},{2,6},{3,7},{4,0},{5,1},{6,2},{7,3},{8,12},{9,13},{10,... | collective-permute-start | bytes 2162696 | tf_op jit(solution)/shard_map/ppermute | solution.py:20
  27.7 1.3 %gather_end.1 = (f32[160,2,128]{2,1,0:T(2,128)S(1)}, f32[160,2,128]{2,1,0:T(2,128)S(1)}, f32[160,2,128]{2,1,0:T(2,128)S(1)}, f32[160,2,128]{2,1,0:T(2,128)S(1)}) custom-call(s32[1]{0:T(128)} %bitcast.3.me_ref, s32[1536]{0:T(1024)S(1)} %bitcast.34, s32[1536]{0:T(1024)S(1)} %bitcast.42, s32[1536]{0:T(1024)S(1)} %bitcast.45, s32[1536]{0:T(1024)S(1)} %bitcast.48, ...), custom_call_target="tpu_custom_call" | custom-call | bytes 4849664 | tf_op jit(solution)/shard_map/gather_end/pallas_call | solution.py:136
  28.9 0.8 collective-permute-start.16
  29.7 2.6 %gather_near.1 = (f32[352,2,128]{2,1,0:T(2,128)S(1)}, f32[352,2,128]{2,1,0:T(2,128)S(1)}, f32[352,2,128]{2,1,0:T(2,128)S(1)}, f32[352,2,128]{2,1,0:T(2,128)S(1)}) custom-call(s32[1]{0:T(128)} %bitcast.3.me_ref, s32[1536]{0:T(1024)S(1)} %bitcast.35, s32[1536]{0:T(1024)S(1)} %bitcast.43, s32[1536]{0:T(1024)S(1)} %bitcast.46, s32[1536]{0:T(1024)S(1)} %bitcast.49, ...), custom_call_target="tpu_custom_call" | custom-call | bytes 5636096 | tf_op jit(solution)/shard_map/gather_near/pallas_call | solution.py:136
  32.4 7.1 %collective-permute-done.18 = f32[640,128]{1,0:T(8,128)S(1)} collective-permute-done((f32[640,128]{1,0:T(8,128)S(1)}, f32[640,128]{1,0:T(8,128)S(1)}, u32[]{:S(2)}, u32[]{:S(2)}) %collective-permute-start.18) | collective-permute-done | bytes 327712 | tf_op jit(solution)/shard_map/ppermute | solution.py:20
  39.5 0.1 collective-permute-start.19
  39.6 0.9 %collective-permute-done.8 = f32[1408,128]{1,0:T(8,128)S(1)} collective-permute-done((f32[1408,128]{1,0:T(8,128)S(1)}, f32[1408,128]{1,0:T(8,128)S(1)}, u32[]{:S(2)}, u32[]{:S(2)}) %collective-permute-start.8) | collective-permute-done | bytes 720928 | tf_op jit(solution)/shard_map/ppermute | solution.py:20
  40.5 0.1 slice_add_fusion.3
  40.6 1.6 %collective-permute-start.9 = (f32[704,128]{1,0:T(8,128)S(1)}, f32[704,128]{1,0:T(8,128)S(1)}, u32[]{:S(2)}, u32[]{:S(2)}) collective-permute-start(f32[704,128]{1,0:T(8,128)S(1)} %get-tuple-element.45), channel_id=1, source_target_pairs={{0,4},{1,5},{2,6},{3,7},{4,0},{5,1},{6,2},{7,3},{8,12},{9,13},{10,... | collective-permute-start | bytes 1081352 | tf_op jit(solution)/shard_map/ppermute | solution.py:20
  42.2 0.0 collective-permute-done.12
  42.2 0.1 slice_add_fusion.1
  42.3 1.6 %collective-permute-start.13 = (f32[704,128]{1,0:T(8,128)S(1)}, f32[704,128]{1,0:T(8,128)S(1)}, u32[]{:S(2)}, u32[]{:S(2)}) collective-permute-start(f32[704,128]{1,0:T(8,128)S(1)} %get-tuple-element.41), channel_id=1, source_target_pairs={{0,2},{1,3},{2,0},{3,1},{4,6},{5,7},{6,4},{7,5},{8,10},{9,11},{10,... | collective-permute-start | bytes 1081352 | tf_op jit(solution)/shard_map/ppermute | solution.py:20
  43.8 0.0 collective-permute-done.16
  43.9 1.7 %collective-permute-start.17 = (f32[320,128]{1,0:T(8,128)S(1)}, f32[320,128]{1,0:T(8,128)S(1)}, u32[]{:S(2)}, u32[]{:S(2)}) collective-permute-start(f32[320,128]{1,0:T(8,128)S(1)} %get-tuple-element.56), channel_id=1, source_target_pairs={{0,16},{1,17},{2,18},{3,19},{4,20},{5,21},{6,22},{7,23},{8,24},{9,... | collective-permute-start | bytes 491528 | tf_op jit(solution)/shard_map/ppermute | solution.py:20
  45.6 4.4 %collective-permute-done.9 = f32[704,128]{1,0:T(8,128)S(1)} collective-permute-done((f32[704,128]{1,0:T(8,128)S(1)}, f32[704,128]{1,0:T(8,128)S(1)}, u32[]{:S(2)}, u32[]{:S(2)}) %collective-permute-start.9) | collective-permute-done | bytes 360480 | tf_op jit(solution)/shard_map/ppermute | solution.py:20
  50.1 1.8 %collective-permute-start.10 = (f32[352,128]{1,0:T(8,128)S(1)}, f32[352,128]{1,0:T(8,128)S(1)}, u32[]{:S(2)}, u32[]{:S(2)}) collective-permute-start(f32[352,128]{1,0:T(8,128)S(1)} %get-tuple-element.43), channel_id=1, source_target_pairs={{0,8},{1,9},{2,10},{3,11},{4,12},{5,13},{6,14},{7,15},{8,0},{9,1},... | collective-permute-start | bytes 540680 | tf_op jit(solution)/shard_map/ppermute | solution.py:20
  51.9 1.2 %collective-permute-start.14 = (f32[352,128]{1,0:T(8,128)S(1)}, f32[352,128]{1,0:T(8,128)S(1)}, u32[]{:S(2)}, u32[]{:S(2)}) collective-permute-start(f32[352,128]{1,0:T(8,128)S(1)} %get-tuple-element.39), channel_id=1, source_target_pairs={{0,8},{1,9},{2,10},{3,11},{4,12},{5,13},{6,14},{7,15},{8,0},{9,1},... | collective-permute-start | bytes 540680 | tf_op jit(solution)/shard_map/ppermute | solution.py:20
  53.1 4.5 %collective-permute-done.10 = f32[352,128]{1,0:T(8,128)S(1)} collective-permute-done((f32[352,128]{1,0:T(8,128)S(1)}, f32[352,128]{1,0:T(8,128)S(1)}, u32[]{:S(2)}, u32[]{:S(2)}) %collective-permute-start.10) | collective-permute-done | bytes 180256 | tf_op jit(solution)/shard_map/ppermute | solution.py:20
  57.7 1.7 %collective-permute-start.11 = (f32[176,128]{1,0:T(8,128)S(1)}, f32[176,128]{1,0:T(8,128)S(1)}, u32[]{:S(2)}, u32[]{:S(2)}) collective-permute-start(f32[176,128]{1,0:T(8,128)S(1)} %get-tuple-element.48.refs_0_), channel_id=1, source_target_pairs={{0,16},{1,17},{2,18},{3,19},{4,20},{5,21},{6,22},{7,23},{8,24},{9,... | collective-permute-start | bytes 270344 | tf_op jit(solution)/shard_map/ppermute | solution.py:20
  59.4 0.0 collective-permute-done.17.first_add_ref
  59.4 0.3 collective-permute-start.20
  59.7 0.9 collective-permute-done.14
  60.6 1.3 %collective-permute-start.15 = (f32[176,128]{1,0:T(8,128)S(1)}, f32[176,128]{1,0:T(8,128)S(1)}, u32[]{:S(2)}, u32[]{:S(2)}) collective-permute-start(f32[176,128]{1,0:T(8,128)S(1)} %get-tuple-element.46), channel_id=1, source_target_pairs={{0,16},{1,17},{2,18},{3,19},{4,20},{5,21},{6,22},{7,23},{8,24},{9,... | collective-permute-start | bytes 270344 | tf_op jit(solution)/shard_map/ppermute | solution.py:20
  62.0 2.9 %collective-permute-done.20 = f32[320,128]{1,0:T(8,128)S(1)} collective-permute-done((f32[320,128]{1,0:T(8,128)S(1)}, f32[320,128]{1,0:T(8,128)S(1)}, u32[]{:S(2)}, u32[]{:S(2)}) %collective-permute-start.20) | collective-permute-done | bytes 163872 | tf_op jit(solution)/shard_map/ppermute | solution.py:20
  64.9 1.9 %collective-permute-start.21 = (f32[160,128]{1,0:T(8,128)S(1)}, f32[160,128]{1,0:T(8,128)S(1)}, u32[]{:S(2)}, u32[]{:S(2)}) collective-permute-start(f32[160,128]{1,0:T(8,128)S(1)} %pad_maximum_fusion.1), channel_id=1, source_target_pairs={{0,4},{1,5},{2,6},{3,7},{4,0},{5,1},{6,2},{7,3},{8,12},{9,13},{10,... | collective-permute-start | bytes 245768 | tf_op jit(solution)/shard_map/ppermute | solution.py:20
  66.8 0.9 collective-permute-done.15.refs_3_
  67.6 0.0 collective-permute-done.11.refs_1_
  67.6 1.7 %collective-permute-done.21.refs_5_ = f32[160,128]{1,0:T(8,128)S(1)} collective-permute-done((f32[160,128]{1,0:T(8,128)S(1)}, f32[160,128]{1,0:T(8,128)S(1)}, u32[]{:S(2)}, u32[]{:S(2)}) %collective-permute-start.21) | collective-permute-done | bytes 81952 | tf_op jit(solution)/shard_map/ppermute | solution.py:20
  69.4 1.4 %gram.1 = (f32[256,256]{1,0:T(8,128)}, f32[256,128]{1,0:T(8,128)S(1)}, f32[128,128]{1,0:T(8,128)S(1)}, f32[128,128]{1,0:T(8,128)S(1)}) custom-call(s32[1]{0:T(128)} %bitcast.ry_ref, s32[1536]{0:T(1024)S(1)} %bitcast.36, f32[176,128]{1,0:T(8,128)S(1)} %get-tuple-element.49.refs_0_, f32[176,128]{1,0:T(8,128)S(1)} %collective-permute-done.11.refs_1_, ...), custom_call_target="tpu_custom_call" | custom-call | flops 100663296 | bytes 1048576 | tf_op jit(solution)/shard_map/gram/pallas_call | solution.py:136
  70.8 0.0 collective-permute-start.22
  70.8 1.3 %collective-permute-done.22 = f32[256,128]{1,0:T(8,128)S(1)} collective-permute-done((f32[256,128]{1,0:T(8,128)S(1)}, f32[256,128]{1,0:T(8,128)S(1)}, u32[]{:S(2)}, u32[]{:S(2)}) %collective-permute-start.22) | collective-permute-done | bytes 131104 | tf_op jit(solution)/shard_map/ppermute | solution.py:20
  72.1 0.4 collective-permute-start.23
  72.6 2.0 %collective-permute-start.24 = (f32[128,128]{1,0:T(8,128)S(1)}, f32[128,128]{1,0:T(8,128)S(1)}, u32[]{:S(2)}, u32[]{:S(2)}) collective-permute-start(f32[128,128]{1,0:T(8,128)S(1)} %get-tuple-element.58), channel_id=1, source_target_pairs={{0,4},{1,5},{2,6},{3,7},{4,0},{5,1},{6,2},{7,3},{8,12},{9,13},{10,... | collective-permute-start | bytes 196616 | tf_op jit(solution)/shard_map/ppermute | solution.py:20
  74.6 1.1 %collective-permute-start.25 = (f32[128,128]{1,0:T(8,128)S(1)}, f32[128,128]{1,0:T(8,128)S(1)}, u32[]{:S(2)}, u32[]{:S(2)}) collective-permute-start(f32[128,128]{1,0:T(8,128)S(1)} %get-tuple-element.59), channel_id=1, source_target_pairs={{0,6},{1,7},{2,4},{3,5},{4,2},{5,3},{6,0},{7,1},{8,14},{9,15},{10,... | collective-permute-start | bytes 196616 | tf_op jit(solution)/shard_map/ppermute | solution.py:20
  75.7 0.8 collective-permute-done.23
  76.5 1.2 %collective-permute-done.24 = f32[128,128]{1,0:T(8,128)S(1)} collective-permute-done((f32[128,128]{1,0:T(8,128)S(1)}, f32[128,128]{1,0:T(8,128)S(1)}, u32[]{:S(2)}, u32[]{:S(2)}) %collective-permute-start.24) | collective-permute-done | bytes 65568 | tf_op jit(solution)/shard_map/ppermute | solution.py:20
  77.6 2.1 %collective-permute-done.25 = f32[128,128]{1,0:T(8,128)S(1)} collective-permute-done((f32[128,128]{1,0:T(8,128)S(1)}, f32[128,128]{1,0:T(8,128)S(1)}, u32[]{:S(2)}, u32[]{:S(2)}) %collective-permute-start.25) | collective-permute-done | bytes 65568 | tf_op jit(solution)/shard_map/ppermute | solution.py:20
  79.8 0.7 collective-permute-start.26
  80.4 1.9 %collective-permute-start.27 = (f32[128,128]{1,0:T(8,128)S(1)}, f32[128,128]{1,0:T(8,128)S(1)}, u32[]{:S(2)}, u32[]{:S(2)}) collective-permute-start(f32[128,128]{1,0:T(8,128)S(1)} %add_add_fusion), channel_id=1, source_target_pairs={{0,16},{1,17},{2,18},{3,19},{4,20},{5,21},{6,22},{7,23},{8,24},{9,... | collective-permute-start | bytes 196616 | tf_op jit(solution)/shard_map/ppermute | solution.py:20
  82.4 1.9 %collective-permute-start.28 = (f32[128,128]{1,0:T(8,128)S(1)}, f32[128,128]{1,0:T(8,128)S(1)}, u32[]{:S(2)}, u32[]{:S(2)}) collective-permute-start(f32[128,128]{1,0:T(8,128)S(1)} %add_add_fusion), channel_id=1, source_target_pairs={{0,24},{1,25},{2,26},{3,27},{4,28},{5,29},{6,30},{7,31},{8,16},{9,... | collective-permute-start | bytes 196616 | tf_op jit(solution)/shard_map/ppermute | solution.py:20
  84.2 0.0 collective-permute-done.26
  84.2 2.6 %collective-permute-done.27 = f32[128,128]{1,0:T(8,128)S(1)} collective-permute-done((f32[128,128]{1,0:T(8,128)S(1)}, f32[128,128]{1,0:T(8,128)S(1)}, u32[]{:S(2)}, u32[]{:S(2)}) %collective-permute-start.27) | collective-permute-done | bytes 65568 | tf_op jit(solution)/shard_map/ppermute | solution.py:20
  86.8 1.6 %collective-permute-done.28 = f32[128,128]{1,0:T(8,128)S(1)} collective-permute-done((f32[128,128]{1,0:T(8,128)S(1)}, f32[128,128]{1,0:T(8,128)S(1)}, u32[]{:S(2)}, u32[]{:S(2)}) %collective-permute-start.28) | collective-permute-done | bytes 65568 | tf_op jit(solution)/shard_map/ppermute | solution.py:20
  88.4 0.6 multiply_bitcast_fusion
  (17 shorter events, 0.3 us)
Async XLA Ops:
  0.6 16.5 %collective-permute-start.7 = (f32[4096,256]{1,0:T(8,128)}, f32[4096,256]{1,0:T(8,128)}, u32[]{:S(2)}, u32[]{:S(2)}) collective-permute-start(f32[4096,256]{1,0:T(8,128)} %refs_0_.1), channel_id=1, source_target_pairs={{0,1},{1,0},{2,3},{3,2},{4,5},{5,4},{6,7},{7,6},{8,9},{9,8},{10,11... | collective-permute-start | bytes 12582920 | tf_op jit(solution)/shard_map/ppermute | solution.py:20
  2.5 14.6 %collective-permute-start.6 = (s32[35,128]{1,0:T(8,128)S(1)}, s32[35,128]{1,0:T(8,128)S(1)}, u32[]{:S(2)}, u32[]{:S(2)}) collective-permute-start(s32[35,128]{1,0:T(8,128)S(1)} %fusion.1.signs_ref), channel_id=1, source_target_pairs={{0,1},{1,0},{2,3},{3,2},{4,5},{5,4},{6,7},{7,6},{8,9},{9,8},{10,11... | collective-permute-start | bytes 53768 | tf_op jit(solution)/shard_map/ppermute | solution.py:20
  2.6 5.6 %collective-permute-start = (s32[3,128]{1,0:T(4,128)S(1)}, s32[3,128]{1,0:T(4,128)S(1)}, u32[]{:S(2)}, u32[]{:S(2)}) collective-permute-start(s32[3,128]{1,0:T(4,128)S(1)} %slice.140.refs_0_), channel_id=1, source_target_pairs={{0,8},{1,9},{2,10},{3,11},{4,12},{5,13},{6,14},{7,15},{8,0},{9,1},... | collective-permute-start | bytes 4616 | tf_op jit(solution)/shard_map/ppermute | solution.py:20
  5.6 4.5 %collective-permute-start.1 = (s32[3,128]{1,0:T(4,128)S(1)}, s32[3,128]{1,0:T(4,128)S(1)}, u32[]{:S(2)}, u32[]{:S(2)}) collective-permute-start(s32[3,128]{1,0:T(4,128)S(1)} %slice.140.refs_0_), channel_id=1, source_target_pairs={{0,16},{1,17},{2,18},{3,19},{4,20},{5,21},{6,22},{7,23},{8,24},{9,... | collective-permute-start | bytes 4616 | tf_op jit(solution)/shard_map/ppermute | solution.py:20
  8.2 5.4 %collective-permute-start.2 = (s32[3,128]{1,0:T(4,128)S(1)}, s32[3,128]{1,0:T(4,128)S(1)}, u32[]{:S(2)}, u32[]{:S(2)}) collective-permute-start(s32[3,128]{1,0:T(4,128)S(1)} %slice.140.refs_0_), channel_id=1, source_target_pairs={{0,24},{1,25},{2,26},{3,27},{4,28},{5,29},{6,30},{7,31},{8,16},{9,... | collective-permute-start | bytes 4616 | tf_op jit(solution)/shard_map/ppermute | solution.py:20
  13.6 7.9 %collective-permute-start.3 = (s32[12,128]{1,0:T(8,128)S(1)}, s32[12,128]{1,0:T(8,128)S(1)}, u32[]{:S(2)}, u32[]{:S(2)}) collective-permute-start(s32[12,128]{1,0:T(8,128)S(1)} %join.1), channel_id=1, source_target_pairs={{0,2},{1,3},{2,0},{3,1},{4,6},{5,7},{6,4},{7,5},{8,10},{9,11},{10,... | collective-permute-start | bytes 18440 | tf_op jit(solution)/shard_map/ppermute | solution.py:20
  15.1 6.4 %collective-permute-start.4 = (s32[12,128]{1,0:T(8,128)S(1)}, s32[12,128]{1,0:T(8,128)S(1)}, u32[]{:S(2)}, u32[]{:S(2)}) collective-permute-start(s32[12,128]{1,0:T(8,128)S(1)} %join.1), channel_id=1, source_target_pairs={{0,4},{1,5},{2,6},{3,7},{4,0},{5,1},{6,2},{7,3},{8,12},{9,13},{10,... | collective-permute-start | bytes 18440 | tf_op jit(solution)/shard_map/ppermute | solution.py:20
  16.6 4.9 %collective-permute-start.5 = (s32[12,128]{1,0:T(8,128)S(1)}, s32[12,128]{1,0:T(8,128)S(1)}, u32[]{:S(2)}, u32[]{:S(2)}) collective-permute-start(s32[12,128]{1,0:T(8,128)S(1)} %join.1), channel_id=1, source_target_pairs={{0,6},{1,7},{2,4},{3,5},{4,2},{5,3},{6,0},{7,1},{8,14},{9,15},{10,... | collective-permute-start | bytes 18440 | tf_op jit(solution)/shard_map/ppermute | solution.py:20
  24.6 15.9 %collective-permute-start.8 = (f32[1408,128]{1,0:T(8,128)S(1)}, f32[1408,128]{1,0:T(8,128)S(1)}, u32[]{:S(2)}, u32[]{:S(2)}) collective-permute-start(f32[1408,128]{1,0:T(8,128)S(1)} %bitcast.51), channel_id=1, source_target_pairs={{0,2},{1,3},{2,0},{3,1},{4,6},{5,7},{6,4},{7,5},{8,10},{9,11},{10,... | collective-permute-start | bytes 2162696 | tf_op jit(solution)/shard_map/ppermute | solution.py:20
  26.2 13.3 %collective-permute-start.18 = (f32[640,128]{1,0:T(8,128)S(1)}, f32[640,128]{1,0:T(8,128)S(1)}, u32[]{:S(2)}, u32[]{:S(2)}) collective-permute-start(f32[640,128]{1,0:T(8,128)S(1)} %bitcast.52), channel_id=1, source_target_pairs={{0,16},{1,17},{2,18},{3,19},{4,20},{5,21},{6,22},{7,23},{8,24},{9,... | collective-permute-start | bytes 983048 | tf_op jit(solution)/shard_map/ppermute | solution.py:20
  26.2 16.0 %collective-permute-start.12 = (f32[1408,128]{1,0:T(8,128)S(1)}, f32[1408,128]{1,0:T(8,128)S(1)}, u32[]{:S(2)}, u32[]{:S(2)}) collective-permute-start(f32[1408,128]{1,0:T(8,128)S(1)} %bitcast.50), channel_id=1, source_target_pairs={{0,4},{1,5},{2,6},{3,7},{4,0},{5,1},{6,2},{7,3},{8,12},{9,13},{10,... | collective-permute-start | bytes 2162696 | tf_op jit(solution)/shard_map/ppermute | solution.py:20
  28.9 15.0 %collective-permute-start.16 = (f32[640,128]{1,0:T(8,128)S(1)}, f32[640,128]{1,0:T(8,128)S(1)}, u32[]{:S(2)}, u32[]{:S(2)}) collective-permute-start(f32[640,128]{1,0:T(8,128)S(1)} %bitcast.27), channel_id=1, source_target_pairs={{0,8},{1,9},{2,10},{3,11},{4,12},{5,13},{6,14},{7,15},{8,0},{9,1},... | collective-permute-start | bytes 983048 | tf_op jit(solution)/shard_map/ppermute | solution.py:20
  39.5 19.9 %collective-permute-start.19 = (f32[320,128]{1,0:T(8,128)S(1)}, f32[320,128]{1,0:T(8,128)S(1)}, u32[]{:S(2)}, u32[]{:S(2)}) collective-permute-start(f32[320,128]{1,0:T(8,128)S(1)} %get-tuple-element.54), channel_id=1, source_target_pairs={{0,8},{1,9},{2,10},{3,11},{4,12},{5,13},{6,14},{7,15},{8,0},{9,1},... | collective-permute-start | bytes 491528 | tf_op jit(solution)/shard_map/ppermute | solution.py:20
  40.6 9.4 %collective-permute-start.9 = (f32[704,128]{1,0:T(8,128)S(1)}, f32[704,128]{1,0:T(8,128)S(1)}, u32[]{:S(2)}, u32[]{:S(2)}) collective-permute-start(f32[704,128]{1,0:T(8,128)S(1)} %get-tuple-element.45), channel_id=1, source_target_pairs={{0,4},{1,5},{2,6},{3,7},{4,0},{5,1},{6,2},{7,3},{8,12},{9,13},{10,... | collective-permute-start | bytes 1081352 | tf_op jit(solution)/shard_map/ppermute | solution.py:20
  42.3 9.6 %collective-permute-start.13 = (f32[704,128]{1,0:T(8,128)S(1)}, f32[704,128]{1,0:T(8,128)S(1)}, u32[]{:S(2)}, u32[]{:S(2)}) collective-permute-start(f32[704,128]{1,0:T(8,128)S(1)} %get-tuple-element.41), channel_id=1, source_target_pairs={{0,2},{1,3},{2,0},{3,1},{4,6},{5,7},{6,4},{7,5},{8,10},{9,11},{10,... | collective-permute-start | bytes 1081352 | tf_op jit(solution)/shard_map/ppermute | solution.py:20
  43.9 15.5 %collective-permute-start.17 = (f32[320,128]{1,0:T(8,128)S(1)}, f32[320,128]{1,0:T(8,128)S(1)}, u32[]{:S(2)}, u32[]{:S(2)}) collective-permute-start(f32[320,128]{1,0:T(8,128)S(1)} %get-tuple-element.56), channel_id=1, source_target_pairs={{0,16},{1,17},{2,18},{3,19},{4,20},{5,21},{6,22},{7,23},{8,24},{9,... | collective-permute-start | bytes 491528 | tf_op jit(solution)/shard_map/ppermute | solution.py:20
  50.1 7.6 %collective-permute-start.10 = (f32[352,128]{1,0:T(8,128)S(1)}, f32[352,128]{1,0:T(8,128)S(1)}, u32[]{:S(2)}, u32[]{:S(2)}) collective-permute-start(f32[352,128]{1,0:T(8,128)S(1)} %get-tuple-element.43), channel_id=1, source_target_pairs={{0,8},{1,9},{2,10},{3,11},{4,12},{5,13},{6,14},{7,15},{8,0},{9,1},... | collective-permute-start | bytes 540680 | tf_op jit(solution)/shard_map/ppermute | solution.py:20
  51.9 8.7 %collective-permute-start.14 = (f32[352,128]{1,0:T(8,128)S(1)}, f32[352,128]{1,0:T(8,128)S(1)}, u32[]{:S(2)}, u32[]{:S(2)}) collective-permute-start(f32[352,128]{1,0:T(8,128)S(1)} %get-tuple-element.39), channel_id=1, source_target_pairs={{0,8},{1,9},{2,10},{3,11},{4,12},{5,13},{6,14},{7,15},{8,0},{9,1},... | collective-permute-start | bytes 540680 | tf_op jit(solution)/shard_map/ppermute | solution.py:20
  57.7 10.0 %collective-permute-start.11 = (f32[176,128]{1,0:T(8,128)S(1)}, f32[176,128]{1,0:T(8,128)S(1)}, u32[]{:S(2)}, u32[]{:S(2)}) collective-permute-start(f32[176,128]{1,0:T(8,128)S(1)} %get-tuple-element.48.refs_0_), channel_id=1, source_target_pairs={{0,16},{1,17},{2,18},{3,19},{4,20},{5,21},{6,22},{7,23},{8,24},{9,... | collective-permute-start | bytes 270344 | tf_op jit(solution)/shard_map/ppermute | solution.py:20
  59.4 5.4 %collective-permute-start.20 = (f32[320,128]{1,0:T(8,128)S(1)}, f32[320,128]{1,0:T(8,128)S(1)}, u32[]{:S(2)}, u32[]{:S(2)}) collective-permute-start(f32[320,128]{1,0:T(8,128)S(1)} %get-tuple-element.33), channel_id=1, source_target_pairs={{0,2},{1,3},{2,0},{3,1},{4,6},{5,7},{6,4},{7,5},{8,10},{9,11},{10,... | collective-permute-start | bytes 491528 | tf_op jit(solution)/shard_map/ppermute | solution.py:20
  60.6 7.0 %collective-permute-start.15 = (f32[176,128]{1,0:T(8,128)S(1)}, f32[176,128]{1,0:T(8,128)S(1)}, u32[]{:S(2)}, u32[]{:S(2)}) collective-permute-start(f32[176,128]{1,0:T(8,128)S(1)} %get-tuple-element.46), channel_id=1, source_target_pairs={{0,16},{1,17},{2,18},{3,19},{4,20},{5,21},{6,22},{7,23},{8,24},{9,... | collective-permute-start | bytes 270344 | tf_op jit(solution)/shard_map/ppermute | solution.py:20
  64.9 4.5 %collective-permute-start.21 = (f32[160,128]{1,0:T(8,128)S(1)}, f32[160,128]{1,0:T(8,128)S(1)}, u32[]{:S(2)}, u32[]{:S(2)}) collective-permute-start(f32[160,128]{1,0:T(8,128)S(1)} %pad_maximum_fusion.1), channel_id=1, source_target_pairs={{0,4},{1,5},{2,6},{3,7},{4,0},{5,1},{6,2},{7,3},{8,12},{9,13},{10,... | collective-permute-start | bytes 245768 | tf_op jit(solution)/shard_map/ppermute | solution.py:20
  70.8 1.3 %collective-permute-start.22 = (f32[256,128]{1,0:T(8,128)S(1)}, f32[256,128]{1,0:T(8,128)S(1)}, u32[]{:S(2)}, u32[]{:S(2)}) collective-permute-start(f32[256,128]{1,0:T(8,128)S(1)} %get-tuple-element.36), channel_id=1, source_target_pairs={{0,1},{1,0},{2,3},{3,2},{4,5},{5,4},{6,7},{7,6},{8,9},{9,8},{10,11... | collective-permute-start | bytes 393224 | tf_op jit(solution)/shard_map/ppermute | solution.py:20
  72.1 4.3 %collective-permute-start.23 = (f32[128,128]{1,0:T(8,128)S(1)}, f32[128,128]{1,0:T(8,128)S(1)}, u32[]{:S(2)}, u32[]{:S(2)}) collective-permute-start(f32[128,128]{1,0:T(8,128)S(1)} %get-tuple-element.59), channel_id=1, source_target_pairs={{0,2},{1,3},{2,0},{3,1},{4,6},{5,7},{6,4},{7,5},{8,10},{9,11},{10,... | collective-permute-start | bytes 196616 | tf_op jit(solution)/shard_map/ppermute | solution.py:20
  72.6 5.1 %collective-permute-start.24 = (f32[128,128]{1,0:T(8,128)S(1)}, f32[128,128]{1,0:T(8,128)S(1)}, u32[]{:S(2)}, u32[]{:S(2)}) collective-permute-start(f32[128,128]{1,0:T(8,128)S(1)} %get-tuple-element.58), channel_id=1, source_target_pairs={{0,4},{1,5},{2,6},{3,7},{4,0},{5,1},{6,2},{7,3},{8,12},{9,13},{10,... | collective-permute-start | bytes 196616 | tf_op jit(solution)/shard_map/ppermute | solution.py:20
  74.6 5.2 %collective-permute-start.25 = (f32[128,128]{1,0:T(8,128)S(1)}, f32[128,128]{1,0:T(8,128)S(1)}, u32[]{:S(2)}, u32[]{:S(2)}) collective-permute-start(f32[128,128]{1,0:T(8,128)S(1)} %get-tuple-element.59), channel_id=1, source_target_pairs={{0,6},{1,7},{2,4},{3,5},{4,2},{5,3},{6,0},{7,1},{8,14},{9,15},{10,... | collective-permute-start | bytes 196616 | tf_op jit(solution)/shard_map/ppermute | solution.py:20
  79.8 4.5 %collective-permute-start.26 = (f32[128,128]{1,0:T(8,128)S(1)}, f32[128,128]{1,0:T(8,128)S(1)}, u32[]{:S(2)}, u32[]{:S(2)}) collective-permute-start(f32[128,128]{1,0:T(8,128)S(1)} %add_add_fusion), channel_id=1, source_target_pairs={{0,8},{1,9},{2,10},{3,11},{4,12},{5,13},{6,14},{7,15},{8,0},{9,1},... | collective-permute-start | bytes 196616 | tf_op jit(solution)/shard_map/ppermute | solution.py:20
  80.4 6.4 %collective-permute-start.27 = (f32[128,128]{1,0:T(8,128)S(1)}, f32[128,128]{1,0:T(8,128)S(1)}, u32[]{:S(2)}, u32[]{:S(2)}) collective-permute-start(f32[128,128]{1,0:T(8,128)S(1)} %add_add_fusion), channel_id=1, source_target_pairs={{0,16},{1,17},{2,18},{3,19},{4,20},{5,21},{6,22},{7,23},{8,24},{9,... | collective-permute-start | bytes 196616 | tf_op jit(solution)/shard_map/ppermute | solution.py:20
  82.4 6.1 %collective-permute-start.28 = (f32[128,128]{1,0:T(8,128)S(1)}, f32[128,128]{1,0:T(8,128)S(1)}, u32[]{:S(2)}, u32[]{:S(2)}) collective-permute-start(f32[128,128]{1,0:T(8,128)S(1)} %add_add_fusion), channel_id=1, source_target_pairs={{0,24},{1,25},{2,26},{3,27},{4,28},{5,29},{6,30},{7,31},{8,16},{9,... | collective-permute-start | bytes 196616 | tf_op jit(solution)/shard_map/ppermute | solution.py:20

commit v5 on v2

--- a/solution.py
+++ b/solution.py
@@ -11,7 +11,7 @@
 MESH_AXES = ("rx", "ry")
 GRANT = 12 * 2**20
 WIDE = 46 * 2**20
-AHEAD = 3
+AHEAD = 2
 REST = 4
 
 
@@ -87,7 +87,7 @@
 
 def transform(full, me, matrix, signs, other_matrix, other_signs):
     rows, width = matrix.shape
-    chunks = 8
+    chunks = 4
     return pl.pallas_call(
         functools.partial(transform_kernel, full, chunks),
         in_specs=specs(1, 2) + [pl.BlockSpec(memory_space=pl.ANY)] * 2,
@@ -145,7 +145,7 @@
     )(*scalars, *arrays, *after)
 
 
-def gram_kernel(ry_ref, live_ref, *refs):
+def gram_kernel(ry_ref, list_ref, *refs):
     *part_refs, sketch_ref, on_ref, mine_ref, next_ref, rows_ref, blocks_ref = refs
     slots, cols = rows_ref.shape[0] // 2, rows_ref.shape[1]
     start = 0
@@ -153,7 +153,7 @@
         rows_ref[start:start + near_ref.shape[0], :] = near_ref[...] + add_ref[...]
         start += near_ref.shape[0]
     values = jnp.concatenate([rows_ref[pl.ds(half, slots, stride=2), :] for half in range(2)], axis=1)
-    live = lax.broadcasted_iota(jnp.int32, values.shape, 0) < live_ref[0]
+    live = lax.broadcasted_iota(jnp.int32, values.shape, 0) < list_ref[slots]
     values = jnp.where(live, values, 0.0)
     sketch_ref[...] = values
     high = values.astype(jnp.bfloat16)
@@ -178,7 +178,7 @@
     rows, width = matrix.shape
     slots = indices.shape[0]
     cols = width // 2
-    tail = slots // 32 * 9
+    tail = slots // 4
     head = slots - tail
     first = slots // 8 * 3
     size_x = lax.axis_size("rx")
@@ -199,7 +199,7 @@
     for bit in range(full - 1):
         other = swap(matrix, 1 << bit)
         matrix = jnp.where(jnp.bitwise_and(jnp.right_shift(me, bit), 1) == 1, other - matrix, matrix + other)
-    own = jnp.concatenate([indices, jnp.broadcast_to(counts, (BLK,)), signs.reshape(-1)]).reshape(-1, BLK)
+    own = jnp.concatenate([indices, jnp.pad(counts, (0, BLK - 1)), signs.reshape(-1)]).reshape(-1, BLK)
     own = lax.optimization_barrier(own)
     own_list = own[:stride // BLK]
     last = 1 << (full - 1)
@@ -231,8 +231,13 @@
     ends = gathered("gather_end", [(head, tail, [z + near for near in (0, 2, 1, 3)]) for z in (0, 8)])
     nears = gathered(
         "gather_near",
-        [(*a, distances(0, 0)), (*a, distances(0, 1)), (*b, distances(0, 0)), (*b, distances(1, 0))],
-        after=(end_add,),
+        [
+            (*a, distances(0, 0)),
+            (*a, distances(0, 1)),
+            (*b, distances(0, 0)),
+            (*b, distances(1, 0)),
+        ],
+        after=(end_on,),
     )
 
     def halved(value):
@@ -254,7 +259,7 @@
     sketch, on, block, far_block = call(
         gram_kernel,
         "gram",
-        (ry.astype(jnp.int32).reshape(1), counts),
+        (ry.astype(jnp.int32).reshape(1), lists[0]),
         (*finals, end, end_add),
         (floats(slots, width), floats(2 * cols, cols), floats(cols, cols), floats(cols, cols)),
         scratch=[pltpu.VMEM((2 * slots, cols), jnp.float32), pltpu.VMEM((4, cols, cols), jnp.float32)],

time: 87.2 us -> 86.6 us (level)
  starting transfers between devices: 33.8 us -> 36 us
  waiting for transfers between devices: 36.7 us -> 34.5 us
    ppermute x27, waiting for transfers between devices: 36.7 us -> 34.5 us  [swap(): return lax.ppermute(value, MESH_AXES, [(i, i ^ bits) for i in range(size)])]
    ppermute x27, starting transfers between devices: 33.8 us -> 36 us  [swap(): return lax.ppermute(value, MESH_AXES, [(i, i ^ bits) for i in range(size)])]
  transfers between devices with their start and end apart: 27 -> 27, of which waited for: 14 -> 16; matrix products, arithmetic and copies ran while one was open for 1% -> 1% of each run, Pallas kernels for 10% -> 9%
where the time goes in v5:
time: 86.6 us; the launch traced here: 86.3 us
  starting transfers between devices  36 us (42%)
  waiting for transfers between devices  34.5 us (40%)
  Pallas kernels  12.6 us (15%)
  other arithmetic  1.83 us (2%)
  between operations  1.39 us (2%)
    ppermute x27, starting transfers between devices, swap(): return lax.ppermute(value, MESH_AXES, [(i, i ^ bits) for i in range(size)])  36 us
    ppermute x27, waiting for transfers between devices, swap(): return lax.ppermute(value, MESH_AXES, [(i, i ^ bits) for i in range(size)])  34.5 us
    pallas_call x5, Pallas kernels, call(): pl.pallas_call(kernel, in_specs=specs(len(scalars), len(arrays)) + [pl.Bl...  8.24 us
    pallas_call x1, Pallas kernels, transform(): pl.pallas_call(functools.partial(transform_kernel, full, chunks), in_spec...  4.4 us
  transfers between devices with their start and end apart: 27, of which 16 were waited for; matrix products, arithmetic and copies ran while one was open for 1% of the time, Pallas kernels for 9%

profile of v5, /device:TPU:0, one launch (start us, length us, event | category | flops | bytes accessed | tf_op | source)
XLA Modules:
  0.0 86.3 jit_solution(12846966039153618031)
XLA Ops:
  0.6 0.5 collective-permute-start.7
  1.8 0.7 fusion.1.signs_ref
  2.5 0.1 collective-permute-start.6
  2.6 5.0 %collective-permute-start.2 = (s32[3,128]{1,0:T(4,128)S(1)}, s32[3,128]{1,0:T(4,128)S(1)}, u32[]{:S(2)}, u32[]{:S(2)}) collective-permute-start(s32[3,128]{1,0:T(4,128)S(1)} %slice.132.refs_0_), channel_id=1, source_target_pairs={{0,24},{1,25},{2,26},{3,27},{4,28},{5,29},{6,30},{7,31},{8,16},{9,... | collective-permute-start | bytes 4616 | tf_op jit(solution)/shard_map/ppermute | solution.py:20
  7.6 0.0 collective-permute-start.1
  7.6 0.6 collective-permute-start
  8.2 1.0 %collective-permute-done.2.refs_3_ = s32[3,128]{1,0:T(4,128)S(1)} collective-permute-done((s32[3,128]{1,0:T(4,128)S(1)}, s32[3,128]{1,0:T(4,128)S(1)}, u32[]{:S(2)}, u32[]{:S(2)}) %collective-permute-start.2) | collective-permute-done | bytes 1568 | tf_op jit(solution)/shard_map/ppermute | solution.py:20
  9.2 2.9 %collective-permute-done.1.refs_2_ = s32[3,128]{1,0:T(4,128)S(1)} collective-permute-done((s32[3,128]{1,0:T(4,128)S(1)}, s32[3,128]{1,0:T(4,128)S(1)}, u32[]{:S(2)}, u32[]{:S(2)}) %collective-permute-start.1) | collective-permute-done | bytes 1568 | tf_op jit(solution)/shard_map/ppermute | solution.py:20
  12.1 0.0 collective-permute-done.refs_1_
  12.1 2.4 %collective-permute-start.5 = (s32[12,128]{1,0:T(8,128)S(1)}, s32[12,128]{1,0:T(8,128)S(1)}, u32[]{:S(2)}, u32[]{:S(2)}) collective-permute-start(s32[12,128]{1,0:T(8,128)S(1)} %join.1), channel_id=1, source_target_pairs={{0,6},{1,7},{2,4},{3,5},{4,2},{5,3},{6,0},{7,1},{8,14},{9,15},{10,... | collective-permute-start | bytes 18440 | tf_op jit(solution)/shard_map/ppermute | solution.py:20
  14.6 0.5 collective-permute-start.4
  15.1 0.5 collective-permute-start.3
  15.6 0.0 collective-permute-done.6.other_signs_ref
  15.6 0.0 collective-permute-done.7.refs_1_
  15.6 4.4 %transform.1 = f32[8192,128]{1,0:T(8,128)S(1)} custom-call(s32[1]{0:T(128)} %bitcast.3.me_ref, s32[35,128]{1,0:T(8,128)S(1)} %fusion.1.signs_ref, s32[35,128]{1,0:T(8,128)S(1)} %collective-permute-done.6.other_signs_ref, f32[4096,256]{1,0:T(8,128)} %refs_0_.1, f32[4096,256]{1,0:T(8,128)} %collective-permute-done.7.refs_1_), custom_call_target="tpu_custom_call" | custom-call | flops 2147483648 | bytes 12582912 | tf_op jit(solution)/shard_map/transform/pallas_call | solution.py:91
  20.0 0.0 collective-permute-done.5
  20.0 0.0 collective-permute-done.4
  20.1 0.0 collective-permute-done.3
  20.1 3.1 %gather_far.1 = (f32[768,2,128]{2,1,0:T(2,128)S(1)}, f32[768,2,128]{2,1,0:T(2,128)S(1)}, f32[512,2,128]{2,1,0:T(2,128)S(1)}) custom-call(s32[1]{0:T(128)} %bitcast.3.me_ref, s32[1536]{0:T(1024)S(1)} %bitcast.31, s32[1536]{0:T(1024)S(1)} %bitcast.41, s32[1536]{0:T(1024)S(1)} %bitcast.38, s32[1536]{0:T(1024)S(1)} %bitcast.35, f32[4096,2,128]{2,1,0:T(2,128)S(1)} %bitcast.20), custom_call_target="tpu_custom_call" | custom-call | bytes 6291456 | tf_op jit(solution)/shard_map/gather_far/pallas_call | solution.py:136
  23.2 1.5 %collective-permute-start.8 = (f32[1536,128]{1,0:T(8,128)S(1)}, f32[1536,128]{1,0:T(8,128)S(1)}, u32[]{:S(2)}, u32[]{:S(2)}) collective-permute-start(f32[1536,128]{1,0:T(8,128)S(1)} %bitcast.45), channel_id=1, source_target_pairs={{0,2},{1,3},{2,0},{3,1},{4,6},{5,7},{6,4},{7,5},{8,10},{9,11},{10,... | collective-permute-start | bytes 2359304 | tf_op jit(solution)/shard_map/ppermute | solution.py:20
  24.7 0.0 collective-permute-start.16
  24.7 1.3 %collective-permute-start.12 = (f32[1536,128]{1,0:T(8,128)S(1)}, f32[1536,128]{1,0:T(8,128)S(1)}, u32[]{:S(2)}, u32[]{:S(2)}) collective-permute-start(f32[1536,128]{1,0:T(8,128)S(1)} %bitcast.44), channel_id=1, source_target_pairs={{0,4},{1,5},{2,6},{3,7},{4,0},{5,1},{6,2},{7,3},{8,12},{9,13},{10,... | collective-permute-start | bytes 2359304 | tf_op jit(solution)/shard_map/ppermute | solution.py:20
  26.0 1.2 %gather_end.1 = (f32[256,2,128]{2,1,0:T(2,128)S(1)}, f32[256,2,128]{2,1,0:T(2,128)S(1)}) custom-call(s32[1]{0:T(128)} %bitcast.3.me_ref, s32[1536]{0:T(1024)S(1)} %bitcast.32, s32[1536]{0:T(1024)S(1)} %bitcast.42, s32[1536]{0:T(1024)S(1)} %bitcast.39, s32[1536]{0:T(1024)S(1)} %bitcast.36, f32[4096,2,128]{2,1,0:T(2,128)S(1)} %bitcast.21), custom_call_target="tpu_custom_call" | custom-call | bytes 4718592 | tf_op jit(solution)/shard_map/gather_end/pallas_call | solution.py:136
  27.2 2.5 %gather_near.1 = (f32[384,2,128]{2,1,0:T(2,128)S(1)}, f32[384,2,128]{2,1,0:T(2,128)S(1)}, f32[384,2,128]{2,1,0:T(2,128)S(1)}, f32[384,2,128]{2,1,0:T(2,128)S(1)}) custom-call(s32[1]{0:T(128)} %bitcast.3.me_ref, s32[1536]{0:T(1024)S(1)} %bitcast.33, s32[1536]{0:T(1024)S(1)} %bitcast.43, s32[1536]{0:T(1024)S(1)} %bitcast.40, s32[1536]{0:T(1024)S(1)} %bitcast.37, ...), custom_call_target="tpu_custom_call" | custom-call | bytes 5767168 | tf_op jit(solution)/shard_map/gather_near/pallas_call | solution.py:136
  29.7 6.4 %collective-permute-done.16 = f32[1024,128]{1,0:T(8,128)S(1)} collective-permute-done((f32[1024,128]{1,0:T(8,128)S(1)}, f32[1024,128]{1,0:T(8,128)S(1)}, u32[]{:S(2)}, u32[]{:S(2)}) %collective-permute-start.16) | collective-permute-done | bytes 524320 | tf_op jit(solution)/shard_map/ppermute | solution.py:20
  36.2 0.1 slice_add_fusion.5
  36.2 2.6 %collective-permute-start.17 = (f32[512,128]{1,0:T(8,128)S(1)}, f32[512,128]{1,0:T(8,128)S(1)}, u32[]{:S(2)}, u32[]{:S(2)}) collective-permute-start(f32[512,128]{1,0:T(8,128)S(1)} %get-tuple-element.39), channel_id=1, source_target_pairs={{0,16},{1,17},{2,18},{3,19},{4,20},{5,21},{6,22},{7,23},{8,24},{9,... | collective-permute-start | bytes 786440 | tf_op jit(solution)/shard_map/ppermute | solution.py:20
  38.8 1.8 %collective-permute-done.8 = f32[1536,128]{1,0:T(8,128)S(1)} collective-permute-done((f32[1536,128]{1,0:T(8,128)S(1)}, f32[1536,128]{1,0:T(8,128)S(1)}, u32[]{:S(2)}, u32[]{:S(2)}) %collective-permute-start.8) | collective-permute-done | bytes 786464 | tf_op jit(solution)/shard_map/ppermute | solution.py:20
  40.6 0.1 slice_add_fusion.3
  40.7 1.5 %collective-permute-start.9 = (f32[768,128]{1,0:T(8,128)S(1)}, f32[768,128]{1,0:T(8,128)S(1)}, u32[]{:S(2)}, u32[]{:S(2)}) collective-permute-start(f32[768,128]{1,0:T(8,128)S(1)} %get-tuple-element.35), channel_id=1, source_target_pairs={{0,4},{1,5},{2,6},{3,7},{4,0},{5,1},{6,2},{7,3},{8,12},{9,13},{10,... | collective-permute-start | bytes 1179656 | tf_op jit(solution)/shard_map/ppermute | solution.py:20
  42.1 1.1 %collective-permute-done.12 = f32[1536,128]{1,0:T(8,128)S(1)} collective-permute-done((f32[1536,128]{1,0:T(8,128)S(1)}, f32[1536,128]{1,0:T(8,128)S(1)}, u32[]{:S(2)}, u32[]{:S(2)}) %collective-permute-start.12) | collective-permute-done | bytes 786464 | tf_op jit(solution)/shard_map/ppermute | solution.py:20
  43.2 0.1 slice_add_fusion.1
  43.3 0.5 collective-permute-start.13
  43.8 4.0 %collective-permute-done.17 = f32[512,128]{1,0:T(8,128)S(1)} collective-permute-done((f32[512,128]{1,0:T(8,128)S(1)}, f32[512,128]{1,0:T(8,128)S(1)}, u32[]{:S(2)}, u32[]{:S(2)}) %collective-permute-start.17) | collective-permute-done | bytes 262176 | tf_op jit(solution)/shard_map/ppermute | solution.py:20
  47.8 0.6 collective-permute-start.18
  48.4 1.9 %collective-permute-done.9 = f32[768,128]{1,0:T(8,128)S(1)} collective-permute-done((f32[768,128]{1,0:T(8,128)S(1)}, f32[768,128]{1,0:T(8,128)S(1)}, u32[]{:S(2)}, u32[]{:S(2)}) %collective-permute-start.9) | collective-permute-done | bytes 393248 | tf_op jit(solution)/shard_map/ppermute | solution.py:20
  50.2 0.1 slice_add_fusion.9
  50.3 1.8 %collective-permute-start.10 = (f32[384,128]{1,0:T(8,128)S(1)}, f32[384,128]{1,0:T(8,128)S(1)}, u32[]{:S(2)}, u32[]{:S(2)}) collective-permute-start(f32[384,128]{1,0:T(8,128)S(1)} %get-tuple-element.33), channel_id=1, source_target_pairs={{0,8},{1,9},{2,10},{3,11},{4,12},{5,13},{6,14},{7,15},{8,0},{9,1},... | collective-permute-start | bytes 589832 | tf_op jit(solution)/shard_map/ppermute | solution.py:20
  52.1 0.5 collective-permute-done.13
  52.6 2.3 %collective-permute-start.14 = (f32[384,128]{1,0:T(8,128)S(1)}, f32[384,128]{1,0:T(8,128)S(1)}, u32[]{:S(2)}, u32[]{:S(2)}) collective-permute-start(f32[384,128]{1,0:T(8,128)S(1)} %get-tuple-element.29), channel_id=1, source_target_pairs={{0,8},{1,9},{2,10},{3,11},{4,12},{5,13},{6,14},{7,15},{8,0},{9,1},... | collective-permute-start | bytes 589832 | tf_op jit(solution)/shard_map/ppermute | solution.py:20
  54.9 3.0 %collective-permute-done.10 = f32[384,128]{1,0:T(8,128)S(1)} collective-permute-done((f32[384,128]{1,0:T(8,128)S(1)}, f32[384,128]{1,0:T(8,128)S(1)}, u32[]{:S(2)}, u32[]{:S(2)}) %collective-permute-start.10) | collective-permute-done | bytes 196640 | tf_op jit(solution)/shard_map/ppermute | solution.py:20
  57.9 2.4 %collective-permute-start.11 = (f32[192,128]{1,0:T(8,128)S(1)}, f32[192,128]{1,0:T(8,128)S(1)}, u32[]{:S(2)}, u32[]{:S(2)}) collective-permute-start(f32[192,128]{1,0:T(8,128)S(1)} %get-tuple-element.42), channel_id=1, source_target_pairs={{0,16},{1,17},{2,18},{3,19},{4,20},{5,21},{6,22},{7,23},{8,24},{9,... | collective-permute-start | bytes 294920 | tf_op jit(solution)/shard_map/ppermute | solution.py:20
  60.3 0.7 collective-permute-done.14
  61.0 2.4 %collective-permute-start.15 = (f32[192,128]{1,0:T(8,128)S(1)}, f32[192,128]{1,0:T(8,128)S(1)}, u32[]{:S(2)}, u32[]{:S(2)}) collective-permute-start(f32[192,128]{1,0:T(8,128)S(1)} %get-tuple-element.40), channel_id=1, source_target_pairs={{0,16},{1,17},{2,18},{3,19},{4,20},{5,21},{6,22},{7,23},{8,24},{9,... | collective-permute-start | bytes 294920 | tf_op jit(solution)/shard_map/ppermute | solution.py:20
  63.4 0.0 collective-permute-done.18
  63.5 1.5 %collective-permute-start.19 = (f32[128,128]{1,0:T(8,128)S(1)}, f32[128,128]{1,0:T(8,128)S(1)}, u32[]{:S(2)}, u32[]{:S(2)}) collective-permute-start(f32[128,128]{1,0:T(8,128)S(1)} %get-tuple-element.44), channel_id=1, source_target_pairs={{0,4},{1,5},{2,6},{3,7},{4,0},{5,1},{6,2},{7,3},{8,12},{9,13},{10,... | collective-permute-start | bytes 196616 | tf_op jit(solution)/shard_map/ppermute | solution.py:20
  64.9 2.9 %collective-permute-done.19.refs_5_ = f32[128,128]{1,0:T(8,128)S(1)} collective-permute-done((f32[128,128]{1,0:T(8,128)S(1)}, f32[128,128]{1,0:T(8,128)S(1)}, u32[]{:S(2)}, u32[]{:S(2)}) %collective-permute-start.19) | collective-permute-done | bytes 65568 | tf_op jit(solution)/shard_map/ppermute | solution.py:20
  67.8 0.0 collective-permute-done.11.refs_1_
  67.8 1.4 %gram.1 = (f32[256,256]{1,0:T(8,128)}, f32[256,128]{1,0:T(8,128)S(1)}, f32[128,128]{1,0:T(8,128)S(1)}, f32[128,128]{1,0:T(8,128)S(1)}) custom-call(s32[1]{0:T(128)} %bitcast.ry_ref, s32[1536]{0:T(1024)S(1)} %bitcast.34, f32[192,128]{1,0:T(8,128)S(1)} %get-tuple-element.43.refs_0_, f32[192,128]{1,0:T(8,128)S(1)} %collective-permute-done.11.refs_1_, ...), custom_call_target="tpu_custom_call" | custom-call | flops 100663296 | bytes 1048576 | tf_op jit(solution)/shard_map/gram/pallas_call | solution.py:136
  69.2 0.0 collective-permute-start.20
  69.2 1.3 %collective-permute-done.20 = f32[256,128]{1,0:T(8,128)S(1)} collective-permute-done((f32[256,128]{1,0:T(8,128)S(1)}, f32[256,128]{1,0:T(8,128)S(1)}, u32[]{:S(2)}, u32[]{:S(2)}) %collective-permute-start.20) | collective-permute-done | bytes 131104 | tf_op jit(solution)/shard_map/ppermute | solution.py:20
  70.6 1.5 %collective-permute-start.22 = (f32[128,128]{1,0:T(8,128)S(1)}, f32[128,128]{1,0:T(8,128)S(1)}, u32[]{:S(2)}, u32[]{:S(2)}) collective-permute-start(f32[128,128]{1,0:T(8,128)S(1)} %get-tuple-element.46), channel_id=1, source_target_pairs={{0,4},{1,5},{2,6},{3,7},{4,0},{5,1},{6,2},{7,3},{8,12},{9,13},{10,... | collective-permute-start | bytes 196616 | tf_op jit(solution)/shard_map/ppermute | solution.py:20
  72.1 0.4 collective-permute-start.23
  72.4 1.7 %collective-permute-start.21 = (f32[128,128]{1,0:T(8,128)S(1)}, f32[128,128]{1,0:T(8,128)S(1)}, u32[]{:S(2)}, u32[]{:S(2)}) collective-permute-start(f32[128,128]{1,0:T(8,128)S(1)} %get-tuple-element.47), channel_id=1, source_target_pairs={{0,2},{1,3},{2,0},{3,1},{4,6},{5,7},{6,4},{7,5},{8,10},{9,11},{10,... | collective-permute-start | bytes 196616 | tf_op jit(solution)/shard_map/ppermute | solution.py:20
  74.1 0.8 collective-permute-done.22
  74.9 2.6 %collective-permute-done.23 = f32[128,128]{1,0:T(8,128)S(1)} collective-permute-done((f32[128,128]{1,0:T(8,128)S(1)}, f32[128,128]{1,0:T(8,128)S(1)}, u32[]{:S(2)}, u32[]{:S(2)}) %collective-permute-start.23) | collective-permute-done | bytes 65568 | tf_op jit(solution)/shard_map/ppermute | solution.py:20
  77.5 0.0 collective-permute-done.21
  77.6 2.3 %collective-permute-start.26 = (f32[128,128]{1,0:T(8,128)S(1)}, f32[128,128]{1,0:T(8,128)S(1)}, u32[]{:S(2)}, u32[]{:S(2)}) collective-permute-start(f32[128,128]{1,0:T(8,128)S(1)} %add_add_fusion), channel_id=1, source_target_pairs={{0,24},{1,25},{2,26},{3,27},{4,28},{5,29},{6,30},{7,31},{8,16},{9,... | collective-permute-start | bytes 196616 | tf_op jit(solution)/shard_map/ppermute | solution.py:20
  79.8 0.0 collective-permute-start.25
  79.8 2.2 %collective-permute-start.24 = (f32[128,128]{1,0:T(8,128)S(1)}, f32[128,128]{1,0:T(8,128)S(1)}, u32[]{:S(2)}, u32[]{:S(2)}) collective-permute-start(f32[128,128]{1,0:T(8,128)S(1)} %add_add_fusion), channel_id=1, source_target_pairs={{0,8},{1,9},{2,10},{3,11},{4,12},{5,13},{6,14},{7,15},{8,0},{9,1},... | collective-permute-start | bytes 196616 | tf_op jit(solution)/shard_map/ppermute | solution.py:20
  82.0 2.2 %collective-permute-done.26 = f32[128,128]{1,0:T(8,128)S(1)} collective-permute-done((f32[128,128]{1,0:T(8,128)S(1)}, f32[128,128]{1,0:T(8,128)S(1)}, u32[]{:S(2)}, u32[]{:S(2)}) %collective-permute-start.26) | collective-permute-done | bytes 65568 | tf_op jit(solution)/shard_map/ppermute | solution.py:20
  84.3 1.4 %collective-permute-done.25 = f32[128,128]{1,0:T(8,128)S(1)} collective-permute-done((f32[128,128]{1,0:T(8,128)S(1)}, f32[128,128]{1,0:T(8,128)S(1)}, u32[]{:S(2)}, u32[]{:S(2)}) %collective-permute-start.25) | collective-permute-done | bytes 65568 | tf_op jit(solution)/shard_map/ppermute | solution.py:20
  85.6 0.0 collective-permute-done.24
  85.6 0.6 multiply_bitcast_fusion
  (10 shorter events, 0.2 us)
Async XLA Ops:
  0.6 15.0 %collective-permute-start.7 = (f32[4096,256]{1,0:T(8,128)}, f32[4096,256]{1,0:T(8,128)}, u32[]{:S(2)}, u32[]{:S(2)}) collective-permute-start(f32[4096,256]{1,0:T(8,128)} %refs_0_.1), channel_id=1, source_target_pairs={{0,1},{1,0},{2,3},{3,2},{4,5},{5,4},{6,7},{7,6},{8,9},{9,8},{10,11... | collective-permute-start | bytes 12582920 | tf_op jit(solution)/shard_map/ppermute | solution.py:20
  2.5 13.1 %collective-permute-start.6 = (s32[35,128]{1,0:T(8,128)S(1)}, s32[35,128]{1,0:T(8,128)S(1)}, u32[]{:S(2)}, u32[]{:S(2)}) collective-permute-start(s32[35,128]{1,0:T(8,128)S(1)} %fusion.1.signs_ref), channel_id=1, source_target_pairs={{0,1},{1,0},{2,3},{3,2},{4,5},{5,4},{6,7},{7,6},{8,9},{9,8},{10,11... | collective-permute-start | bytes 53768 | tf_op jit(solution)/shard_map/ppermute | solution.py:20
  2.6 6.6 %collective-permute-start.2 = (s32[3,128]{1,0:T(4,128)S(1)}, s32[3,128]{1,0:T(4,128)S(1)}, u32[]{:S(2)}, u32[]{:S(2)}) collective-permute-start(s32[3,128]{1,0:T(4,128)S(1)} %slice.132.refs_0_), channel_id=1, source_target_pairs={{0,24},{1,25},{2,26},{3,27},{4,28},{5,29},{6,30},{7,31},{8,16},{9,... | collective-permute-start | bytes 4616 | tf_op jit(solution)/shard_map/ppermute | solution.py:20
  7.6 4.5 %collective-permute-start.1 = (s32[3,128]{1,0:T(4,128)S(1)}, s32[3,128]{1,0:T(4,128)S(1)}, u32[]{:S(2)}, u32[]{:S(2)}) collective-permute-start(s32[3,128]{1,0:T(4,128)S(1)} %slice.132.refs_0_), channel_id=1, source_target_pairs={{0,16},{1,17},{2,18},{3,19},{4,20},{5,21},{6,22},{7,23},{8,24},{9,... | collective-permute-start | bytes 4616 | tf_op jit(solution)/shard_map/ppermute | solution.py:20
  7.6 4.5 %collective-permute-start = (s32[3,128]{1,0:T(4,128)S(1)}, s32[3,128]{1,0:T(4,128)S(1)}, u32[]{:S(2)}, u32[]{:S(2)}) collective-permute-start(s32[3,128]{1,0:T(4,128)S(1)} %slice.132.refs_0_), channel_id=1, source_target_pairs={{0,8},{1,9},{2,10},{3,11},{4,12},{5,13},{6,14},{7,15},{8,0},{9,1},... | collective-permute-start | bytes 4616 | tf_op jit(solution)/shard_map/ppermute | solution.py:20
  12.1 7.9 %collective-permute-start.5 = (s32[12,128]{1,0:T(8,128)S(1)}, s32[12,128]{1,0:T(8,128)S(1)}, u32[]{:S(2)}, u32[]{:S(2)}) collective-permute-start(s32[12,128]{1,0:T(8,128)S(1)} %join.1), channel_id=1, source_target_pairs={{0,6},{1,7},{2,4},{3,5},{4,2},{5,3},{6,0},{7,1},{8,14},{9,15},{10,... | collective-permute-start | bytes 18440 | tf_op jit(solution)/shard_map/ppermute | solution.py:20
  14.6 5.5 %collective-permute-start.4 = (s32[12,128]{1,0:T(8,128)S(1)}, s32[12,128]{1,0:T(8,128)S(1)}, u32[]{:S(2)}, u32[]{:S(2)}) collective-permute-start(s32[12,128]{1,0:T(8,128)S(1)} %join.1), channel_id=1, source_target_pairs={{0,4},{1,5},{2,6},{3,7},{4,0},{5,1},{6,2},{7,3},{8,12},{9,13},{10,... | collective-permute-start | bytes 18440 | tf_op jit(solution)/shard_map/ppermute | solution.py:20
  15.1 5.0 %collective-permute-start.3 = (s32[12,128]{1,0:T(8,128)S(1)}, s32[12,128]{1,0:T(8,128)S(1)}, u32[]{:S(2)}, u32[]{:S(2)}) collective-permute-start(s32[12,128]{1,0:T(8,128)S(1)} %join.1), channel_id=1, source_target_pairs={{0,2},{1,3},{2,0},{3,1},{4,6},{5,7},{6,4},{7,5},{8,10},{9,11},{10,... | collective-permute-start | bytes 18440 | tf_op jit(solution)/shard_map/ppermute | solution.py:20
  23.2 17.4 %collective-permute-start.8 = (f32[1536,128]{1,0:T(8,128)S(1)}, f32[1536,128]{1,0:T(8,128)S(1)}, u32[]{:S(2)}, u32[]{:S(2)}) collective-permute-start(f32[1536,128]{1,0:T(8,128)S(1)} %bitcast.45), channel_id=1, source_target_pairs={{0,2},{1,3},{2,0},{3,1},{4,6},{5,7},{6,4},{7,5},{8,10},{9,11},{10,... | collective-permute-start | bytes 2359304 | tf_op jit(solution)/shard_map/ppermute | solution.py:20
  24.7 11.5 %collective-permute-start.16 = (f32[1024,128]{1,0:T(8,128)S(1)}, f32[1024,128]{1,0:T(8,128)S(1)}, u32[]{:S(2)}, u32[]{:S(2)}) collective-permute-start(f32[1024,128]{1,0:T(8,128)S(1)} %bitcast.23), channel_id=1, source_target_pairs={{0,8},{1,9},{2,10},{3,11},{4,12},{5,13},{6,14},{7,15},{8,0},{9,1},... | collective-permute-start | bytes 1572872 | tf_op jit(solution)/shard_map/ppermute | solution.py:20
  24.7 18.5 %collective-permute-start.12 = (f32[1536,128]{1,0:T(8,128)S(1)}, f32[1536,128]{1,0:T(8,128)S(1)}, u32[]{:S(2)}, u32[]{:S(2)}) collective-permute-start(f32[1536,128]{1,0:T(8,128)S(1)} %bitcast.44), channel_id=1, source_target_pairs={{0,4},{1,5},{2,6},{3,7},{4,0},{5,1},{6,2},{7,3},{8,12},{9,13},{10,... | collective-permute-start | bytes 2359304 | tf_op jit(solution)/shard_map/ppermute | solution.py:20
  36.2 11.5 %collective-permute-start.17 = (f32[512,128]{1,0:T(8,128)S(1)}, f32[512,128]{1,0:T(8,128)S(1)}, u32[]{:S(2)}, u32[]{:S(2)}) collective-permute-start(f32[512,128]{1,0:T(8,128)S(1)} %get-tuple-element.39), channel_id=1, source_target_pairs={{0,16},{1,17},{2,18},{3,19},{4,20},{5,21},{6,22},{7,23},{8,24},{9,... | collective-permute-start | bytes 786440 | tf_op jit(solution)/shard_map/ppermute | solution.py:20
  40.7 9.6 %collective-permute-start.9 = (f32[768,128]{1,0:T(8,128)S(1)}, f32[768,128]{1,0:T(8,128)S(1)}, u32[]{:S(2)}, u32[]{:S(2)}) collective-permute-start(f32[768,128]{1,0:T(8,128)S(1)} %get-tuple-element.35), channel_id=1, source_target_pairs={{0,4},{1,5},{2,6},{3,7},{4,0},{5,1},{6,2},{7,3},{8,12},{9,13},{10,... | collective-permute-start | bytes 1179656 | tf_op jit(solution)/shard_map/ppermute | solution.py:20
  43.3 9.2 %collective-permute-start.13 = (f32[768,128]{1,0:T(8,128)S(1)}, f32[768,128]{1,0:T(8,128)S(1)}, u32[]{:S(2)}, u32[]{:S(2)}) collective-permute-start(f32[768,128]{1,0:T(8,128)S(1)} %get-tuple-element.31), channel_id=1, source_target_pairs={{0,2},{1,3},{2,0},{3,1},{4,6},{5,7},{6,4},{7,5},{8,10},{9,11},{10,... | collective-permute-start | bytes 1179656 | tf_op jit(solution)/shard_map/ppermute | solution.py:20
  47.8 15.7 %collective-permute-start.18 = (f32[256,128]{1,0:T(8,128)S(1)}, f32[256,128]{1,0:T(8,128)S(1)}, u32[]{:S(2)}, u32[]{:S(2)}) collective-permute-start(f32[256,128]{1,0:T(8,128)S(1)} %get-tuple-element.37), channel_id=1, source_target_pairs={{0,2},{1,3},{2,0},{3,1},{4,6},{5,7},{6,4},{7,5},{8,10},{9,11},{10,... | collective-permute-start | bytes 393224 | tf_op jit(solution)/shard_map/ppermute | solution.py:20
  50.3 7.6 %collective-permute-start.10 = (f32[384,128]{1,0:T(8,128)S(1)}, f32[384,128]{1,0:T(8,128)S(1)}, u32[]{:S(2)}, u32[]{:S(2)}) collective-permute-start(f32[384,128]{1,0:T(8,128)S(1)} %get-tuple-element.33), channel_id=1, source_target_pairs={{0,8},{1,9},{2,10},{3,11},{4,12},{5,13},{6,14},{7,15},{8,0},{9,1},... | collective-permute-start | bytes 589832 | tf_op jit(solution)/shard_map/ppermute | solution.py:20
  52.6 8.4 %collective-permute-start.14 = (f32[384,128]{1,0:T(8,128)S(1)}, f32[384,128]{1,0:T(8,128)S(1)}, u32[]{:S(2)}, u32[]{:S(2)}) collective-permute-start(f32[384,128]{1,0:T(8,128)S(1)} %get-tuple-element.29), channel_id=1, source_target_pairs={{0,8},{1,9},{2,10},{3,11},{4,12},{5,13},{6,14},{7,15},{8,0},{9,1},... | collective-permute-start | bytes 589832 | tf_op jit(solution)/shard_map/ppermute | solution.py:20
  57.9 9.9 %collective-permute-start.11 = (f32[192,128]{1,0:T(8,128)S(1)}, f32[192,128]{1,0:T(8,128)S(1)}, u32[]{:S(2)}, u32[]{:S(2)}) collective-permute-start(f32[192,128]{1,0:T(8,128)S(1)} %get-tuple-element.42), channel_id=1, source_target_pairs={{0,16},{1,17},{2,18},{3,19},{4,20},{5,21},{6,22},{7,23},{8,24},{9,... | collective-permute-start | bytes 294920 | tf_op jit(solution)/shard_map/ppermute | solution.py:20
  61.0 6.8 %collective-permute-start.15 = (f32[192,128]{1,0:T(8,128)S(1)}, f32[192,128]{1,0:T(8,128)S(1)}, u32[]{:S(2)}, u32[]{:S(2)}) collective-permute-start(f32[192,128]{1,0:T(8,128)S(1)} %get-tuple-element.40), channel_id=1, source_target_pairs={{0,16},{1,17},{2,18},{3,19},{4,20},{5,21},{6,22},{7,23},{8,24},{9,... | collective-permute-start | bytes 294920 | tf_op jit(solution)/shard_map/ppermute | solution.py:20
  63.5 4.3 %collective-permute-start.19 = (f32[128,128]{1,0:T(8,128)S(1)}, f32[128,128]{1,0:T(8,128)S(1)}, u32[]{:S(2)}, u32[]{:S(2)}) collective-permute-start(f32[128,128]{1,0:T(8,128)S(1)} %get-tuple-element.44), channel_id=1, source_target_pairs={{0,4},{1,5},{2,6},{3,7},{4,0},{5,1},{6,2},{7,3},{8,12},{9,13},{10,... | collective-permute-start | bytes 196616 | tf_op jit(solution)/shard_map/ppermute | solution.py:20
  69.2 1.3 %collective-permute-start.20 = (f32[256,128]{1,0:T(8,128)S(1)}, f32[256,128]{1,0:T(8,128)S(1)}, u32[]{:S(2)}, u32[]{:S(2)}) collective-permute-start(f32[256,128]{1,0:T(8,128)S(1)} %get-tuple-element.26), channel_id=1, source_target_pairs={{0,1},{1,0},{2,3},{3,2},{4,5},{5,4},{6,7},{7,6},{8,9},{9,8},{10,11... | collective-permute-start | bytes 393224 | tf_op jit(solution)/shard_map/ppermute | solution.py:20
  70.6 4.3 %collective-permute-start.22 = (f32[128,128]{1,0:T(8,128)S(1)}, f32[128,128]{1,0:T(8,128)S(1)}, u32[]{:S(2)}, u32[]{:S(2)}) collective-permute-start(f32[128,128]{1,0:T(8,128)S(1)} %get-tuple-element.46), channel_id=1, source_target_pairs={{0,4},{1,5},{2,6},{3,7},{4,0},{5,1},{6,2},{7,3},{8,12},{9,13},{10,... | collective-permute-start | bytes 196616 | tf_op jit(solution)/shard_map/ppermute | solution.py:20
  72.1 5.5 %collective-permute-start.23 = (f32[128,128]{1,0:T(8,128)S(1)}, f32[128,128]{1,0:T(8,128)S(1)}, u32[]{:S(2)}, u32[]{:S(2)}) collective-permute-start(f32[128,128]{1,0:T(8,128)S(1)} %get-tuple-element.47), channel_id=1, source_target_pairs={{0,6},{1,7},{2,4},{3,5},{4,2},{5,3},{6,0},{7,1},{8,14},{9,15},{10,... | collective-permute-start | bytes 196616 | tf_op jit(solution)/shard_map/ppermute | solution.py:20
  72.4 5.1 %collective-permute-start.21 = (f32[128,128]{1,0:T(8,128)S(1)}, f32[128,128]{1,0:T(8,128)S(1)}, u32[]{:S(2)}, u32[]{:S(2)}) collective-permute-start(f32[128,128]{1,0:T(8,128)S(1)} %get-tuple-element.47), channel_id=1, source_target_pairs={{0,2},{1,3},{2,0},{3,1},{4,6},{5,7},{6,4},{7,5},{8,10},{9,11},{10,... | collective-permute-start | bytes 196616 | tf_op jit(solution)/shard_map/ppermute | solution.py:20
  77.6 6.7 %collective-permute-start.26 = (f32[128,128]{1,0:T(8,128)S(1)}, f32[128,128]{1,0:T(8,128)S(1)}, u32[]{:S(2)}, u32[]{:S(2)}) collective-permute-start(f32[128,128]{1,0:T(8,128)S(1)} %add_add_fusion), channel_id=1, source_target_pairs={{0,24},{1,25},{2,26},{3,27},{4,28},{5,29},{6,30},{7,31},{8,16},{9,... | collective-permute-start | bytes 196616 | tf_op jit(solution)/shard_map/ppermute | solution.py:20
  79.8 5.8 %collective-permute-start.25 = (f32[128,128]{1,0:T(8,128)S(1)}, f32[128,128]{1,0:T(8,128)S(1)}, u32[]{:S(2)}, u32[]{:S(2)}) collective-permute-start(f32[128,128]{1,0:T(8,128)S(1)} %add_add_fusion), channel_id=1, source_target_pairs={{0,16},{1,17},{2,18},{3,19},{4,20},{5,21},{6,22},{7,23},{8,24},{9,... | collective-permute-start | bytes 196616 | tf_op jit(solution)/shard_map/ppermute | solution.py:20
  79.8 5.8 %collective-permute-start.24 = (f32[128,128]{1,0:T(8,128)S(1)}, f32[128,128]{1,0:T(8,128)S(1)}, u32[]{:S(2)}, u32[]{:S(2)}) collective-permute-start(f32[128,128]{1,0:T(8,128)S(1)} %add_add_fusion), channel_id=1, source_target_pairs={{0,8},{1,9},{2,10},{3,11},{4,12},{5,13},{6,14},{7,15},{8,0},{9,1},... | collective-permute-start | bytes 196616 | tf_op jit(solution)/shard_map/ppermute | solution.py:20

commit v6 on v5

--- a/solution.py
+++ b/solution.py
@@ -145,7 +145,7 @@
     )(*scalars, *arrays, *after)
 
 
-def gram_kernel(ry_ref, list_ref, *refs):
+def gram_kernel(ry_ref, live_ref, *refs):
     *part_refs, sketch_ref, on_ref, mine_ref, next_ref, rows_ref, blocks_ref = refs
     slots, cols = rows_ref.shape[0] // 2, rows_ref.shape[1]
     start = 0
@@ -153,7 +153,7 @@
         rows_ref[start:start + near_ref.shape[0], :] = near_ref[...] + add_ref[...]
         start += near_ref.shape[0]
     values = jnp.concatenate([rows_ref[pl.ds(half, slots, stride=2), :] for half in range(2)], axis=1)
-    live = lax.broadcasted_iota(jnp.int32, values.shape, 0) < list_ref[slots]
+    live = lax.broadcasted_iota(jnp.int32, values.shape, 0) < live_ref[0]
     values = jnp.where(live, values, 0.0)
     sketch_ref[...] = values
     high = values.astype(jnp.bfloat16)
@@ -178,9 +178,9 @@
     rows, width = matrix.shape
     slots = indices.shape[0]
     cols = width // 2
-    tail = slots // 4
+    tail = slots // 32 * 9
     head = slots - tail
-    first = slots // 8 * 3
+    first = head // 2
     size_x = lax.axis_size("rx")
     size_y = lax.axis_size("ry")
     size = size_x * size_y
@@ -259,7 +259,7 @@
     sketch, on, block, far_block = call(
         gram_kernel,
         "gram",
-        (ry.astype(jnp.int32).reshape(1), lists[0]),
+        (ry.astype(jnp.int32).reshape(1), counts),
         (*finals, end, end_add),
         (floats(slots, width), floats(2 * cols, cols), floats(cols, cols), floats(cols, cols)),
         scratch=[pltpu.VMEM((2 * slots, cols), jnp.float32), pltpu.VMEM((4, cols, cols), jnp.float32)],

time: 86.6 us -> 87.1 us (level)
  waiting for transfers between devices: 34.5 us -> 32.1 us
  starting transfers between devices: 36 us -> 37.9 us
    ppermute x27, waiting for transfers between devices: 34.5 us -> 32.1 us  [swap(): return lax.ppermute(value, MESH_AXES, [(i, i ^ bits) for i in range(size)])]
    ppermute x27, starting transfers between devices: 36 us -> 37.9 us  [swap(): return lax.ppermute(value, MESH_AXES, [(i, i ^ bits) for i in range(size)])]
  transfers between devices with their start and end apart: 27 -> 27, of which waited for: 16 -> 16; matrix products, arithmetic and copies ran while one was open for 1% -> 1% of each run, Pallas kernels for 9% -> 10%
where the time goes in v6:
time: 87.1 us; the launch traced here: 86.2 us
  starting transfers between devices  37.9 us (44%)
  waiting for transfers between devices  32.1 us (37%)
  Pallas kernels  12.9 us (15%)
  other arithmetic  1.85 us (2%)
  between operations  1.4 us (2%)
    ppermute x27, starting transfers between devices, swap(): return lax.ppermute(value, MESH_AXES, [(i, i ^ bits) for i in range(size)])  37.9 us
    ppermute x27, waiting for transfers between devices, swap(): return lax.ppermute(value, MESH_AXES, [(i, i ^ bits) for i in range(size)])  32.1 us
    pallas_call x5, Pallas kernels, call(): pl.pallas_call(kernel, in_specs=specs(len(scalars), len(arrays)) + [pl.Bl...  8.5 us
    pallas_call x1, Pallas kernels, transform(): pl.pallas_call(functools.partial(transform_kernel, full, chunks), in_spec...  4.4 us
  transfers between devices with their start and end apart: 27, of which 16 were waited for; matrix products, arithmetic and copies ran while one was open for 1% of the time, Pallas kernels for 10%

profile of v6, /device:TPU:0, one launch (start us, length us, event | category | flops | bytes accessed | tf_op | source)
XLA Modules:
  0.0 86.2 jit_solution(16575675892719090672)
XLA Ops:
  0.6 0.5 collective-permute-start.7
  1.8 0.7 fusion.1.signs_ref
  2.5 0.1 collective-permute-start.6
  2.6 5.0 %collective-permute-start.2 = (s32[3,128]{1,0:T(4,128)S(1)}, s32[3,128]{1,0:T(4,128)S(1)}, u32[]{:S(2)}, u32[]{:S(2)}) collective-permute-start(s32[3,128]{1,0:T(4,128)S(1)} %slice.132.refs_0_), channel_id=1, source_target_pairs={{0,24},{1,25},{2,26},{3,27},{4,28},{5,29},{6,30},{7,31},{8,16},{9,... | collective-permute-start | bytes 4616 | tf_op jit(solution)/shard_map/ppermute | solution.py:20
  7.6 0.0 collective-permute-start.1
  7.6 0.6 collective-permute-start
  8.2 1.0 %collective-permute-done.2.refs_3_ = s32[3,128]{1,0:T(4,128)S(1)} collective-permute-done((s32[3,128]{1,0:T(4,128)S(1)}, s32[3,128]{1,0:T(4,128)S(1)}, u32[]{:S(2)}, u32[]{:S(2)}) %collective-permute-start.2) | collective-permute-done | bytes 1568 | tf_op jit(solution)/shard_map/ppermute | solution.py:20
  9.2 2.9 %collective-permute-done.1.refs_2_ = s32[3,128]{1,0:T(4,128)S(1)} collective-permute-done((s32[3,128]{1,0:T(4,128)S(1)}, s32[3,128]{1,0:T(4,128)S(1)}, u32[]{:S(2)}, u32[]{:S(2)}) %collective-permute-start.1) | collective-permute-done | bytes 1568 | tf_op jit(solution)/shard_map/ppermute | solution.py:20
  12.1 0.0 collective-permute-done.refs_1_
  12.1 2.4 %collective-permute-start.5 = (s32[12,128]{1,0:T(8,128)S(1)}, s32[12,128]{1,0:T(8,128)S(1)}, u32[]{:S(2)}, u32[]{:S(2)}) collective-permute-start(s32[12,128]{1,0:T(8,128)S(1)} %join.1), channel_id=1, source_target_pairs={{0,6},{1,7},{2,4},{3,5},{4,2},{5,3},{6,0},{7,1},{8,14},{9,15},{10,... | collective-permute-start | bytes 18440 | tf_op jit(solution)/shard_map/ppermute | solution.py:20
  14.6 0.5 collective-permute-start.4
  15.1 0.5 collective-permute-start.3
  15.6 0.0 collective-permute-done.6.other_signs_ref
  15.6 0.0 collective-permute-done.7.refs_1_
  15.6 4.4 %transform.1 = f32[8192,128]{1,0:T(8,128)S(1)} custom-call(s32[1]{0:T(128)} %bitcast.1.me_ref, s32[35,128]{1,0:T(8,128)S(1)} %fusion.1.signs_ref, s32[35,128]{1,0:T(8,128)S(1)} %collective-permute-done.6.other_signs_ref, f32[4096,256]{1,0:T(8,128)} %refs_0_.1, f32[4096,256]{1,0:T(8,128)} %collective-permute-done.7.refs_1_), custom_call_target="tpu_custom_call" | custom-call | flops 2147483648 | bytes 12582912 | tf_op jit(solution)/shard_map/transform/pallas_call | solution.py:91
  20.0 0.0 collective-permute-done.5
  20.0 0.0 collective-permute-done.4
  20.1 0.0 collective-permute-done.3
  20.1 3.5 %gather_far.1 = (f32[736,2,128]{2,1,0:T(2,128)S(1)}, f32[736,2,128]{2,1,0:T(2,128)S(1)}, f32[576,2,128]{2,1,0:T(2,128)S(1)}) custom-call(s32[1]{0:T(128)} %bitcast.1.me_ref, s32[1536]{0:T(1024)S(1)} %bitcast.31, s32[1536]{0:T(1024)S(1)} %bitcast.40, s32[1536]{0:T(1024)S(1)} %bitcast.37, s32[1536]{0:T(1024)S(1)} %bitcast.34, f32[4096,2,128]{2,1,0:T(2,128)S(1)} %bitcast.20), custom_call_target="tpu_custom_call" | custom-call | bytes 6291456 | tf_op jit(solution)/shard_map/gather_far/pallas_call | solution.py:136
  23.6 0.1 collective-permute-start.16
  23.7 1.6 %collective-permute-start.8 = (f32[1472,128]{1,0:T(8,128)S(1)}, f32[1472,128]{1,0:T(8,128)S(1)}, u32[]{:S(2)}, u32[]{:S(2)}) collective-permute-start(f32[1472,128]{1,0:T(8,128)S(1)} %bitcast.44), channel_id=1, source_target_pairs={{0,2},{1,3},{2,0},{3,1},{4,6},{5,7},{6,4},{7,5},{8,10},{9,11},{10,... | collective-permute-start | bytes 2261000 | tf_op jit(solution)/shard_map/ppermute | solution.py:20
  25.2 1.5 %collective-permute-start.12 = (f32[1472,128]{1,0:T(8,128)S(1)}, f32[1472,128]{1,0:T(8,128)S(1)}, u32[]{:S(2)}, u32[]{:S(2)}) collective-permute-start(f32[1472,128]{1,0:T(8,128)S(1)} %bitcast.43), channel_id=1, source_target_pairs={{0,4},{1,5},{2,6},{3,7},{4,0},{5,1},{6,2},{7,3},{8,12},{9,13},{10,... | collective-permute-start | bytes 2261000 | tf_op jit(solution)/shard_map/ppermute | solution.py:20
  26.7 1.3 %gather_end.1 = (f32[288,2,128]{2,1,0:T(2,128)S(1)}, f32[288,2,128]{2,1,0:T(2,128)S(1)}) custom-call(s32[1]{0:T(128)} %bitcast.1.me_ref, s32[1536]{0:T(1024)S(1)} %bitcast.32, s32[1536]{0:T(1024)S(1)} %bitcast.41, s32[1536]{0:T(1024)S(1)} %bitcast.38, s32[1536]{0:T(1024)S(1)} %bitcast.35, f32[4096,2,128]{2,1,0:T(2,128)S(1)} %bitcast.21), custom_call_target="tpu_custom_call" | custom-call | bytes 4784128 | tf_op jit(solution)/shard_map/gather_end/pallas_call | solution.py:136
  28.0 2.9 %gather_near.1 = (f32[368,2,128]{2,1,0:T(2,128)S(1)}, f32[368,2,128]{2,1,0:T(2,128)S(1)}, f32[368,2,128]{2,1,0:T(2,128)S(1)}, f32[368,2,128]{2,1,0:T(2,128)S(1)}) custom-call(s32[1]{0:T(128)} %bitcast.1.me_ref, s32[1536]{0:T(1024)S(1)} %bitcast.33, s32[1536]{0:T(1024)S(1)} %bitcast.42, s32[1536]{0:T(1024)S(1)} %bitcast.39, s32[1536]{0:T(1024)S(1)} %bitcast.36, ...), custom_call_target="tpu_custom_call" | custom-call | bytes 5701632 | tf_op jit(solution)/shard_map/gather_near/pallas_call | solution.py:136
  30.9 5.3 %collective-permute-done.16 = f32[1152,128]{1,0:T(8,128)S(1)} collective-permute-done((f32[1152,128]{1,0:T(8,128)S(1)}, f32[1152,128]{1,0:T(8,128)S(1)}, u32[]{:S(2)}, u32[]{:S(2)}) %collective-permute-start.16) | collective-permute-done | bytes 589856 | tf_op jit(solution)/shard_map/ppermute | solution.py:20
  36.2 0.1 slice_add_fusion.5
  36.3 2.8 %collective-permute-start.17 = (f32[576,128]{1,0:T(8,128)S(1)}, f32[576,128]{1,0:T(8,128)S(1)}, u32[]{:S(2)}, u32[]{:S(2)}) collective-permute-start(f32[576,128]{1,0:T(8,128)S(1)} %get-tuple-element.39), channel_id=1, source_target_pairs={{0,16},{1,17},{2,18},{3,19},{4,20},{5,21},{6,22},{7,23},{8,24},{9,... | collective-permute-start | bytes 884744 | tf_op jit(solution)/shard_map/ppermute | solution.py:20
  39.2 0.5 collective-permute-done.8
  39.7 0.1 slice_add_fusion.3
  39.7 2.0 %collective-permute-start.9 = (f32[736,128]{1,0:T(8,128)S(1)}, f32[736,128]{1,0:T(8,128)S(1)}, u32[]{:S(2)}, u32[]{:S(2)}) collective-permute-start(f32[736,128]{1,0:T(8,128)S(1)} %get-tuple-element.35), channel_id=1, source_target_pairs={{0,4},{1,5},{2,6},{3,7},{4,0},{5,1},{6,2},{7,3},{8,12},{9,13},{10,... | collective-permute-start | bytes 1130504 | tf_op jit(solution)/shard_map/ppermute | solution.py:20
  41.7 1.1 %collective-permute-done.12 = f32[1472,128]{1,0:T(8,128)S(1)} collective-permute-done((f32[1472,128]{1,0:T(8,128)S(1)}, f32[1472,128]{1,0:T(8,128)S(1)}, u32[]{:S(2)}, u32[]{:S(2)}) %collective-permute-start.12) | collective-permute-done | bytes 753696 | tf_op jit(solution)/shard_map/ppermute | solution.py:20
  42.8 0.1 slice_add_fusion.1
  42.8 0.9 collective-permute-start.13
  43.7 4.9 %collective-permute-done.17 = f32[576,128]{1,0:T(8,128)S(1)} collective-permute-done((f32[576,128]{1,0:T(8,128)S(1)}, f32[576,128]{1,0:T(8,128)S(1)}, u32[]{:S(2)}, u32[]{:S(2)}) %collective-permute-start.17) | collective-permute-done | bytes 294944 | tf_op jit(solution)/shard_map/ppermute | solution.py:20
  48.6 1.5 %collective-permute-start.18 = (f32[288,128]{1,0:T(8,128)S(1)}, f32[288,128]{1,0:T(8,128)S(1)}, u32[]{:S(2)}, u32[]{:S(2)}) collective-permute-start(f32[288,128]{1,0:T(8,128)S(1)} %get-tuple-element.37), channel_id=1, source_target_pairs={{0,2},{1,3},{2,0},{3,1},{4,6},{5,7},{6,4},{7,5},{8,10},{9,11},{10,... | collective-permute-start | bytes 442376 | tf_op jit(solution)/shard_map/ppermute | solution.py:20
  50.2 0.0 collective-permute-done.9
  50.2 0.1 slice_add_fusion.9
  50.2 0.7 collective-permute-start.10
  50.9 0.1 collective-permute-done.13
  51.0 3.1 %collective-permute-start.14 = (f32[368,128]{1,0:T(8,128)S(1)}, f32[368,128]{1,0:T(8,128)S(1)}, u32[]{:S(2)}, u32[]{:S(2)}) collective-permute-start(f32[368,128]{1,0:T(8,128)S(1)} %get-tuple-element.29), channel_id=1, source_target_pairs={{0,8},{1,9},{2,10},{3,11},{4,12},{5,13},{6,14},{7,15},{8,0},{9,1},... | collective-permute-start | bytes 565256 | tf_op jit(solution)/shard_map/ppermute | solution.py:20
  54.1 3.5 %collective-permute-done.10 = f32[368,128]{1,0:T(8,128)S(1)} collective-permute-done((f32[368,128]{1,0:T(8,128)S(1)}, f32[368,128]{1,0:T(8,128)S(1)}, u32[]{:S(2)}, u32[]{:S(2)}) %collective-permute-start.10) | collective-permute-done | bytes 188448 | tf_op jit(solution)/shard_map/ppermute | solution.py:20
  57.7 1.3 %collective-permute-start.11 = (f32[184,128]{1,0:T(8,128)S(1)}, f32[184,128]{1,0:T(8,128)S(1)}, u32[]{:S(2)}, u32[]{:S(2)}) collective-permute-start(f32[184,128]{1,0:T(8,128)S(1)} %get-tuple-element.42), channel_id=1, source_target_pairs={{0,16},{1,17},{2,18},{3,19},{4,20},{5,21},{6,22},{7,23},{8,24},{9,... | collective-permute-start | bytes 282632 | tf_op jit(solution)/shard_map/ppermute | solution.py:20
  58.9 1.4 %collective-permute-done.14 = f32[368,128]{1,0:T(8,128)S(1)} collective-permute-done((f32[368,128]{1,0:T(8,128)S(1)}, f32[368,128]{1,0:T(8,128)S(1)}, u32[]{:S(2)}, u32[]{:S(2)}) %collective-permute-start.14) | collective-permute-done | bytes 188448 | tf_op jit(solution)/shard_map/ppermute | solution.py:20
  60.4 1.6 %collective-permute-start.15 = (f32[184,128]{1,0:T(8,128)S(1)}, f32[184,128]{1,0:T(8,128)S(1)}, u32[]{:S(2)}, u32[]{:S(2)}) collective-permute-start(f32[184,128]{1,0:T(8,128)S(1)} %get-tuple-element.40), channel_id=1, source_target_pairs={{0,16},{1,17},{2,18},{3,19},{4,20},{5,21},{6,22},{7,23},{8,24},{9,... | collective-permute-start | bytes 282632 | tf_op jit(solution)/shard_map/ppermute | solution.py:20
  62.0 0.0 collective-permute-done.18
  62.0 2.3 %collective-permute-start.19 = (f32[144,128]{1,0:T(8,128)S(1)}, f32[144,128]{1,0:T(8,128)S(1)}, u32[]{:S(2)}, u32[]{:S(2)}) collective-permute-start(f32[144,128]{1,0:T(8,128)S(1)} %get-tuple-element.44), channel_id=1, source_target_pairs={{0,4},{1,5},{2,6},{3,7},{4,0},{5,1},{6,2},{7,3},{8,12},{9,13},{10,... | collective-permute-start | bytes 221192 | tf_op jit(solution)/shard_map/ppermute | solution.py:20
  64.3 2.3 %collective-permute-done.19.refs_5_ = f32[144,128]{1,0:T(8,128)S(1)} collective-permute-done((f32[144,128]{1,0:T(8,128)S(1)}, f32[144,128]{1,0:T(8,128)S(1)}, u32[]{:S(2)}, u32[]{:S(2)}) %collective-permute-start.19) | collective-permute-done | bytes 73760 | tf_op jit(solution)/shard_map/ppermute | solution.py:20
  66.6 0.0 collective-permute-done.11.refs_1_
  66.6 0.3 collective-permute-done.15.refs_3_
  66.9 0.8 gram.1
  67.7 0.0 collective-permute-start.20
  67.7 1.3 %collective-permute-done.20 = f32[256,128]{1,0:T(8,128)S(1)} collective-permute-done((f32[256,128]{1,0:T(8,128)S(1)}, f32[256,128]{1,0:T(8,128)S(1)}, u32[]{:S(2)}, u32[]{:S(2)}) %collective-permute-start.20) | collective-permute-done | bytes 131104 | tf_op jit(solution)/shard_map/ppermute | solution.py:20
  69.1 3.0 %collective-permute-start.22 = (f32[128,128]{1,0:T(8,128)S(1)}, f32[128,128]{1,0:T(8,128)S(1)}, u32[]{:S(2)}, u32[]{:S(2)}) collective-permute-start(f32[128,128]{1,0:T(8,128)S(1)} %get-tuple-element.46), channel_id=1, source_target_pairs={{0,4},{1,5},{2,6},{3,7},{4,0},{5,1},{6,2},{7,3},{8,12},{9,13},{10,... | collective-permute-start | bytes 196616 | tf_op jit(solution)/shard_map/ppermute | solution.py:20
  72.0 0.0 collective-permute-start.23
  72.0 1.5 %collective-permute-start.21 = (f32[128,128]{1,0:T(8,128)S(1)}, f32[128,128]{1,0:T(8,128)S(1)}, u32[]{:S(2)}, u32[]{:S(2)}) collective-permute-start(f32[128,128]{1,0:T(8,128)S(1)} %get-tuple-element.47), channel_id=1, source_target_pairs={{0,2},{1,3},{2,0},{3,1},{4,6},{5,7},{6,4},{7,5},{8,10},{9,11},{10,... | collective-permute-start | bytes 196616 | tf_op jit(solution)/shard_map/ppermute | solution.py:20
  73.6 1.3 %collective-permute-done.22 = f32[128,128]{1,0:T(8,128)S(1)} collective-permute-done((f32[128,128]{1,0:T(8,128)S(1)}, f32[128,128]{1,0:T(8,128)S(1)}, u32[]{:S(2)}, u32[]{:S(2)}) %collective-permute-start.22) | collective-permute-done | bytes 65568 | tf_op jit(solution)/shard_map/ppermute | solution.py:20
  74.8 2.7 %collective-permute-done.23 = f32[128,128]{1,0:T(8,128)S(1)} collective-permute-done((f32[128,128]{1,0:T(8,128)S(1)}, f32[128,128]{1,0:T(8,128)S(1)}, u32[]{:S(2)}, u32[]{:S(2)}) %collective-permute-start.23) | collective-permute-done | bytes 65568 | tf_op jit(solution)/shard_map/ppermute | solution.py:20
  77.5 0.0 collective-permute-done.21
  77.5 2.2 %collective-permute-start.26 = (f32[128,128]{1,0:T(8,128)S(1)}, f32[128,128]{1,0:T(8,128)S(1)}, u32[]{:S(2)}, u32[]{:S(2)}) collective-permute-start(f32[128,128]{1,0:T(8,128)S(1)} %add_add_fusion), channel_id=1, source_target_pairs={{0,24},{1,25},{2,26},{3,27},{4,28},{5,29},{6,30},{7,31},{8,16},{9,... | collective-permute-start | bytes 196616 | tf_op jit(solution)/shard_map/ppermute | solution.py:20
  79.7 2.3 %collective-permute-start.24 = (f32[128,128]{1,0:T(8,128)S(1)}, f32[128,128]{1,0:T(8,128)S(1)}, u32[]{:S(2)}, u32[]{:S(2)}) collective-permute-start(f32[128,128]{1,0:T(8,128)S(1)} %add_add_fusion), channel_id=1, source_target_pairs={{0,8},{1,9},{2,10},{3,11},{4,12},{5,13},{6,14},{7,15},{8,0},{9,1},... | collective-permute-start | bytes 196616 | tf_op jit(solution)/shard_map/ppermute | solution.py:20
  82.0 2.2 %collective-permute-done.26 = f32[128,128]{1,0:T(8,128)S(1)} collective-permute-done((f32[128,128]{1,0:T(8,128)S(1)}, f32[128,128]{1,0:T(8,128)S(1)}, u32[]{:S(2)}, u32[]{:S(2)}) %collective-permute-start.26) | collective-permute-done | bytes 65568 | tf_op jit(solution)/shard_map/ppermute | solution.py:20
  84.2 1.4 %collective-permute-done.25 = f32[128,128]{1,0:T(8,128)S(1)} collective-permute-done((f32[128,128]{1,0:T(8,128)S(1)}, f32[128,128]{1,0:T(8,128)S(1)}, u32[]{:S(2)}, u32[]{:S(2)}) %collective-permute-start.25) | collective-permute-done | bytes 65568 | tf_op jit(solution)/shard_map/ppermute | solution.py:20
  85.5 0.0 collective-permute-done.24
  85.5 0.6 multiply_bitcast_fusion
  (10 shorter events, 0.2 us)
Async XLA Ops:
  0.6 15.0 %collective-permute-start.7 = (f32[4096,256]{1,0:T(8,128)}, f32[4096,256]{1,0:T(8,128)}, u32[]{:S(2)}, u32[]{:S(2)}) collective-permute-start(f32[4096,256]{1,0:T(8,128)} %refs_0_.1), channel_id=1, source_target_pairs={{0,1},{1,0},{2,3},{3,2},{4,5},{5,4},{6,7},{7,6},{8,9},{9,8},{10,11... | collective-permute-start | bytes 12582920 | tf_op jit(solution)/shard_map/ppermute | solution.py:20
  2.5 13.1 %collective-permute-start.6 = (s32[35,128]{1,0:T(8,128)S(1)}, s32[35,128]{1,0:T(8,128)S(1)}, u32[]{:S(2)}, u32[]{:S(2)}) collective-permute-start(s32[35,128]{1,0:T(8,128)S(1)} %fusion.1.signs_ref), channel_id=1, source_target_pairs={{0,1},{1,0},{2,3},{3,2},{4,5},{5,4},{6,7},{7,6},{8,9},{9,8},{10,11... | collective-permute-start | bytes 53768 | tf_op jit(solution)/shard_map/ppermute | solution.py:20
  2.6 6.6 %collective-permute-start.2 = (s32[3,128]{1,0:T(4,128)S(1)}, s32[3,128]{1,0:T(4,128)S(1)}, u32[]{:S(2)}, u32[]{:S(2)}) collective-permute-start(s32[3,128]{1,0:T(4,128)S(1)} %slice.132.refs_0_), channel_id=1, source_target_pairs={{0,24},{1,25},{2,26},{3,27},{4,28},{5,29},{6,30},{7,31},{8,16},{9,... | collective-permute-start | bytes 4616 | tf_op jit(solution)/shard_map/ppermute | solution.py:20
  7.6 4.5 %collective-permute-start.1 = (s32[3,128]{1,0:T(4,128)S(1)}, s32[3,128]{1,0:T(4,128)S(1)}, u32[]{:S(2)}, u32[]{:S(2)}) collective-permute-start(s32[3,128]{1,0:T(4,128)S(1)} %slice.132.refs_0_), channel_id=1, source_target_pairs={{0,16},{1,17},{2,18},{3,19},{4,20},{5,21},{6,22},{7,23},{8,24},{9,... | collective-permute-start | bytes 4616 | tf_op jit(solution)/shard_map/ppermute | solution.py:20
  7.6 4.5 %collective-permute-start = (s32[3,128]{1,0:T(4,128)S(1)}, s32[3,128]{1,0:T(4,128)S(1)}, u32[]{:S(2)}, u32[]{:S(2)}) collective-permute-start(s32[3,128]{1,0:T(4,128)S(1)} %slice.132.refs_0_), channel_id=1, source_target_pairs={{0,8},{1,9},{2,10},{3,11},{4,12},{5,13},{6,14},{7,15},{8,0},{9,1},... | collective-permute-start | bytes 4616 | tf_op jit(solution)/shard_map/ppermute | solution.py:20
  12.1 7.9 %collective-permute-start.5 = (s32[12,128]{1,0:T(8,128)S(1)}, s32[12,128]{1,0:T(8,128)S(1)}, u32[]{:S(2)}, u32[]{:S(2)}) collective-permute-start(s32[12,128]{1,0:T(8,128)S(1)} %join.1), channel_id=1, source_target_pairs={{0,6},{1,7},{2,4},{3,5},{4,2},{5,3},{6,0},{7,1},{8,14},{9,15},{10,... | collective-permute-start | bytes 18440 | tf_op jit(solution)/shard_map/ppermute | solution.py:20
  14.6 5.5 %collective-permute-start.4 = (s32[12,128]{1,0:T(8,128)S(1)}, s32[12,128]{1,0:T(8,128)S(1)}, u32[]{:S(2)}, u32[]{:S(2)}) collective-permute-start(s32[12,128]{1,0:T(8,128)S(1)} %join.1), channel_id=1, source_target_pairs={{0,4},{1,5},{2,6},{3,7},{4,0},{5,1},{6,2},{7,3},{8,12},{9,13},{10,... | collective-permute-start | bytes 18440 | tf_op jit(solution)/shard_map/ppermute | solution.py:20
  15.1 5.0 %collective-permute-start.3 = (s32[12,128]{1,0:T(8,128)S(1)}, s32[12,128]{1,0:T(8,128)S(1)}, u32[]{:S(2)}, u32[]{:S(2)}) collective-permute-start(s32[12,128]{1,0:T(8,128)S(1)} %join.1), channel_id=1, source_target_pairs={{0,2},{1,3},{2,0},{3,1},{4,6},{5,7},{6,4},{7,5},{8,10},{9,11},{10,... | collective-permute-start | bytes 18440 | tf_op jit(solution)/shard_map/ppermute | solution.py:20
  23.6 12.7 %collective-permute-start.16 = (f32[1152,128]{1,0:T(8,128)S(1)}, f32[1152,128]{1,0:T(8,128)S(1)}, u32[]{:S(2)}, u32[]{:S(2)}) collective-permute-start(f32[1152,128]{1,0:T(8,128)S(1)} %bitcast.23), channel_id=1, source_target_pairs={{0,8},{1,9},{2,10},{3,11},{4,12},{5,13},{6,14},{7,15},{8,0},{9,1},... | collective-permute-start | bytes 1769480 | tf_op jit(solution)/shard_map/ppermute | solution.py:20
  23.7 16.0 %collective-permute-start.8 = (f32[1472,128]{1,0:T(8,128)S(1)}, f32[1472,128]{1,0:T(8,128)S(1)}, u32[]{:S(2)}, u32[]{:S(2)}) collective-permute-start(f32[1472,128]{1,0:T(8,128)S(1)} %bitcast.44), channel_id=1, source_target_pairs={{0,2},{1,3},{2,0},{3,1},{4,6},{5,7},{6,4},{7,5},{8,10},{9,11},{10,... | collective-permute-start | bytes 2261000 | tf_op jit(solution)/shard_map/ppermute | solution.py:20
  25.2 17.5 %collective-permute-start.12 = (f32[1472,128]{1,0:T(8,128)S(1)}, f32[1472,128]{1,0:T(8,128)S(1)}, u32[]{:S(2)}, u32[]{:S(2)}) collective-permute-start(f32[1472,128]{1,0:T(8,128)S(1)} %bitcast.43), channel_id=1, source_target_pairs={{0,4},{1,5},{2,6},{3,7},{4,0},{5,1},{6,2},{7,3},{8,12},{9,13},{10,... | collective-permute-start | bytes 2261000 | tf_op jit(solution)/shard_map/ppermute | solution.py:20
  36.3 12.3 %collective-permute-start.17 = (f32[576,128]{1,0:T(8,128)S(1)}, f32[576,128]{1,0:T(8,128)S(1)}, u32[]{:S(2)}, u32[]{:S(2)}) collective-permute-start(f32[576,128]{1,0:T(8,128)S(1)} %get-tuple-element.39), channel_id=1, source_target_pairs={{0,16},{1,17},{2,18},{3,19},{4,20},{5,21},{6,22},{7,23},{8,24},{9,... | collective-permute-start | bytes 884744 | tf_op jit(solution)/shard_map/ppermute | solution.py:20
  39.7 10.5 %collective-permute-start.9 = (f32[736,128]{1,0:T(8,128)S(1)}, f32[736,128]{1,0:T(8,128)S(1)}, u32[]{:S(2)}, u32[]{:S(2)}) collective-permute-start(f32[736,128]{1,0:T(8,128)S(1)} %get-tuple-element.35), channel_id=1, source_target_pairs={{0,4},{1,5},{2,6},{3,7},{4,0},{5,1},{6,2},{7,3},{8,12},{9,13},{10,... | collective-permute-start | bytes 1130504 | tf_op jit(solution)/shard_map/ppermute | solution.py:20
  42.8 8.2 %collective-permute-start.13 = (f32[736,128]{1,0:T(8,128)S(1)}, f32[736,128]{1,0:T(8,128)S(1)}, u32[]{:S(2)}, u32[]{:S(2)}) collective-permute-start(f32[736,128]{1,0:T(8,128)S(1)} %get-tuple-element.31), channel_id=1, source_target_pairs={{0,2},{1,3},{2,0},{3,1},{4,6},{5,7},{6,4},{7,5},{8,10},{9,11},{10,... | collective-permute-start | bytes 1130504 | tf_op jit(solution)/shard_map/ppermute | solution.py:20
  48.6 13.4 %collective-permute-start.18 = (f32[288,128]{1,0:T(8,128)S(1)}, f32[288,128]{1,0:T(8,128)S(1)}, u32[]{:S(2)}, u32[]{:S(2)}) collective-permute-start(f32[288,128]{1,0:T(8,128)S(1)} %get-tuple-element.37), channel_id=1, source_target_pairs={{0,2},{1,3},{2,0},{3,1},{4,6},{5,7},{6,4},{7,5},{8,10},{9,11},{10,... | collective-permute-start | bytes 442376 | tf_op jit(solution)/shard_map/ppermute | solution.py:20
  50.2 7.4 %collective-permute-start.10 = (f32[368,128]{1,0:T(8,128)S(1)}, f32[368,128]{1,0:T(8,128)S(1)}, u32[]{:S(2)}, u32[]{:S(2)}) collective-permute-start(f32[368,128]{1,0:T(8,128)S(1)} %get-tuple-element.33), channel_id=1, source_target_pairs={{0,8},{1,9},{2,10},{3,11},{4,12},{5,13},{6,14},{7,15},{8,0},{9,1},... | collective-permute-start | bytes 565256 | tf_op jit(solution)/shard_map/ppermute | solution.py:20
  51.0 9.3 %collective-permute-start.14 = (f32[368,128]{1,0:T(8,128)S(1)}, f32[368,128]{1,0:T(8,128)S(1)}, u32[]{:S(2)}, u32[]{:S(2)}) collective-permute-start(f32[368,128]{1,0:T(8,128)S(1)} %get-tuple-element.29), channel_id=1, source_target_pairs={{0,8},{1,9},{2,10},{3,11},{4,12},{5,13},{6,14},{7,15},{8,0},{9,1},... | collective-permute-start | bytes 565256 | tf_op jit(solution)/shard_map/ppermute | solution.py:20
  57.7 9.0 %collective-permute-start.11 = (f32[184,128]{1,0:T(8,128)S(1)}, f32[184,128]{1,0:T(8,128)S(1)}, u32[]{:S(2)}, u32[]{:S(2)}) collective-permute-start(f32[184,128]{1,0:T(8,128)S(1)} %get-tuple-element.42), channel_id=1, source_target_pairs={{0,16},{1,17},{2,18},{3,19},{4,20},{5,21},{6,22},{7,23},{8,24},{9,... | collective-permute-start | bytes 282632 | tf_op jit(solution)/shard_map/ppermute | solution.py:20
  60.4 6.5 %collective-permute-start.15 = (f32[184,128]{1,0:T(8,128)S(1)}, f32[184,128]{1,0:T(8,128)S(1)}, u32[]{:S(2)}, u32[]{:S(2)}) collective-permute-start(f32[184,128]{1,0:T(8,128)S(1)} %get-tuple-element.40), channel_id=1, source_target_pairs={{0,16},{1,17},{2,18},{3,19},{4,20},{5,21},{6,22},{7,23},{8,24},{9,... | collective-permute-start | bytes 282632 | tf_op jit(solution)/shard_map/ppermute | solution.py:20
  62.0 4.6 %collective-permute-start.19 = (f32[144,128]{1,0:T(8,128)S(1)}, f32[144,128]{1,0:T(8,128)S(1)}, u32[]{:S(2)}, u32[]{:S(2)}) collective-permute-start(f32[144,128]{1,0:T(8,128)S(1)} %get-tuple-element.44), channel_id=1, source_target_pairs={{0,4},{1,5},{2,6},{3,7},{4,0},{5,1},{6,2},{7,3},{8,12},{9,13},{10,... | collective-permute-start | bytes 221192 | tf_op jit(solution)/shard_map/ppermute | solution.py:20
  67.7 1.3 %collective-permute-start.20 = (f32[256,128]{1,0:T(8,128)S(1)}, f32[256,128]{1,0:T(8,128)S(1)}, u32[]{:S(2)}, u32[]{:S(2)}) collective-permute-start(f32[256,128]{1,0:T(8,128)S(1)} %get-tuple-element.26), channel_id=1, source_target_pairs={{0,1},{1,0},{2,3},{3,2},{4,5},{5,4},{6,7},{7,6},{8,9},{9,8},{10,11... | collective-permute-start | bytes 393224 | tf_op jit(solution)/shard_map/ppermute | solution.py:20
  69.1 5.7 %collective-permute-start.22 = (f32[128,128]{1,0:T(8,128)S(1)}, f32[128,128]{1,0:T(8,128)S(1)}, u32[]{:S(2)}, u32[]{:S(2)}) collective-permute-start(f32[128,128]{1,0:T(8,128)S(1)} %get-tuple-element.46), channel_id=1, source_target_pairs={{0,4},{1,5},{2,6},{3,7},{4,0},{5,1},{6,2},{7,3},{8,12},{9,13},{10,... | collective-permute-start | bytes 196616 | tf_op jit(solution)/shard_map/ppermute | solution.py:20
  72.0 5.5 %collective-permute-start.23 = (f32[128,128]{1,0:T(8,128)S(1)}, f32[128,128]{1,0:T(8,128)S(1)}, u32[]{:S(2)}, u32[]{:S(2)}) collective-permute-start(f32[128,128]{1,0:T(8,128)S(1)} %get-tuple-element.47), channel_id=1, source_target_pairs={{0,6},{1,7},{2,4},{3,5},{4,2},{5,3},{6,0},{7,1},{8,14},{9,15},{10,... | collective-permute-start | bytes 196616 | tf_op jit(solution)/shard_map/ppermute | solution.py:20
  72.0 5.5 %collective-permute-start.21 = (f32[128,128]{1,0:T(8,128)S(1)}, f32[128,128]{1,0:T(8,128)S(1)}, u32[]{:S(2)}, u32[]{:S(2)}) collective-permute-start(f32[128,128]{1,0:T(8,128)S(1)} %get-tuple-element.47), channel_id=1, source_target_pairs={{0,2},{1,3},{2,0},{3,1},{4,6},{5,7},{6,4},{7,5},{8,10},{9,11},{10,... | collective-permute-start | bytes 196616 | tf_op jit(solution)/shard_map/ppermute | solution.py:20
  77.5 6.6 %collective-permute-start.26 = (f32[128,128]{1,0:T(8,128)S(1)}, f32[128,128]{1,0:T(8,128)S(1)}, u32[]{:S(2)}, u32[]{:S(2)}) collective-permute-start(f32[128,128]{1,0:T(8,128)S(1)} %add_add_fusion), channel_id=1, source_target_pairs={{0,24},{1,25},{2,26},{3,27},{4,28},{5,29},{6,30},{7,31},{8,16},{9,... | collective-permute-start | bytes 196616 | tf_op jit(solution)/shard_map/ppermute | solution.py:20
  79.7 5.8 %collective-permute-start.25 = (f32[128,128]{1,0:T(8,128)S(1)}, f32[128,128]{1,0:T(8,128)S(1)}, u32[]{:S(2)}, u32[]{:S(2)}) collective-permute-start(f32[128,128]{1,0:T(8,128)S(1)} %add_add_fusion), channel_id=1, source_target_pairs={{0,16},{1,17},{2,18},{3,19},{4,20},{5,21},{6,22},{7,23},{8,24},{9,... | collective-permute-start | bytes 196616 | tf_op jit(solution)/shard_map/ppermute | solution.py:20
  79.7 5.8 %collective-permute-start.24 = (f32[128,128]{1,0:T(8,128)S(1)}, f32[128,128]{1,0:T(8,128)S(1)}, u32[]{:S(2)}, u32[]{:S(2)}) collective-permute-start(f32[128,128]{1,0:T(8,128)S(1)} %add_add_fusion), channel_id=1, source_target_pairs={{0,8},{1,9},{2,10},{3,11},{4,12},{5,13},{6,14},{7,15},{8,0},{9,1},... | collective-permute-start | bytes 196616 | tf_op jit(solution)/shard_map/ppermute | solution.py:20

commit v7 on v6

--- a/solution.py
+++ b/solution.py
@@ -178,7 +178,7 @@
     rows, width = matrix.shape
     slots = indices.shape[0]
     cols = width // 2
-    tail = slots // 32 * 9
+    tail = slots // 4
     head = slots - tail
     first = head // 2
     size_x = lax.axis_size("rx")

time: 87.1 us -> 85.7 us (0.984)
  starting transfers between devices: 37.9 us -> 35.6 us
  waiting for transfers between devices: 32.1 us -> 33.9 us
    ppermute x27, starting transfers between devices: 37.9 us -> 35.6 us  [swap(): return lax.ppermute(value, MESH_AXES, [(i, i ^ bits) for i in range(size)])]
    ppermute x27, waiting for transfers between devices: 32.1 us -> 33.9 us  [swap(): return lax.ppermute(value, MESH_AXES, [(i, i ^ bits) for i in range(size)])]
where the time goes in v7:
time: 85.7 us; the launch traced here: 85.3 us
  starting transfers between devices  35.6 us (42%)
  waiting for transfers between devices  33.9 us (40%)
  Pallas kernels  12.6 us (15%)
  other arithmetic  1.83 us (2%)
  between operations  1.4 us (2%)
    ppermute x27, starting transfers between devices, swap(): return lax.ppermute(value, MESH_AXES, [(i, i ^ bits) for i in range(size)])  35.6 us
    ppermute x27, waiting for transfers between devices, swap(): return lax.ppermute(value, MESH_AXES, [(i, i ^ bits) for i in range(size)])  33.9 us
    pallas_call x5, Pallas kernels, call(): pl.pallas_call(kernel, in_specs=specs(len(scalars), len(arrays)) + [pl.Bl...  8.15 us
    pallas_call x1, Pallas kernels, transform(): pl.pallas_call(functools.partial(transform_kernel, full, chunks), in_spec...  4.4 us
  transfers between devices with their start and end apart: 27, of which 16 were waited for; matrix products, arithmetic and copies ran while one was open for 1% of the time, Pallas kernels for 10%

profile of v7, /device:TPU:0, one launch (start us, length us, event | category | flops | bytes accessed | tf_op | source)
XLA Modules:
  0.0 85.3 jit_solution(18250982962362996619)
XLA Ops:
  0.6 0.5 collective-permute-start.7
  1.8 0.7 fusion.1.signs_ref
  2.5 0.1 collective-permute-start.6
  2.6 5.0 %collective-permute-start.2 = (s32[3,128]{1,0:T(4,128)S(1)}, s32[3,128]{1,0:T(4,128)S(1)}, u32[]{:S(2)}, u32[]{:S(2)}) collective-permute-start(s32[3,128]{1,0:T(4,128)S(1)} %slice.132.refs_0_), channel_id=1, source_target_pairs={{0,24},{1,25},{2,26},{3,27},{4,28},{5,29},{6,30},{7,31},{8,16},{9,... | collective-permute-start | bytes 4616 | tf_op jit(solution)/shard_map/ppermute | solution.py:20
  7.6 0.0 collective-permute-start.1
  7.6 0.6 collective-permute-start
  8.2 1.0 %collective-permute-done.2.refs_3_ = s32[3,128]{1,0:T(4,128)S(1)} collective-permute-done((s32[3,128]{1,0:T(4,128)S(1)}, s32[3,128]{1,0:T(4,128)S(1)}, u32[]{:S(2)}, u32[]{:S(2)}) %collective-permute-start.2) | collective-permute-done | bytes 1568 | tf_op jit(solution)/shard_map/ppermute | solution.py:20
  9.2 2.9 %collective-permute-done.1.refs_2_ = s32[3,128]{1,0:T(4,128)S(1)} collective-permute-done((s32[3,128]{1,0:T(4,128)S(1)}, s32[3,128]{1,0:T(4,128)S(1)}, u32[]{:S(2)}, u32[]{:S(2)}) %collective-permute-start.1) | collective-permute-done | bytes 1568 | tf_op jit(solution)/shard_map/ppermute | solution.py:20
  12.1 0.0 collective-permute-done.refs_1_
  12.1 2.4 %collective-permute-start.5 = (s32[12,128]{1,0:T(8,128)S(1)}, s32[12,128]{1,0:T(8,128)S(1)}, u32[]{:S(2)}, u32[]{:S(2)}) collective-permute-start(s32[12,128]{1,0:T(8,128)S(1)} %join.1), channel_id=1, source_target_pairs={{0,6},{1,7},{2,4},{3,5},{4,2},{5,3},{6,0},{7,1},{8,14},{9,15},{10,... | collective-permute-start | bytes 18440 | tf_op jit(solution)/shard_map/ppermute | solution.py:20
  14.6 0.5 collective-permute-start.4
  15.1 0.5 collective-permute-start.3
  15.6 0.0 collective-permute-done.6.other_signs_ref
  15.6 0.0 collective-permute-done.7.refs_1_
  15.6 4.4 %transform.1 = f32[8192,128]{1,0:T(8,128)S(1)} custom-call(s32[1]{0:T(128)} %bitcast.1.me_ref, s32[35,128]{1,0:T(8,128)S(1)} %fusion.1.signs_ref, s32[35,128]{1,0:T(8,128)S(1)} %collective-permute-done.6.other_signs_ref, f32[4096,256]{1,0:T(8,128)} %refs_0_.1, f32[4096,256]{1,0:T(8,128)} %collective-permute-done.7.refs_1_), custom_call_target="tpu_custom_call" | custom-call | flops 2147483648 | bytes 12582912 | tf_op jit(solution)/shard_map/transform/pallas_call | solution.py:91
  20.0 0.0 collective-permute-done.5
  20.0 0.0 collective-permute-done.4
  20.1 0.0 collective-permute-done.3
  20.1 3.3 %gather_far.1 = (f32[768,2,128]{2,1,0:T(2,128)S(1)}, f32[768,2,128]{2,1,0:T(2,128)S(1)}, f32[512,2,128]{2,1,0:T(2,128)S(1)}) custom-call(s32[1]{0:T(128)} %bitcast.1.me_ref, s32[1536]{0:T(1024)S(1)} %bitcast.31, s32[1536]{0:T(1024)S(1)} %bitcast.40, s32[1536]{0:T(1024)S(1)} %bitcast.37, s32[1536]{0:T(1024)S(1)} %bitcast.34, f32[4096,2,128]{2,1,0:T(2,128)S(1)} %bitcast.20), custom_call_target="tpu_custom_call" | custom-call | bytes 6291456 | tf_op jit(solution)/shard_map/gather_far/pallas_call | solution.py:136
  23.3 1.6 %collective-permute-start.8 = (f32[1536,128]{1,0:T(8,128)S(1)}, f32[1536,128]{1,0:T(8,128)S(1)}, u32[]{:S(2)}, u32[]{:S(2)}) collective-permute-start(f32[1536,128]{1,0:T(8,128)S(1)} %bitcast.44), channel_id=1, source_target_pairs={{0,2},{1,3},{2,0},{3,1},{4,6},{5,7},{6,4},{7,5},{8,10},{9,11},{10,... | collective-permute-start | bytes 2359304 | tf_op jit(solution)/shard_map/ppermute | solution.py:20
  24.9 0.0 collective-permute-start.16
  24.9 1.5 %collective-permute-start.12 = (f32[1536,128]{1,0:T(8,128)S(1)}, f32[1536,128]{1,0:T(8,128)S(1)}, u32[]{:S(2)}, u32[]{:S(2)}) collective-permute-start(f32[1536,128]{1,0:T(8,128)S(1)} %bitcast.43), channel_id=1, source_target_pairs={{0,4},{1,5},{2,6},{3,7},{4,0},{5,1},{6,2},{7,3},{8,12},{9,13},{10,... | collective-permute-start | bytes 2359304 | tf_op jit(solution)/shard_map/ppermute | solution.py:20
  26.4 1.2 %gather_end.1 = (f32[256,2,128]{2,1,0:T(2,128)S(1)}, f32[256,2,128]{2,1,0:T(2,128)S(1)}) custom-call(s32[1]{0:T(128)} %bitcast.1.me_ref, s32[1536]{0:T(1024)S(1)} %bitcast.32, s32[1536]{0:T(1024)S(1)} %bitcast.41, s32[1536]{0:T(1024)S(1)} %bitcast.38, s32[1536]{0:T(1024)S(1)} %bitcast.35, f32[4096,2,128]{2,1,0:T(2,128)S(1)} %bitcast.21), custom_call_target="tpu_custom_call" | custom-call | bytes 4718592 | tf_op jit(solution)/shard_map/gather_end/pallas_call | solution.py:136
  27.7 2.9 %gather_near.1 = (f32[384,2,128]{2,1,0:T(2,128)S(1)}, f32[384,2,128]{2,1,0:T(2,128)S(1)}, f32[384,2,128]{2,1,0:T(2,128)S(1)}, f32[384,2,128]{2,1,0:T(2,128)S(1)}) custom-call(s32[1]{0:T(128)} %bitcast.1.me_ref, s32[1536]{0:T(1024)S(1)} %bitcast.33, s32[1536]{0:T(1024)S(1)} %bitcast.42, s32[1536]{0:T(1024)S(1)} %bitcast.39, s32[1536]{0:T(1024)S(1)} %bitcast.36, ...), custom_call_target="tpu_custom_call" | custom-call | bytes 5767168 | tf_op jit(solution)/shard_map/gather_near/pallas_call | solution.py:136
  30.5 5.5 %collective-permute-done.16 = f32[1024,128]{1,0:T(8,128)S(1)} collective-permute-done((f32[1024,128]{1,0:T(8,128)S(1)}, f32[1024,128]{1,0:T(8,128)S(1)}, u32[]{:S(2)}, u32[]{:S(2)}) %collective-permute-start.16) | collective-permute-done | bytes 524320 | tf_op jit(solution)/shard_map/ppermute | solution.py:20
  36.1 0.1 slice_add_fusion.5
  36.1 2.9 %collective-permute-start.17 = (f32[512,128]{1,0:T(8,128)S(1)}, f32[512,128]{1,0:T(8,128)S(1)}, u32[]{:S(2)}, u32[]{:S(2)}) collective-permute-start(f32[512,128]{1,0:T(8,128)S(1)} %get-tuple-element.39), channel_id=1, source_target_pairs={{0,16},{1,17},{2,18},{3,19},{4,20},{5,21},{6,22},{7,23},{8,24},{9,... | collective-permute-start | bytes 786440 | tf_op jit(solution)/shard_map/ppermute | solution.py:20
  39.0 1.4 %collective-permute-done.8 = f32[1536,128]{1,0:T(8,128)S(1)} collective-permute-done((f32[1536,128]{1,0:T(8,128)S(1)}, f32[1536,128]{1,0:T(8,128)S(1)}, u32[]{:S(2)}, u32[]{:S(2)}) %collective-permute-start.8) | collective-permute-done | bytes 786464 | tf_op jit(solution)/shard_map/ppermute | solution.py:20
  40.4 0.1 slice_add_fusion.3
  40.4 1.4 %collective-permute-start.9 = (f32[768,128]{1,0:T(8,128)S(1)}, f32[768,128]{1,0:T(8,128)S(1)}, u32[]{:S(2)}, u32[]{:S(2)}) collective-permute-start(f32[768,128]{1,0:T(8,128)S(1)} %get-tuple-element.35), channel_id=1, source_target_pairs={{0,4},{1,5},{2,6},{3,7},{4,0},{5,1},{6,2},{7,3},{8,12},{9,13},{10,... | collective-permute-start | bytes 1179656 | tf_op jit(solution)/shard_map/ppermute | solution.py:20
  41.8 1.5 %collective-permute-done.12 = f32[1536,128]{1,0:T(8,128)S(1)} collective-permute-done((f32[1536,128]{1,0:T(8,128)S(1)}, f32[1536,128]{1,0:T(8,128)S(1)}, u32[]{:S(2)}, u32[]{:S(2)}) %collective-permute-start.12) | collective-permute-done | bytes 786464 | tf_op jit(solution)/shard_map/ppermute | solution.py:20
  43.3 0.1 slice_add_fusion.1
  43.4 0.1 collective-permute-start.13
  43.5 3.5 %collective-permute-done.17 = f32[512,128]{1,0:T(8,128)S(1)} collective-permute-done((f32[512,128]{1,0:T(8,128)S(1)}, f32[512,128]{1,0:T(8,128)S(1)}, u32[]{:S(2)}, u32[]{:S(2)}) %collective-permute-start.17) | collective-permute-done | bytes 262176 | tf_op jit(solution)/shard_map/ppermute | solution.py:20
  47.1 0.7 collective-permute-start.18
  47.7 2.2 %collective-permute-done.9 = f32[768,128]{1,0:T(8,128)S(1)} collective-permute-done((f32[768,128]{1,0:T(8,128)S(1)}, f32[768,128]{1,0:T(8,128)S(1)}, u32[]{:S(2)}, u32[]{:S(2)}) %collective-permute-start.9) | collective-permute-done | bytes 393248 | tf_op jit(solution)/shard_map/ppermute | solution.py:20
  50.0 0.1 slice_add_fusion.9
  50.0 1.8 %collective-permute-start.10 = (f32[384,128]{1,0:T(8,128)S(1)}, f32[384,128]{1,0:T(8,128)S(1)}, u32[]{:S(2)}, u32[]{:S(2)}) collective-permute-start(f32[384,128]{1,0:T(8,128)S(1)} %get-tuple-element.33), channel_id=1, source_target_pairs={{0,8},{1,9},{2,10},{3,11},{4,12},{5,13},{6,14},{7,15},{8,0},{9,1},... | collective-permute-start | bytes 589832 | tf_op jit(solution)/shard_map/ppermute | solution.py:20
  51.8 0.8 collective-permute-done.13
  52.7 2.1 %collective-permute-start.14 = (f32[384,128]{1,0:T(8,128)S(1)}, f32[384,128]{1,0:T(8,128)S(1)}, u32[]{:S(2)}, u32[]{:S(2)}) collective-permute-start(f32[384,128]{1,0:T(8,128)S(1)} %get-tuple-element.29), channel_id=1, source_target_pairs={{0,8},{1,9},{2,10},{3,11},{4,12},{5,13},{6,14},{7,15},{8,0},{9,1},... | collective-permute-start | bytes 589832 | tf_op jit(solution)/shard_map/ppermute | solution.py:20
  54.8 2.8 %collective-permute-done.10 = f32[384,128]{1,0:T(8,128)S(1)} collective-permute-done((f32[384,128]{1,0:T(8,128)S(1)}, f32[384,128]{1,0:T(8,128)S(1)}, u32[]{:S(2)}, u32[]{:S(2)}) %collective-permute-start.10) | collective-permute-done | bytes 196640 | tf_op jit(solution)/shard_map/ppermute | solution.py:20
  57.6 2.3 %collective-permute-start.11 = (f32[192,128]{1,0:T(8,128)S(1)}, f32[192,128]{1,0:T(8,128)S(1)}, u32[]{:S(2)}, u32[]{:S(2)}) collective-permute-start(f32[192,128]{1,0:T(8,128)S(1)} %get-tuple-element.42), channel_id=1, source_target_pairs={{0,16},{1,17},{2,18},{3,19},{4,20},{5,21},{6,22},{7,23},{8,24},{9,... | collective-permute-start | bytes 294920 | tf_op jit(solution)/shard_map/ppermute | solution.py:20
  59.9 0.8 collective-permute-done.14
  60.7 2.3 %collective-permute-start.15 = (f32[192,128]{1,0:T(8,128)S(1)}, f32[192,128]{1,0:T(8,128)S(1)}, u32[]{:S(2)}, u32[]{:S(2)}) collective-permute-start(f32[192,128]{1,0:T(8,128)S(1)} %get-tuple-element.40), channel_id=1, source_target_pairs={{0,16},{1,17},{2,18},{3,19},{4,20},{5,21},{6,22},{7,23},{8,24},{9,... | collective-permute-start | bytes 294920 | tf_op jit(solution)/shard_map/ppermute | solution.py:20
  63.1 0.0 collective-permute-done.18
  63.1 1.2 %collective-permute-start.19 = (f32[128,128]{1,0:T(8,128)S(1)}, f32[128,128]{1,0:T(8,128)S(1)}, u32[]{:S(2)}, u32[]{:S(2)}) collective-permute-start(f32[128,128]{1,0:T(8,128)S(1)} %get-tuple-element.44), channel_id=1, source_target_pairs={{0,4},{1,5},{2,6},{3,7},{4,0},{5,1},{6,2},{7,3},{8,12},{9,13},{10,... | collective-permute-start | bytes 196616 | tf_op jit(solution)/shard_map/ppermute | solution.py:20
  64.3 3.1 %collective-permute-done.19.refs_5_ = f32[128,128]{1,0:T(8,128)S(1)} collective-permute-done((f32[128,128]{1,0:T(8,128)S(1)}, f32[128,128]{1,0:T(8,128)S(1)}, u32[]{:S(2)}, u32[]{:S(2)}) %collective-permute-start.19) | collective-permute-done | bytes 65568 | tf_op jit(solution)/shard_map/ppermute | solution.py:20
  67.4 0.0 collective-permute-done.11.refs_1_
  67.4 0.0 collective-permute-done.15.refs_3_
  67.4 0.8 gram.1
  68.2 0.0 collective-permute-start.20
  68.2 1.3 %collective-permute-done.20 = f32[256,128]{1,0:T(8,128)S(1)} collective-permute-done((f32[256,128]{1,0:T(8,128)S(1)}, f32[256,128]{1,0:T(8,128)S(1)}, u32[]{:S(2)}, u32[]{:S(2)}) %collective-permute-start.20) | collective-permute-done | bytes 131104 | tf_op jit(solution)/shard_map/ppermute | solution.py:20
  69.6 1.3 %collective-permute-start.22 = (f32[128,128]{1,0:T(8,128)S(1)}, f32[128,128]{1,0:T(8,128)S(1)}, u32[]{:S(2)}, u32[]{:S(2)}) collective-permute-start(f32[128,128]{1,0:T(8,128)S(1)} %get-tuple-element.46), channel_id=1, source_target_pairs={{0,4},{1,5},{2,6},{3,7},{4,0},{5,1},{6,2},{7,3},{8,12},{9,13},{10,... | collective-permute-start | bytes 196616 | tf_op jit(solution)/shard_map/ppermute | solution.py:20
  70.9 0.5 collective-permute-start.23
  71.4 1.8 %collective-permute-start.21 = (f32[128,128]{1,0:T(8,128)S(1)}, f32[128,128]{1,0:T(8,128)S(1)}, u32[]{:S(2)}, u32[]{:S(2)}) collective-permute-start(f32[128,128]{1,0:T(8,128)S(1)} %get-tuple-element.47), channel_id=1, source_target_pairs={{0,2},{1,3},{2,0},{3,1},{4,6},{5,7},{6,4},{7,5},{8,10},{9,11},{10,... | collective-permute-start | bytes 196616 | tf_op jit(solution)/shard_map/ppermute | solution.py:20
  73.2 0.8 collective-permute-done.22
  73.9 2.5 %collective-permute-done.23 = f32[128,128]{1,0:T(8,128)S(1)} collective-permute-done((f32[128,128]{1,0:T(8,128)S(1)}, f32[128,128]{1,0:T(8,128)S(1)}, u32[]{:S(2)}, u32[]{:S(2)}) %collective-permute-start.23) | collective-permute-done | bytes 65568 | tf_op jit(solution)/shard_map/ppermute | solution.py:20
  76.4 0.0 collective-permute-done.21
  76.4 2.9 %collective-permute-start.26 = (f32[128,128]{1,0:T(8,128)S(1)}, f32[128,128]{1,0:T(8,128)S(1)}, u32[]{:S(2)}, u32[]{:S(2)}) collective-permute-start(f32[128,128]{1,0:T(8,128)S(1)} %add_add_fusion), channel_id=1, source_target_pairs={{0,24},{1,25},{2,26},{3,27},{4,28},{5,29},{6,30},{7,31},{8,16},{9,... | collective-permute-start | bytes 196616 | tf_op jit(solution)/shard_map/ppermute | solution.py:20
  79.3 0.0 collective-permute-start.25
  79.3 1.5 %collective-permute-start.24 = (f32[128,128]{1,0:T(8,128)S(1)}, f32[128,128]{1,0:T(8,128)S(1)}, u32[]{:S(2)}, u32[]{:S(2)}) collective-permute-start(f32[128,128]{1,0:T(8,128)S(1)} %add_add_fusion), channel_id=1, source_target_pairs={{0,8},{1,9},{2,10},{3,11},{4,12},{5,13},{6,14},{7,15},{8,0},{9,1},... | collective-permute-start | bytes 196616 | tf_op jit(solution)/shard_map/ppermute | solution.py:20
  80.9 2.2 %collective-permute-done.26 = f32[128,128]{1,0:T(8,128)S(1)} collective-permute-done((f32[128,128]{1,0:T(8,128)S(1)}, f32[128,128]{1,0:T(8,128)S(1)}, u32[]{:S(2)}, u32[]{:S(2)}) %collective-permute-start.26) | collective-permute-done | bytes 65568 | tf_op jit(solution)/shard_map/ppermute | solution.py:20
  83.0 1.6 %collective-permute-done.25 = f32[128,128]{1,0:T(8,128)S(1)} collective-permute-done((f32[128,128]{1,0:T(8,128)S(1)}, f32[128,128]{1,0:T(8,128)S(1)}, u32[]{:S(2)}, u32[]{:S(2)}) %collective-permute-start.25) | collective-permute-done | bytes 65568 | tf_op jit(solution)/shard_map/ppermute | solution.py:20
  84.7 0.6 multiply_bitcast_fusion
  (10 shorter events, 0.2 us)
Async XLA Ops:
  0.6 15.0 %collective-permute-start.7 = (f32[4096,256]{1,0:T(8,128)}, f32[4096,256]{1,0:T(8,128)}, u32[]{:S(2)}, u32[]{:S(2)}) collective-permute-start(f32[4096,256]{1,0:T(8,128)} %refs_0_.1), channel_id=1, source_target_pairs={{0,1},{1,0},{2,3},{3,2},{4,5},{5,4},{6,7},{7,6},{8,9},{9,8},{10,11... | collective-permute-start | bytes 12582920 | tf_op jit(solution)/shard_map/ppermute | solution.py:20
  2.5 13.1 %collective-permute-start.6 = (s32[35,128]{1,0:T(8,128)S(1)}, s32[35,128]{1,0:T(8,128)S(1)}, u32[]{:S(2)}, u32[]{:S(2)}) collective-permute-start(s32[35,128]{1,0:T(8,128)S(1)} %fusion.1.signs_ref), channel_id=1, source_target_pairs={{0,1},{1,0},{2,3},{3,2},{4,5},{5,4},{6,7},{7,6},{8,9},{9,8},{10,11... | collective-permute-start | bytes 53768 | tf_op jit(solution)/shard_map/ppermute | solution.py:20
  2.6 6.6 %collective-permute-start.2 = (s32[3,128]{1,0:T(4,128)S(1)}, s32[3,128]{1,0:T(4,128)S(1)}, u32[]{:S(2)}, u32[]{:S(2)}) collective-permute-start(s32[3,128]{1,0:T(4,128)S(1)} %slice.132.refs_0_), channel_id=1, source_target_pairs={{0,24},{1,25},{2,26},{3,27},{4,28},{5,29},{6,30},{7,31},{8,16},{9,... | collective-permute-start | bytes 4616 | tf_op jit(solution)/shard_map/ppermute | solution.py:20
  7.6 4.5 %collective-permute-start.1 = (s32[3,128]{1,0:T(4,128)S(1)}, s32[3,128]{1,0:T(4,128)S(1)}, u32[]{:S(2)}, u32[]{:S(2)}) collective-permute-start(s32[3,128]{1,0:T(4,128)S(1)} %slice.132.refs_0_), channel_id=1, source_target_pairs={{0,16},{1,17},{2,18},{3,19},{4,20},{5,21},{6,22},{7,23},{8,24},{9,... | collective-permute-start | bytes 4616 | tf_op jit(solution)/shard_map/ppermute | solution.py:20
  7.6 4.5 %collective-permute-start = (s32[3,128]{1,0:T(4,128)S(1)}, s32[3,128]{1,0:T(4,128)S(1)}, u32[]{:S(2)}, u32[]{:S(2)}) collective-permute-start(s32[3,128]{1,0:T(4,128)S(1)} %slice.132.refs_0_), channel_id=1, source_target_pairs={{0,8},{1,9},{2,10},{3,11},{4,12},{5,13},{6,14},{7,15},{8,0},{9,1},... | collective-permute-start | bytes 4616 | tf_op jit(solution)/shard_map/ppermute | solution.py:20
  12.1 7.9 %collective-permute-start.5 = (s32[12,128]{1,0:T(8,128)S(1)}, s32[12,128]{1,0:T(8,128)S(1)}, u32[]{:S(2)}, u32[]{:S(2)}) collective-permute-start(s32[12,128]{1,0:T(8,128)S(1)} %join.1), channel_id=1, source_target_pairs={{0,6},{1,7},{2,4},{3,5},{4,2},{5,3},{6,0},{7,1},{8,14},{9,15},{10,... | collective-permute-start | bytes 18440 | tf_op jit(solution)/shard_map/ppermute | solution.py:20
  14.6 5.5 %collective-permute-start.4 = (s32[12,128]{1,0:T(8,128)S(1)}, s32[12,128]{1,0:T(8,128)S(1)}, u32[]{:S(2)}, u32[]{:S(2)}) collective-permute-start(s32[12,128]{1,0:T(8,128)S(1)} %join.1), channel_id=1, source_target_pairs={{0,4},{1,5},{2,6},{3,7},{4,0},{5,1},{6,2},{7,3},{8,12},{9,13},{10,... | collective-permute-start | bytes 18440 | tf_op jit(solution)/shard_map/ppermute | solution.py:20
  15.1 5.0 %collective-permute-start.3 = (s32[12,128]{1,0:T(8,128)S(1)}, s32[12,128]{1,0:T(8,128)S(1)}, u32[]{:S(2)}, u32[]{:S(2)}) collective-permute-start(s32[12,128]{1,0:T(8,128)S(1)} %join.1), channel_id=1, source_target_pairs={{0,2},{1,3},{2,0},{3,1},{4,6},{5,7},{6,4},{7,5},{8,10},{9,11},{10,... | collective-permute-start | bytes 18440 | tf_op jit(solution)/shard_map/ppermute | solution.py:20
  23.3 17.0 %collective-permute-start.8 = (f32[1536,128]{1,0:T(8,128)S(1)}, f32[1536,128]{1,0:T(8,128)S(1)}, u32[]{:S(2)}, u32[]{:S(2)}) collective-permute-start(f32[1536,128]{1,0:T(8,128)S(1)} %bitcast.44), channel_id=1, source_target_pairs={{0,2},{1,3},{2,0},{3,1},{4,6},{5,7},{6,4},{7,5},{8,10},{9,11},{10,... | collective-permute-start | bytes 2359304 | tf_op jit(solution)/shard_map/ppermute | solution.py:20
  24.9 11.2 %collective-permute-start.16 = (f32[1024,128]{1,0:T(8,128)S(1)}, f32[1024,128]{1,0:T(8,128)S(1)}, u32[]{:S(2)}, u32[]{:S(2)}) collective-permute-start(f32[1024,128]{1,0:T(8,128)S(1)} %bitcast.23), channel_id=1, source_target_pairs={{0,8},{1,9},{2,10},{3,11},{4,12},{5,13},{6,14},{7,15},{8,0},{9,1},... | collective-permute-start | bytes 1572872 | tf_op jit(solution)/shard_map/ppermute | solution.py:20
  24.9 18.4 %collective-permute-start.12 = (f32[1536,128]{1,0:T(8,128)S(1)}, f32[1536,128]{1,0:T(8,128)S(1)}, u32[]{:S(2)}, u32[]{:S(2)}) collective-permute-start(f32[1536,128]{1,0:T(8,128)S(1)} %bitcast.43), channel_id=1, source_target_pairs={{0,4},{1,5},{2,6},{3,7},{4,0},{5,1},{6,2},{7,3},{8,12},{9,13},{10,... | collective-permute-start | bytes 2359304 | tf_op jit(solution)/shard_map/ppermute | solution.py:20
  36.1 10.9 %collective-permute-start.17 = (f32[512,128]{1,0:T(8,128)S(1)}, f32[512,128]{1,0:T(8,128)S(1)}, u32[]{:S(2)}, u32[]{:S(2)}) collective-permute-start(f32[512,128]{1,0:T(8,128)S(1)} %get-tuple-element.39), channel_id=1, source_target_pairs={{0,16},{1,17},{2,18},{3,19},{4,20},{5,21},{6,22},{7,23},{8,24},{9,... | collective-permute-start | bytes 786440 | tf_op jit(solution)/shard_map/ppermute | solution.py:20
  40.4 9.5 %collective-permute-start.9 = (f32[768,128]{1,0:T(8,128)S(1)}, f32[768,128]{1,0:T(8,128)S(1)}, u32[]{:S(2)}, u32[]{:S(2)}) collective-permute-start(f32[768,128]{1,0:T(8,128)S(1)} %get-tuple-element.35), channel_id=1, source_target_pairs={{0,4},{1,5},{2,6},{3,7},{4,0},{5,1},{6,2},{7,3},{8,12},{9,13},{10,... | collective-permute-start | bytes 1179656 | tf_op jit(solution)/shard_map/ppermute | solution.py:20
  43.4 9.2 %collective-permute-start.13 = (f32[768,128]{1,0:T(8,128)S(1)}, f32[768,128]{1,0:T(8,128)S(1)}, u32[]{:S(2)}, u32[]{:S(2)}) collective-permute-start(f32[768,128]{1,0:T(8,128)S(1)} %get-tuple-element.31), channel_id=1, source_target_pairs={{0,2},{1,3},{2,0},{3,1},{4,6},{5,7},{6,4},{7,5},{8,10},{9,11},{10,... | collective-permute-start | bytes 1179656 | tf_op jit(solution)/shard_map/ppermute | solution.py:20
  47.1 16.0 %collective-permute-start.18 = (f32[256,128]{1,0:T(8,128)S(1)}, f32[256,128]{1,0:T(8,128)S(1)}, u32[]{:S(2)}, u32[]{:S(2)}) collective-permute-start(f32[256,128]{1,0:T(8,128)S(1)} %get-tuple-element.37), channel_id=1, source_target_pairs={{0,2},{1,3},{2,0},{3,1},{4,6},{5,7},{6,4},{7,5},{8,10},{9,11},{10,... | collective-permute-start | bytes 393224 | tf_op jit(solution)/shard_map/ppermute | solution.py:20
  50.0 7.5 %collective-permute-start.10 = (f32[384,128]{1,0:T(8,128)S(1)}, f32[384,128]{1,0:T(8,128)S(1)}, u32[]{:S(2)}, u32[]{:S(2)}) collective-permute-start(f32[384,128]{1,0:T(8,128)S(1)} %get-tuple-element.33), channel_id=1, source_target_pairs={{0,8},{1,9},{2,10},{3,11},{4,12},{5,13},{6,14},{7,15},{8,0},{9,1},... | collective-permute-start | bytes 589832 | tf_op jit(solution)/shard_map/ppermute | solution.py:20
  52.7 8.0 %collective-permute-start.14 = (f32[384,128]{1,0:T(8,128)S(1)}, f32[384,128]{1,0:T(8,128)S(1)}, u32[]{:S(2)}, u32[]{:S(2)}) collective-permute-start(f32[384,128]{1,0:T(8,128)S(1)} %get-tuple-element.29), channel_id=1, source_target_pairs={{0,8},{1,9},{2,10},{3,11},{4,12},{5,13},{6,14},{7,15},{8,0},{9,1},... | collective-permute-start | bytes 589832 | tf_op jit(solution)/shard_map/ppermute | solution.py:20
  57.6 9.9 %collective-permute-start.11 = (f32[192,128]{1,0:T(8,128)S(1)}, f32[192,128]{1,0:T(8,128)S(1)}, u32[]{:S(2)}, u32[]{:S(2)}) collective-permute-start(f32[192,128]{1,0:T(8,128)S(1)} %get-tuple-element.42), channel_id=1, source_target_pairs={{0,16},{1,17},{2,18},{3,19},{4,20},{5,21},{6,22},{7,23},{8,24},{9,... | collective-permute-start | bytes 294920 | tf_op jit(solution)/shard_map/ppermute | solution.py:20
  60.7 6.7 %collective-permute-start.15 = (f32[192,128]{1,0:T(8,128)S(1)}, f32[192,128]{1,0:T(8,128)S(1)}, u32[]{:S(2)}, u32[]{:S(2)}) collective-permute-start(f32[192,128]{1,0:T(8,128)S(1)} %get-tuple-element.40), channel_id=1, source_target_pairs={{0,16},{1,17},{2,18},{3,19},{4,20},{5,21},{6,22},{7,23},{8,24},{9,... | collective-permute-start | bytes 294920 | tf_op jit(solution)/shard_map/ppermute | solution.py:20
  63.1 4.3 %collective-permute-start.19 = (f32[128,128]{1,0:T(8,128)S(1)}, f32[128,128]{1,0:T(8,128)S(1)}, u32[]{:S(2)}, u32[]{:S(2)}) collective-permute-start(f32[128,128]{1,0:T(8,128)S(1)} %get-tuple-element.44), channel_id=1, source_target_pairs={{0,4},{1,5},{2,6},{3,7},{4,0},{5,1},{6,2},{7,3},{8,12},{9,13},{10,... | collective-permute-start | bytes 196616 | tf_op jit(solution)/shard_map/ppermute | solution.py:20
  68.2 1.3 %collective-permute-start.20 = (f32[256,128]{1,0:T(8,128)S(1)}, f32[256,128]{1,0:T(8,128)S(1)}, u32[]{:S(2)}, u32[]{:S(2)}) collective-permute-start(f32[256,128]{1,0:T(8,128)S(1)} %get-tuple-element.26), channel_id=1, source_target_pairs={{0,1},{1,0},{2,3},{3,2},{4,5},{5,4},{6,7},{7,6},{8,9},{9,8},{10,11... | collective-permute-start | bytes 393224 | tf_op jit(solution)/shard_map/ppermute | solution.py:20
  69.6 4.3 %collective-permute-start.22 = (f32[128,128]{1,0:T(8,128)S(1)}, f32[128,128]{1,0:T(8,128)S(1)}, u32[]{:S(2)}, u32[]{:S(2)}) collective-permute-start(f32[128,128]{1,0:T(8,128)S(1)} %get-tuple-element.46), channel_id=1, source_target_pairs={{0,4},{1,5},{2,6},{3,7},{4,0},{5,1},{6,2},{7,3},{8,12},{9,13},{10,... | collective-permute-start | bytes 196616 | tf_op jit(solution)/shard_map/ppermute | solution.py:20
  70.9 5.5 %collective-permute-start.23 = (f32[128,128]{1,0:T(8,128)S(1)}, f32[128,128]{1,0:T(8,128)S(1)}, u32[]{:S(2)}, u32[]{:S(2)}) collective-permute-start(f32[128,128]{1,0:T(8,128)S(1)} %get-tuple-element.47), channel_id=1, source_target_pairs={{0,6},{1,7},{2,4},{3,5},{4,2},{5,3},{6,0},{7,1},{8,14},{9,15},{10,... | collective-permute-start | bytes 196616 | tf_op jit(solution)/shard_map/ppermute | solution.py:20
  71.4 5.0 %collective-permute-start.21 = (f32[128,128]{1,0:T(8,128)S(1)}, f32[128,128]{1,0:T(8,128)S(1)}, u32[]{:S(2)}, u32[]{:S(2)}) collective-permute-start(f32[128,128]{1,0:T(8,128)S(1)} %get-tuple-element.47), channel_id=1, source_target_pairs={{0,2},{1,3},{2,0},{3,1},{4,6},{5,7},{6,4},{7,5},{8,10},{9,11},{10,... | collective-permute-start | bytes 196616 | tf_op jit(solution)/shard_map/ppermute | solution.py:20
  76.4 6.6 %collective-permute-start.26 = (f32[128,128]{1,0:T(8,128)S(1)}, f32[128,128]{1,0:T(8,128)S(1)}, u32[]{:S(2)}, u32[]{:S(2)}) collective-permute-start(f32[128,128]{1,0:T(8,128)S(1)} %add_add_fusion), channel_id=1, source_target_pairs={{0,24},{1,25},{2,26},{3,27},{4,28},{5,29},{6,30},{7,31},{8,16},{9,... | collective-permute-start | bytes 196616 | tf_op jit(solution)/shard_map/ppermute | solution.py:20
  79.3 5.3 %collective-permute-start.25 = (f32[128,128]{1,0:T(8,128)S(1)}, f32[128,128]{1,0:T(8,128)S(1)}, u32[]{:S(2)}, u32[]{:S(2)}) collective-permute-start(f32[128,128]{1,0:T(8,128)S(1)} %add_add_fusion), channel_id=1, source_target_pairs={{0,16},{1,17},{2,18},{3,19},{4,20},{5,21},{6,22},{7,23},{8,24},{9,... | collective-permute-start | bytes 196616 | tf_op jit(solution)/shard_map/ppermute | solution.py:20
  79.3 5.3 %collective-permute-start.24 = (f32[128,128]{1,0:T(8,128)S(1)}, f32[128,128]{1,0:T(8,128)S(1)}, u32[]{:S(2)}, u32[]{:S(2)}) collective-permute-start(f32[128,128]{1,0:T(8,128)S(1)} %add_add_fusion), channel_id=1, source_target_pairs={{0,8},{1,9},{2,10},{3,11},{4,12},{5,13},{6,14},{7,15},{8,0},{9,1},... | collective-permute-start | bytes 196616 | tf_op jit(solution)/shard_map/ppermute | solution.py:20

commit v8 on v7

--- a/solution.py
+++ b/solution.py
@@ -11,7 +11,7 @@
 MESH_AXES = ("rx", "ry")
 GRANT = 12 * 2**20
 WIDE = 46 * 2**20
-AHEAD = 2
+AHEAD = 4
 REST = 4
 
 

time: 85.7 us -> 85.4 us (level)
  transfers between devices with their start and end apart: 27 -> 27, of which waited for: 16 -> 16; matrix products, arithmetic and copies ran while one was open for 1% -> 1% of each run, Pallas kernels for 10% -> 9%
where the time goes in v8:
time: 85.4 us; the launch traced here: 85.1 us
  starting transfers between devices  35.9 us (42%)
  waiting for transfers between devices  34.1 us (40%)
  Pallas kernels  11.8 us (14%)
  other arithmetic  1.83 us (2%)
  between operations  1.4 us (2%)
    ppermute x27, starting transfers between devices, swap(): return lax.ppermute(value, MESH_AXES, [(i, i ^ bits) for i in range(size)])  35.9 us
    ppermute x27, waiting for transfers between devices, swap(): return lax.ppermute(value, MESH_AXES, [(i, i ^ bits) for i in range(size)])  34.1 us
    pallas_call x5, Pallas kernels, call(): pl.pallas_call(kernel, in_specs=specs(len(scalars), len(arrays)) + [pl.Bl...  7.81 us
    pallas_call x1, Pallas kernels, transform(): pl.pallas_call(functools.partial(transform_kernel, full, chunks), in_spec...  3.98 us
  transfers between devices with their start and end apart: 27, of which 16 were waited for; matrix products, arithmetic and copies ran while one was open for 1% of the time, Pallas kernels for 9%

profile of v8, /device:TPU:0, one launch (start us, length us, event | category | flops | bytes accessed | tf_op | source)
XLA Modules:
  0.0 85.1 jit_solution(8065547270077450521)
XLA Ops:
  0.6 0.5 collective-permute-start.7
  1.8 0.7 fusion.1.signs_ref
  2.5 0.1 collective-permute-start.6
  2.6 5.0 %collective-permute-start.2 = (s32[3,128]{1,0:T(4,128)S(1)}, s32[3,128]{1,0:T(4,128)S(1)}, u32[]{:S(2)}, u32[]{:S(2)}) collective-permute-start(s32[3,128]{1,0:T(4,128)S(1)} %slice.132.refs_0_), channel_id=1, source_target_pairs={{0,24},{1,25},{2,26},{3,27},{4,28},{5,29},{6,30},{7,31},{8,16},{9,... | collective-permute-start | bytes 4616 | tf_op jit(solution)/shard_map/ppermute | solution.py:20
  7.6 0.0 collective-permute-start.1
  7.6 0.6 collective-permute-start
  8.2 1.0 %collective-permute-done.2.refs_3_ = s32[3,128]{1,0:T(4,128)S(1)} collective-permute-done((s32[3,128]{1,0:T(4,128)S(1)}, s32[3,128]{1,0:T(4,128)S(1)}, u32[]{:S(2)}, u32[]{:S(2)}) %collective-permute-start.2) | collective-permute-done | bytes 1568 | tf_op jit(solution)/shard_map/ppermute | solution.py:20
  9.2 2.9 %collective-permute-done.1.refs_2_ = s32[3,128]{1,0:T(4,128)S(1)} collective-permute-done((s32[3,128]{1,0:T(4,128)S(1)}, s32[3,128]{1,0:T(4,128)S(1)}, u32[]{:S(2)}, u32[]{:S(2)}) %collective-permute-start.1) | collective-permute-done | bytes 1568 | tf_op jit(solution)/shard_map/ppermute | solution.py:20
  12.1 0.0 collective-permute-done.refs_1_
  12.1 2.4 %collective-permute-start.5 = (s32[12,128]{1,0:T(8,128)S(1)}, s32[12,128]{1,0:T(8,128)S(1)}, u32[]{:S(2)}, u32[]{:S(2)}) collective-permute-start(s32[12,128]{1,0:T(8,128)S(1)} %join.1), channel_id=1, source_target_pairs={{0,6},{1,7},{2,4},{3,5},{4,2},{5,3},{6,0},{7,1},{8,14},{9,15},{10,... | collective-permute-start | bytes 18440 | tf_op jit(solution)/shard_map/ppermute | solution.py:20
  14.6 0.5 collective-permute-start.4
  15.1 0.5 collective-permute-start.3
  15.6 0.0 collective-permute-done.6.other_signs_ref
  15.6 0.0 collective-permute-done.7.refs_1_
  15.6 4.0 %transform.1 = f32[8192,128]{1,0:T(8,128)S(1)} custom-call(s32[1]{0:T(128)} %bitcast.1.me_ref, s32[35,128]{1,0:T(8,128)S(1)} %fusion.1.signs_ref, s32[35,128]{1,0:T(8,128)S(1)} %collective-permute-done.6.other_signs_ref, f32[4096,256]{1,0:T(8,128)} %refs_0_.1, f32[4096,256]{1,0:T(8,128)} %collective-permute-done.7.refs_1_), custom_call_target="tpu_custom_call" | custom-call | flops 2147483648 | bytes 12582912 | tf_op jit(solution)/shard_map/transform/pallas_call | solution.py:91
  19.6 0.0 collective-permute-done.5
  19.6 0.0 collective-permute-done.4
  19.6 0.0 collective-permute-done.3
  19.6 3.1 %gather_far.1 = (f32[768,2,128]{2,1,0:T(2,128)S(1)}, f32[768,2,128]{2,1,0:T(2,128)S(1)}, f32[512,2,128]{2,1,0:T(2,128)S(1)}) custom-call(s32[1]{0:T(128)} %bitcast.1.me_ref, s32[1536]{0:T(1024)S(1)} %bitcast.31, s32[1536]{0:T(1024)S(1)} %bitcast.40, s32[1536]{0:T(1024)S(1)} %bitcast.37, s32[1536]{0:T(1024)S(1)} %bitcast.34, f32[4096,2,128]{2,1,0:T(2,128)S(1)} %bitcast.20), custom_call_target="tpu_custom_call" | custom-call | bytes 6291456 | tf_op jit(solution)/shard_map/gather_far/pallas_call | solution.py:136
  22.7 1.6 %collective-permute-start.8 = (f32[1536,128]{1,0:T(8,128)S(1)}, f32[1536,128]{1,0:T(8,128)S(1)}, u32[]{:S(2)}, u32[]{:S(2)}) collective-permute-start(f32[1536,128]{1,0:T(8,128)S(1)} %bitcast.44), channel_id=1, source_target_pairs={{0,2},{1,3},{2,0},{3,1},{4,6},{5,7},{6,4},{7,5},{8,10},{9,11},{10,... | collective-permute-start | bytes 2359304 | tf_op jit(solution)/shard_map/ppermute | solution.py:20
  24.3 0.0 collective-permute-start.16
  24.3 1.5 %collective-permute-start.12 = (f32[1536,128]{1,0:T(8,128)S(1)}, f32[1536,128]{1,0:T(8,128)S(1)}, u32[]{:S(2)}, u32[]{:S(2)}) collective-permute-start(f32[1536,128]{1,0:T(8,128)S(1)} %bitcast.43), channel_id=1, source_target_pairs={{0,4},{1,5},{2,6},{3,7},{4,0},{5,1},{6,2},{7,3},{8,12},{9,13},{10,... | collective-permute-start | bytes 2359304 | tf_op jit(solution)/shard_map/ppermute | solution.py:20
  25.8 1.2 %gather_end.1 = (f32[256,2,128]{2,1,0:T(2,128)S(1)}, f32[256,2,128]{2,1,0:T(2,128)S(1)}) custom-call(s32[1]{0:T(128)} %bitcast.1.me_ref, s32[1536]{0:T(1024)S(1)} %bitcast.32, s32[1536]{0:T(1024)S(1)} %bitcast.41, s32[1536]{0:T(1024)S(1)} %bitcast.38, s32[1536]{0:T(1024)S(1)} %bitcast.35, f32[4096,2,128]{2,1,0:T(2,128)S(1)} %bitcast.21), custom_call_target="tpu_custom_call" | custom-call | bytes 4718592 | tf_op jit(solution)/shard_map/gather_end/pallas_call | solution.py:136
  27.0 2.8 %gather_near.1 = (f32[384,2,128]{2,1,0:T(2,128)S(1)}, f32[384,2,128]{2,1,0:T(2,128)S(1)}, f32[384,2,128]{2,1,0:T(2,128)S(1)}, f32[384,2,128]{2,1,0:T(2,128)S(1)}) custom-call(s32[1]{0:T(128)} %bitcast.1.me_ref, s32[1536]{0:T(1024)S(1)} %bitcast.33, s32[1536]{0:T(1024)S(1)} %bitcast.42, s32[1536]{0:T(1024)S(1)} %bitcast.39, s32[1536]{0:T(1024)S(1)} %bitcast.36, ...), custom_call_target="tpu_custom_call" | custom-call | bytes 5767168 | tf_op jit(solution)/shard_map/gather_near/pallas_call | solution.py:136
  29.7 6.0 %collective-permute-done.16 = f32[1024,128]{1,0:T(8,128)S(1)} collective-permute-done((f32[1024,128]{1,0:T(8,128)S(1)}, f32[1024,128]{1,0:T(8,128)S(1)}, u32[]{:S(2)}, u32[]{:S(2)}) %collective-permute-start.16) | collective-permute-done | bytes 524320 | tf_op jit(solution)/shard_map/ppermute | solution.py:20
  35.7 0.1 slice_add_fusion.5
  35.8 2.6 %collective-permute-start.17 = (f32[512,128]{1,0:T(8,128)S(1)}, f32[512,128]{1,0:T(8,128)S(1)}, u32[]{:S(2)}, u32[]{:S(2)}) collective-permute-start(f32[512,128]{1,0:T(8,128)S(1)} %get-tuple-element.39), channel_id=1, source_target_pairs={{0,16},{1,17},{2,18},{3,19},{4,20},{5,21},{6,22},{7,23},{8,24},{9,... | collective-permute-start | bytes 786440 | tf_op jit(solution)/shard_map/ppermute | solution.py:20
  38.4 1.7 %collective-permute-done.8 = f32[1536,128]{1,0:T(8,128)S(1)} collective-permute-done((f32[1536,128]{1,0:T(8,128)S(1)}, f32[1536,128]{1,0:T(8,128)S(1)}, u32[]{:S(2)}, u32[]{:S(2)}) %collective-permute-start.8) | collective-permute-done | bytes 786464 | tf_op jit(solution)/shard_map/ppermute | solution.py:20
  40.1 0.1 slice_add_fusion.3
  40.2 1.4 %collective-permute-start.9 = (f32[768,128]{1,0:T(8,128)S(1)}, f32[768,128]{1,0:T(8,128)S(1)}, u32[]{:S(2)}, u32[]{:S(2)}) collective-permute-start(f32[768,128]{1,0:T(8,128)S(1)} %get-tuple-element.35), channel_id=1, source_target_pairs={{0,4},{1,5},{2,6},{3,7},{4,0},{5,1},{6,2},{7,3},{8,12},{9,13},{10,... | collective-permute-start | bytes 1179656 | tf_op jit(solution)/shard_map/ppermute | solution.py:20
  41.6 1.2 %collective-permute-done.12 = f32[1536,128]{1,0:T(8,128)S(1)} collective-permute-done((f32[1536,128]{1,0:T(8,128)S(1)}, f32[1536,128]{1,0:T(8,128)S(1)}, u32[]{:S(2)}, u32[]{:S(2)}) %collective-permute-start.12) | collective-permute-done | bytes 786464 | tf_op jit(solution)/shard_map/ppermute | solution.py:20
  42.8 0.1 slice_add_fusion.1
  42.9 0.4 collective-permute-start.13
  43.3 4.0 %collective-permute-done.17 = f32[512,128]{1,0:T(8,128)S(1)} collective-permute-done((f32[512,128]{1,0:T(8,128)S(1)}, f32[512,128]{1,0:T(8,128)S(1)}, u32[]{:S(2)}, u32[]{:S(2)}) %collective-permute-start.17) | collective-permute-done | bytes 262176 | tf_op jit(solution)/shard_map/ppermute | solution.py:20
  47.3 0.6 collective-permute-start.18
  47.9 1.9 %collective-permute-done.9 = f32[768,128]{1,0:T(8,128)S(1)} collective-permute-done((f32[768,128]{1,0:T(8,128)S(1)}, f32[768,128]{1,0:T(8,128)S(1)}, u32[]{:S(2)}, u32[]{:S(2)}) %collective-permute-start.9) | collective-permute-done | bytes 393248 | tf_op jit(solution)/shard_map/ppermute | solution.py:20
  49.7 0.1 slice_add_fusion.9
  49.8 1.8 %collective-permute-start.10 = (f32[384,128]{1,0:T(8,128)S(1)}, f32[384,128]{1,0:T(8,128)S(1)}, u32[]{:S(2)}, u32[]{:S(2)}) collective-permute-start(f32[384,128]{1,0:T(8,128)S(1)} %get-tuple-element.33), channel_id=1, source_target_pairs={{0,8},{1,9},{2,10},{3,11},{4,12},{5,13},{6,14},{7,15},{8,0},{9,1},... | collective-permute-start | bytes 589832 | tf_op jit(solution)/shard_map/ppermute | solution.py:20
  51.6 0.5 collective-permute-done.13
  52.1 2.5 %collective-permute-start.14 = (f32[384,128]{1,0:T(8,128)S(1)}, f32[384,128]{1,0:T(8,128)S(1)}, u32[]{:S(2)}, u32[]{:S(2)}) collective-permute-start(f32[384,128]{1,0:T(8,128)S(1)} %get-tuple-element.29), channel_id=1, source_target_pairs={{0,8},{1,9},{2,10},{3,11},{4,12},{5,13},{6,14},{7,15},{8,0},{9,1},... | collective-permute-start | bytes 589832 | tf_op jit(solution)/shard_map/ppermute | solution.py:20
  54.7 2.7 %collective-permute-done.10 = f32[384,128]{1,0:T(8,128)S(1)} collective-permute-done((f32[384,128]{1,0:T(8,128)S(1)}, f32[384,128]{1,0:T(8,128)S(1)}, u32[]{:S(2)}, u32[]{:S(2)}) %collective-permute-start.10) | collective-permute-done | bytes 196640 | tf_op jit(solution)/shard_map/ppermute | solution.py:20
  57.4 2.2 %collective-permute-start.11 = (f32[192,128]{1,0:T(8,128)S(1)}, f32[192,128]{1,0:T(8,128)S(1)}, u32[]{:S(2)}, u32[]{:S(2)}) collective-permute-start(f32[192,128]{1,0:T(8,128)S(1)} %get-tuple-element.42), channel_id=1, source_target_pairs={{0,16},{1,17},{2,18},{3,19},{4,20},{5,21},{6,22},{7,23},{8,24},{9,... | collective-permute-start | bytes 294920 | tf_op jit(solution)/shard_map/ppermute | solution.py:20
  59.6 0.9 %collective-permute-done.14 = f32[384,128]{1,0:T(8,128)S(1)} collective-permute-done((f32[384,128]{1,0:T(8,128)S(1)}, f32[384,128]{1,0:T(8,128)S(1)}, u32[]{:S(2)}, u32[]{:S(2)}) %collective-permute-start.14) | collective-permute-done | bytes 196640 | tf_op jit(solution)/shard_map/ppermute | solution.py:20
  60.6 2.2 %collective-permute-start.15 = (f32[192,128]{1,0:T(8,128)S(1)}, f32[192,128]{1,0:T(8,128)S(1)}, u32[]{:S(2)}, u32[]{:S(2)}) collective-permute-start(f32[192,128]{1,0:T(8,128)S(1)} %get-tuple-element.40), channel_id=1, source_target_pairs={{0,16},{1,17},{2,18},{3,19},{4,20},{5,21},{6,22},{7,23},{8,24},{9,... | collective-permute-start | bytes 294920 | tf_op jit(solution)/shard_map/ppermute | solution.py:20
  62.8 0.0 collective-permute-done.18
  62.8 1.4 %collective-permute-start.19 = (f32[128,128]{1,0:T(8,128)S(1)}, f32[128,128]{1,0:T(8,128)S(1)}, u32[]{:S(2)}, u32[]{:S(2)}) collective-permute-start(f32[128,128]{1,0:T(8,128)S(1)} %get-tuple-element.44), channel_id=1, source_target_pairs={{0,4},{1,5},{2,6},{3,7},{4,0},{5,1},{6,2},{7,3},{8,12},{9,13},{10,... | collective-permute-start | bytes 196616 | tf_op jit(solution)/shard_map/ppermute | solution.py:20
  64.2 2.9 %collective-permute-done.19.refs_5_ = f32[128,128]{1,0:T(8,128)S(1)} collective-permute-done((f32[128,128]{1,0:T(8,128)S(1)}, f32[128,128]{1,0:T(8,128)S(1)}, u32[]{:S(2)}, u32[]{:S(2)}) %collective-permute-start.19) | collective-permute-done | bytes 65568 | tf_op jit(solution)/shard_map/ppermute | solution.py:20
  67.1 0.0 collective-permute-done.11.refs_1_
  67.1 0.0 collective-permute-done.15.refs_3_
  67.1 0.8 gram.1
  67.9 0.0 collective-permute-start.20
  67.9 1.3 %collective-permute-done.20 = f32[256,128]{1,0:T(8,128)S(1)} collective-permute-done((f32[256,128]{1,0:T(8,128)S(1)}, f32[256,128]{1,0:T(8,128)S(1)}, u32[]{:S(2)}, u32[]{:S(2)}) %collective-permute-start.20) | collective-permute-done | bytes 131104 | tf_op jit(solution)/shard_map/ppermute | solution.py:20
  69.3 1.4 %collective-permute-start.22 = (f32[128,128]{1,0:T(8,128)S(1)}, f32[128,128]{1,0:T(8,128)S(1)}, u32[]{:S(2)}, u32[]{:S(2)}) collective-permute-start(f32[128,128]{1,0:T(8,128)S(1)} %get-tuple-element.46), channel_id=1, source_target_pairs={{0,4},{1,5},{2,6},{3,7},{4,0},{5,1},{6,2},{7,3},{8,12},{9,13},{10,... | collective-permute-start | bytes 196616 | tf_op jit(solution)/shard_map/ppermute | solution.py:20
  70.7 0.8 collective-permute-start.23
  71.5 1.3 %collective-permute-start.21 = (f32[128,128]{1,0:T(8,128)S(1)}, f32[128,128]{1,0:T(8,128)S(1)}, u32[]{:S(2)}, u32[]{:S(2)}) collective-permute-start(f32[128,128]{1,0:T(8,128)S(1)} %get-tuple-element.47), channel_id=1, source_target_pairs={{0,2},{1,3},{2,0},{3,1},{4,6},{5,7},{6,4},{7,5},{8,10},{9,11},{10,... | collective-permute-start | bytes 196616 | tf_op jit(solution)/shard_map/ppermute | solution.py:20
  72.8 0.8 collective-permute-done.22
  73.6 2.6 %collective-permute-done.23 = f32[128,128]{1,0:T(8,128)S(1)} collective-permute-done((f32[128,128]{1,0:T(8,128)S(1)}, f32[128,128]{1,0:T(8,128)S(1)}, u32[]{:S(2)}, u32[]{:S(2)}) %collective-permute-start.23) | collective-permute-done | bytes 65568 | tf_op jit(solution)/shard_map/ppermute | solution.py:20
  76.2 0.0 collective-permute-done.21
  76.2 3.0 %collective-permute-start.26 = (f32[128,128]{1,0:T(8,128)S(1)}, f32[128,128]{1,0:T(8,128)S(1)}, u32[]{:S(2)}, u32[]{:S(2)}) collective-permute-start(f32[128,128]{1,0:T(8,128)S(1)} %add_add_fusion), channel_id=1, source_target_pairs={{0,24},{1,25},{2,26},{3,27},{4,28},{5,29},{6,30},{7,31},{8,16},{9,... | collective-permute-start | bytes 196616 | tf_op jit(solution)/shard_map/ppermute | solution.py:20
  79.2 1.5 %collective-permute-start.24 = (f32[128,128]{1,0:T(8,128)S(1)}, f32[128,128]{1,0:T(8,128)S(1)}, u32[]{:S(2)}, u32[]{:S(2)}) collective-permute-start(f32[128,128]{1,0:T(8,128)S(1)} %add_add_fusion), channel_id=1, source_target_pairs={{0,8},{1,9},{2,10},{3,11},{4,12},{5,13},{6,14},{7,15},{8,0},{9,1},... | collective-permute-start | bytes 196616 | tf_op jit(solution)/shard_map/ppermute | solution.py:20
  80.6 2.0 %collective-permute-done.26 = f32[128,128]{1,0:T(8,128)S(1)} collective-permute-done((f32[128,128]{1,0:T(8,128)S(1)}, f32[128,128]{1,0:T(8,128)S(1)}, u32[]{:S(2)}, u32[]{:S(2)}) %collective-permute-start.26) | collective-permute-done | bytes 65568 | tf_op jit(solution)/shard_map/ppermute | solution.py:20
  82.7 1.7 %collective-permute-done.25 = f32[128,128]{1,0:T(8,128)S(1)} collective-permute-done((f32[128,128]{1,0:T(8,128)S(1)}, f32[128,128]{1,0:T(8,128)S(1)}, u32[]{:S(2)}, u32[]{:S(2)}) %collective-permute-start.25) | collective-permute-done | bytes 65568 | tf_op jit(solution)/shard_map/ppermute | solution.py:20
  84.4 0.0 collective-permute-done.24
  84.4 0.6 multiply_bitcast_fusion
  (10 shorter events, 0.2 us)
Async XLA Ops:
  0.6 15.0 %collective-permute-start.7 = (f32[4096,256]{1,0:T(8,128)}, f32[4096,256]{1,0:T(8,128)}, u32[]{:S(2)}, u32[]{:S(2)}) collective-permute-start(f32[4096,256]{1,0:T(8,128)} %refs_0_.1), channel_id=1, source_target_pairs={{0,1},{1,0},{2,3},{3,2},{4,5},{5,4},{6,7},{7,6},{8,9},{9,8},{10,11... | collective-permute-start | bytes 12582920 | tf_op jit(solution)/shard_map/ppermute | solution.py:20
  2.5 13.1 %collective-permute-start.6 = (s32[35,128]{1,0:T(8,128)S(1)}, s32[35,128]{1,0:T(8,128)S(1)}, u32[]{:S(2)}, u32[]{:S(2)}) collective-permute-start(s32[35,128]{1,0:T(8,128)S(1)} %fusion.1.signs_ref), channel_id=1, source_target_pairs={{0,1},{1,0},{2,3},{3,2},{4,5},{5,4},{6,7},{7,6},{8,9},{9,8},{10,11... | collective-permute-start | bytes 53768 | tf_op jit(solution)/shard_map/ppermute | solution.py:20
  2.6 6.6 %collective-permute-start.2 = (s32[3,128]{1,0:T(4,128)S(1)}, s32[3,128]{1,0:T(4,128)S(1)}, u32[]{:S(2)}, u32[]{:S(2)}) collective-permute-start(s32[3,128]{1,0:T(4,128)S(1)} %slice.132.refs_0_), channel_id=1, source_target_pairs={{0,24},{1,25},{2,26},{3,27},{4,28},{5,29},{6,30},{7,31},{8,16},{9,... | collective-permute-start | bytes 4616 | tf_op jit(solution)/shard_map/ppermute | solution.py:20
  7.6 4.5 %collective-permute-start.1 = (s32[3,128]{1,0:T(4,128)S(1)}, s32[3,128]{1,0:T(4,128)S(1)}, u32[]{:S(2)}, u32[]{:S(2)}) collective-permute-start(s32[3,128]{1,0:T(4,128)S(1)} %slice.132.refs_0_), channel_id=1, source_target_pairs={{0,16},{1,17},{2,18},{3,19},{4,20},{5,21},{6,22},{7,23},{8,24},{9,... | collective-permute-start | bytes 4616 | tf_op jit(solution)/shard_map/ppermute | solution.py:20
  7.6 4.5 %collective-permute-start = (s32[3,128]{1,0:T(4,128)S(1)}, s32[3,128]{1,0:T(4,128)S(1)}, u32[]{:S(2)}, u32[]{:S(2)}) collective-permute-start(s32[3,128]{1,0:T(4,128)S(1)} %slice.132.refs_0_), channel_id=1, source_target_pairs={{0,8},{1,9},{2,10},{3,11},{4,12},{5,13},{6,14},{7,15},{8,0},{9,1},... | collective-permute-start | bytes 4616 | tf_op jit(solution)/shard_map/ppermute | solution.py:20
  12.1 7.5 %collective-permute-start.5 = (s32[12,128]{1,0:T(8,128)S(1)}, s32[12,128]{1,0:T(8,128)S(1)}, u32[]{:S(2)}, u32[]{:S(2)}) collective-permute-start(s32[12,128]{1,0:T(8,128)S(1)} %join.1), channel_id=1, source_target_pairs={{0,6},{1,7},{2,4},{3,5},{4,2},{5,3},{6,0},{7,1},{8,14},{9,15},{10,... | collective-permute-start | bytes 18440 | tf_op jit(solution)/shard_map/ppermute | solution.py:20
  14.6 5.0 %collective-permute-start.4 = (s32[12,128]{1,0:T(8,128)S(1)}, s32[12,128]{1,0:T(8,128)S(1)}, u32[]{:S(2)}, u32[]{:S(2)}) collective-permute-start(s32[12,128]{1,0:T(8,128)S(1)} %join.1), channel_id=1, source_target_pairs={{0,4},{1,5},{2,6},{3,7},{4,0},{5,1},{6,2},{7,3},{8,12},{9,13},{10,... | collective-permute-start | bytes 18440 | tf_op jit(solution)/shard_map/ppermute | solution.py:20
  15.1 4.6 %collective-permute-start.3 = (s32[12,128]{1,0:T(8,128)S(1)}, s32[12,128]{1,0:T(8,128)S(1)}, u32[]{:S(2)}, u32[]{:S(2)}) collective-permute-start(s32[12,128]{1,0:T(8,128)S(1)} %join.1), channel_id=1, source_target_pairs={{0,2},{1,3},{2,0},{3,1},{4,6},{5,7},{6,4},{7,5},{8,10},{9,11},{10,... | collective-permute-start | bytes 18440 | tf_op jit(solution)/shard_map/ppermute | solution.py:20
  22.7 17.4 %collective-permute-start.8 = (f32[1536,128]{1,0:T(8,128)S(1)}, f32[1536,128]{1,0:T(8,128)S(1)}, u32[]{:S(2)}, u32[]{:S(2)}) collective-permute-start(f32[1536,128]{1,0:T(8,128)S(1)} %bitcast.44), channel_id=1, source_target_pairs={{0,2},{1,3},{2,0},{3,1},{4,6},{5,7},{6,4},{7,5},{8,10},{9,11},{10,... | collective-permute-start | bytes 2359304 | tf_op jit(solution)/shard_map/ppermute | solution.py:20
  24.3 11.4 %collective-permute-start.16 = (f32[1024,128]{1,0:T(8,128)S(1)}, f32[1024,128]{1,0:T(8,128)S(1)}, u32[]{:S(2)}, u32[]{:S(2)}) collective-permute-start(f32[1024,128]{1,0:T(8,128)S(1)} %bitcast.23), channel_id=1, source_target_pairs={{0,8},{1,9},{2,10},{3,11},{4,12},{5,13},{6,14},{7,15},{8,0},{9,1},... | collective-permute-start | bytes 1572872 | tf_op jit(solution)/shard_map/ppermute | solution.py:20
  24.3 18.5 %collective-permute-start.12 = (f32[1536,128]{1,0:T(8,128)S(1)}, f32[1536,128]{1,0:T(8,128)S(1)}, u32[]{:S(2)}, u32[]{:S(2)}) collective-permute-start(f32[1536,128]{1,0:T(8,128)S(1)} %bitcast.43), channel_id=1, source_target_pairs={{0,4},{1,5},{2,6},{3,7},{4,0},{5,1},{6,2},{7,3},{8,12},{9,13},{10,... | collective-permute-start | bytes 2359304 | tf_op jit(solution)/shard_map/ppermute | solution.py:20
  35.8 11.5 %collective-permute-start.17 = (f32[512,128]{1,0:T(8,128)S(1)}, f32[512,128]{1,0:T(8,128)S(1)}, u32[]{:S(2)}, u32[]{:S(2)}) collective-permute-start(f32[512,128]{1,0:T(8,128)S(1)} %get-tuple-element.39), channel_id=1, source_target_pairs={{0,16},{1,17},{2,18},{3,19},{4,20},{5,21},{6,22},{7,23},{8,24},{9,... | collective-permute-start | bytes 786440 | tf_op jit(solution)/shard_map/ppermute | solution.py:20
  40.2 9.6 %collective-permute-start.9 = (f32[768,128]{1,0:T(8,128)S(1)}, f32[768,128]{1,0:T(8,128)S(1)}, u32[]{:S(2)}, u32[]{:S(2)}) collective-permute-start(f32[768,128]{1,0:T(8,128)S(1)} %get-tuple-element.35), channel_id=1, source_target_pairs={{0,4},{1,5},{2,6},{3,7},{4,0},{5,1},{6,2},{7,3},{8,12},{9,13},{10,... | collective-permute-start | bytes 1179656 | tf_op jit(solution)/shard_map/ppermute | solution.py:20
  42.9 9.2 %collective-permute-start.13 = (f32[768,128]{1,0:T(8,128)S(1)}, f32[768,128]{1,0:T(8,128)S(1)}, u32[]{:S(2)}, u32[]{:S(2)}) collective-permute-start(f32[768,128]{1,0:T(8,128)S(1)} %get-tuple-element.31), channel_id=1, source_target_pairs={{0,2},{1,3},{2,0},{3,1},{4,6},{5,7},{6,4},{7,5},{8,10},{9,11},{10,... | collective-permute-start | bytes 1179656 | tf_op jit(solution)/shard_map/ppermute | solution.py:20
  47.3 15.5 %collective-permute-start.18 = (f32[256,128]{1,0:T(8,128)S(1)}, f32[256,128]{1,0:T(8,128)S(1)}, u32[]{:S(2)}, u32[]{:S(2)}) collective-permute-start(f32[256,128]{1,0:T(8,128)S(1)} %get-tuple-element.37), channel_id=1, source_target_pairs={{0,2},{1,3},{2,0},{3,1},{4,6},{5,7},{6,4},{7,5},{8,10},{9,11},{10,... | collective-permute-start | bytes 393224 | tf_op jit(solution)/shard_map/ppermute | solution.py:20
  49.8 7.6 %collective-permute-start.10 = (f32[384,128]{1,0:T(8,128)S(1)}, f32[384,128]{1,0:T(8,128)S(1)}, u32[]{:S(2)}, u32[]{:S(2)}) collective-permute-start(f32[384,128]{1,0:T(8,128)S(1)} %get-tuple-element.33), channel_id=1, source_target_pairs={{0,8},{1,9},{2,10},{3,11},{4,12},{5,13},{6,14},{7,15},{8,0},{9,1},... | collective-permute-start | bytes 589832 | tf_op jit(solution)/shard_map/ppermute | solution.py:20
  52.1 8.4 %collective-permute-start.14 = (f32[384,128]{1,0:T(8,128)S(1)}, f32[384,128]{1,0:T(8,128)S(1)}, u32[]{:S(2)}, u32[]{:S(2)}) collective-permute-start(f32[384,128]{1,0:T(8,128)S(1)} %get-tuple-element.29), channel_id=1, source_target_pairs={{0,8},{1,9},{2,10},{3,11},{4,12},{5,13},{6,14},{7,15},{8,0},{9,1},... | collective-permute-start | bytes 589832 | tf_op jit(solution)/shard_map/ppermute | solution.py:20
  57.4 9.7 %collective-permute-start.11 = (f32[192,128]{1,0:T(8,128)S(1)}, f32[192,128]{1,0:T(8,128)S(1)}, u32[]{:S(2)}, u32[]{:S(2)}) collective-permute-start(f32[192,128]{1,0:T(8,128)S(1)} %get-tuple-element.42), channel_id=1, source_target_pairs={{0,16},{1,17},{2,18},{3,19},{4,20},{5,21},{6,22},{7,23},{8,24},{9,... | collective-permute-start | bytes 294920 | tf_op jit(solution)/shard_map/ppermute | solution.py:20
  60.6 6.5 %collective-permute-start.15 = (f32[192,128]{1,0:T(8,128)S(1)}, f32[192,128]{1,0:T(8,128)S(1)}, u32[]{:S(2)}, u32[]{:S(2)}) collective-permute-start(f32[192,128]{1,0:T(8,128)S(1)} %get-tuple-element.40), channel_id=1, source_target_pairs={{0,16},{1,17},{2,18},{3,19},{4,20},{5,21},{6,22},{7,23},{8,24},{9,... | collective-permute-start | bytes 294920 | tf_op jit(solution)/shard_map/ppermute | solution.py:20
  62.8 4.3 %collective-permute-start.19 = (f32[128,128]{1,0:T(8,128)S(1)}, f32[128,128]{1,0:T(8,128)S(1)}, u32[]{:S(2)}, u32[]{:S(2)}) collective-permute-start(f32[128,128]{1,0:T(8,128)S(1)} %get-tuple-element.44), channel_id=1, source_target_pairs={{0,4},{1,5},{2,6},{3,7},{4,0},{5,1},{6,2},{7,3},{8,12},{9,13},{10,... | collective-permute-start | bytes 196616 | tf_op jit(solution)/shard_map/ppermute | solution.py:20
  67.9 1.3 %collective-permute-start.20 = (f32[256,128]{1,0:T(8,128)S(1)}, f32[256,128]{1,0:T(8,128)S(1)}, u32[]{:S(2)}, u32[]{:S(2)}) collective-permute-start(f32[256,128]{1,0:T(8,128)S(1)} %get-tuple-element.26), channel_id=1, source_target_pairs={{0,1},{1,0},{2,3},{3,2},{4,5},{5,4},{6,7},{7,6},{8,9},{9,8},{10,11... | collective-permute-start | bytes 393224 | tf_op jit(solution)/shard_map/ppermute | solution.py:20
  69.3 4.3 %collective-permute-start.22 = (f32[128,128]{1,0:T(8,128)S(1)}, f32[128,128]{1,0:T(8,128)S(1)}, u32[]{:S(2)}, u32[]{:S(2)}) collective-permute-start(f32[128,128]{1,0:T(8,128)S(1)} %get-tuple-element.46), channel_id=1, source_target_pairs={{0,4},{1,5},{2,6},{3,7},{4,0},{5,1},{6,2},{7,3},{8,12},{9,13},{10,... | collective-permute-start | bytes 196616 | tf_op jit(solution)/shard_map/ppermute | solution.py:20
  70.7 5.5 %collective-permute-start.23 = (f32[128,128]{1,0:T(8,128)S(1)}, f32[128,128]{1,0:T(8,128)S(1)}, u32[]{:S(2)}, u32[]{:S(2)}) collective-permute-start(f32[128,128]{1,0:T(8,128)S(1)} %get-tuple-element.47), channel_id=1, source_target_pairs={{0,6},{1,7},{2,4},{3,5},{4,2},{5,3},{6,0},{7,1},{8,14},{9,15},{10,... | collective-permute-start | bytes 196616 | tf_op jit(solution)/shard_map/ppermute | solution.py:20
  71.5 4.6 %collective-permute-start.21 = (f32[128,128]{1,0:T(8,128)S(1)}, f32[128,128]{1,0:T(8,128)S(1)}, u32[]{:S(2)}, u32[]{:S(2)}) collective-permute-start(f32[128,128]{1,0:T(8,128)S(1)} %get-tuple-element.47), channel_id=1, source_target_pairs={{0,2},{1,3},{2,0},{3,1},{4,6},{5,7},{6,4},{7,5},{8,10},{9,11},{10,... | collective-permute-start | bytes 196616 | tf_op jit(solution)/shard_map/ppermute | solution.py:20
  76.2 6.5 %collective-permute-start.26 = (f32[128,128]{1,0:T(8,128)S(1)}, f32[128,128]{1,0:T(8,128)S(1)}, u32[]{:S(2)}, u32[]{:S(2)}) collective-permute-start(f32[128,128]{1,0:T(8,128)S(1)} %add_add_fusion), channel_id=1, source_target_pairs={{0,24},{1,25},{2,26},{3,27},{4,28},{5,29},{6,30},{7,31},{8,16},{9,... | collective-permute-start | bytes 196616 | tf_op jit(solution)/shard_map/ppermute | solution.py:20
  79.2 5.2 %collective-permute-start.25 = (f32[128,128]{1,0:T(8,128)S(1)}, f32[128,128]{1,0:T(8,128)S(1)}, u32[]{:S(2)}, u32[]{:S(2)}) collective-permute-start(f32[128,128]{1,0:T(8,128)S(1)} %add_add_fusion), channel_id=1, source_target_pairs={{0,16},{1,17},{2,18},{3,19},{4,20},{5,21},{6,22},{7,23},{8,24},{9,... | collective-permute-start | bytes 196616 | tf_op jit(solution)/shard_map/ppermute | solution.py:20
  79.2 5.2 %collective-permute-start.24 = (f32[128,128]{1,0:T(8,128)S(1)}, f32[128,128]{1,0:T(8,128)S(1)}, u32[]{:S(2)}, u32[]{:S(2)}) collective-permute-start(f32[128,128]{1,0:T(8,128)S(1)} %add_add_fusion), channel_id=1, source_target_pairs={{0,8},{1,9},{2,10},{3,11},{4,12},{5,13},{6,14},{7,15},{8,0},{9,1},... | collective-permute-start | bytes 196616 | tf_op jit(solution)/shard_map/ppermute | solution.py:20
